TPU v7x, 32 devices: a whole 2x2x4 slice. The times are simulated.
32 devices in a mesh: groups: 2 (over y), space: 16 (over z, x, core).
Axes of the slice: x: 2, y: 2, z: 4, core: 2. Of those that a mesh axis runs over, the one named last changes fastest.
Arguments:
- latent: bfloat16 [2048, 8, 1024], P(('groups', 'space')), parts along dimension 0, may hold values from -6 to 6
- w_src: bfloat16 [1024, 1024], replicated, may hold values from -0.1875 to 0.1875
- b_hidden: float32 [1024], replicated, may hold values from -3 to 3
- w_out: bfloat16 [1024, 100], replicated, may hold values from -0.1875 to 0.1875
- b_out: float32 [100], replicated, may hold values from -3 to 3
- targets: float32 [100, 8192], P(None, ('groups', 'space')), parts along dimension 1, may hold values from -6 to 6
- var_weight: float32 [100], replicated, may hold values from 0.2 to 2
- area_weight: float32 [4096], P('space'), may hold values from 0.5 to 18
- edge_src: int32 [4096, 3], P('space'), may hold values from 0 to 95, as said below
- edge_coef: float32 [4096, 3], P('space'), may hold values from 0.2 to 1
- send_rows: int32 [16, 16, 2], P('space'), may hold values from -1 to 63, as said below
Outputs:
- loss: float32 [2], P('groups'), parts along dimension 0
- grad_latent: float32 [2048, 8, 1024], P(('groups', 'space')), parts along dimension 0
- grad_w_src: float32 [2048, 1024], P(('groups', 'space')), parts along dimension 0
- grad_w_out: float32 [2048, 100], P(('groups', 'space')), parts along dimension 0
There are 2 independent parts, one for each index of `groups`. A program takes and returns all parts, laid end to end along the dimension named above; an argument that names none is the same for every part. Nothing has to cross between parts.
Inputs may be any that keep to these rules, and one draw needn't show every extreme that they name: `send_rows`: -1 marks an empty slot, other entries are rows of the sender's 64 mesh nodes; filled slots come first; every sender fills at least one slot for every receiver, and some receiver gets all 2 slots filled by every sender. `edge_src`: an entry below 64 is a mesh row of the grid point's own device; an entry 64 + s * 2 + b names a filled slot b of sender s for that device.
All inputs are finite; a program needn't handle non-finite values.
Results may differ from a plain program's by a relative error of at most 0.013.
Values may be sent and summed in bfloat16 or wider, within the bound.
No kernel may reach another device: no remote copies, remote signals or barrier semaphores. Data moves between devices by JAX's collectives and lax.ppermute only.
A program may use at most 128 MiB of HBM per device.

v0:
```python
import jax
import jax.numpy as jnp
from jax import lax
from jax.sharding import PartitionSpec as P

WSCALE = 2048


alpha_fair = 0.95
smooth_sq = 0.01


def spread_coef(members):
    return alpha_fair / (2.0 * members * (members - 1)) + (1.0 - alpha_fair) / (
        2.0 * members * members
    )


def shard_work(
    lookup, edge_src, edge_coef, targets, area_weight, var_weight, b_hidden, w_out, b_out, mean_area
):
    grid_dev = targets.shape[1]
    block_size = 128
    row_count, members, hidden_width = lookup.shape
    spread = spread_coef(members)
    offdiag = 1.0 - jnp.eye(members, dtype=jnp.float32)
    table_flat = lookup.reshape(row_count, members * hidden_width)
    column = jnp.arange(row_count, dtype=jnp.int32)
    contract_rows = (((0,), (0,)), ((), ()))

    def one_block(carry, index):
        loss_sum, dwout, dtable = carry
        first = index * block_size
        source_idx = lax.dynamic_slice_in_dim(edge_src, first, block_size, 0)
        edge_weight = lax.dynamic_slice_in_dim(edge_coef, first, block_size, 0)
        truth = lax.dynamic_slice_in_dim(targets, first, block_size, 1)
        block_area = lax.dynamic_slice_in_dim(area_weight, first, block_size, 0)
        matches = (source_idx[:, :, None] == column[None, None, :]).astype(jnp.float32)
        edge_matrix = jnp.sum(edge_weight[:, :, None] * matches, axis=1)
        coef_high = edge_matrix.astype(jnp.bfloat16)
        coef_low = (edge_matrix - coef_high.astype(jnp.float32)).astype(jnp.bfloat16)
        gathered = jnp.dot(coef_high, table_flat, preferred_element_type=jnp.float32) + jnp.dot(
            coef_low, table_flat, preferred_element_type=jnp.float32
        )
        preact = gathered.reshape(block_size, members, hidden_width) + b_hidden
        hidden, gelu_back = jax.vjp(jax.nn.gelu, preact)
        hidden_b = hidden.astype(jnp.bfloat16)
        pred = (
            jnp.einsum("gmh,hv->mvg", hidden_b, w_out, preferred_element_type=jnp.float32)
            + b_out[None, :, None]
        )
        misfit = pred - truth[None]
        smooth = jnp.sqrt(misfit * misfit + smooth_sq)
        pairwise = pred[:, None] - pred[None, :]
        pair_smooth = jnp.sqrt(pairwise * pairwise + smooth_sq)
        crps_score = jnp.mean(smooth, axis=0) - spread * jnp.sum(
            pair_smooth * offdiag[:, :, None, None], axis=(0, 1)
        )
        weighting = var_weight[:, None] * block_area[None, :]
        loss_sum = loss_sum + jnp.sum(weighting * crps_score)
        gradient = misfit / smooth / members - 2.0 * spread * jnp.sum(
            pairwise / pair_smooth * offdiag[:, :, None, None], axis=1
        )
        dpred = (gradient * (weighting / mean_area)[None]).astype(jnp.bfloat16)
        dhidden = jnp.einsum("mvg,hv->gmh", dpred, w_out, preferred_element_type=jnp.float32)
        dpreact = (
            gelu_back(dhidden)[0].astype(jnp.bfloat16).reshape(block_size, members * hidden_width)
        )
        dwout = dwout + jnp.einsum(
            "gmh,mvg->hv", hidden_b, dpred, preferred_element_type=jnp.float32
        )
        dtable = dtable + lax.dot_general(
            coef_high, dpreact, contract_rows, preferred_element_type=jnp.float32
        )
        dtable = dtable + lax.dot_general(
            coef_low, dpreact, contract_rows, preferred_element_type=jnp.float32
        )
        return ((loss_sum, dwout, dtable), None)

    init = (
        jnp.zeros((), jnp.float32),
        jnp.zeros(w_out.shape, jnp.float32),
        jnp.zeros((row_count, members * hidden_width), jnp.float32),
    )
    result, _ = lax.scan(one_block, init, jnp.arange(grid_dev // block_size, dtype=jnp.int32))
    return result


def per_device(
    latent,
    w_src,
    b_hidden,
    w_out,
    b_out,
    targets,
    var_weight,
    area_weight,
    edge_src,
    edge_coef,
    send_rows,
):
    mesh_rows, members, hidden_width = latent.shape
    shards = lax.axis_size("space")
    slot_count = send_rows.shape[2]
    grid_dev = targets.shape[1]
    flat_width = members * hidden_width
    latent_flat = latent.reshape(mesh_rows * members, hidden_width)
    projected = jnp.dot(latent_flat, w_src, preferred_element_type=jnp.float32).astype(jnp.bfloat16)
    projected_rows = projected.reshape(mesh_rows, flat_width)
    slot_rows = send_rows[0]
    mesh_column = jnp.arange(mesh_rows, dtype=jnp.int32)
    selector = (slot_rows.reshape(shards * slot_count)[:, None] == mesh_column[None, :]).astype(
        jnp.bfloat16
    )
    outgoing = jnp.dot(selector, projected_rows, preferred_element_type=jnp.float32).astype(
        jnp.bfloat16
    )
    outgoing = outgoing.reshape(shards, slot_count, members, hidden_width)
    arrived = lax.all_to_all(outgoing, "space", split_axis=0, concat_axis=0, tiled=True)
    lookup = jnp.concatenate(
        [
            projected.reshape(mesh_rows, members, hidden_width),
            arrived.reshape(shards * slot_count, members, hidden_width),
        ],
        axis=0,
    )
    area_total = lax.psum(jnp.sum(area_weight), "space")
    mean_area = area_total / (grid_dev * shards)
    loss_sum, dwout, dtable = shard_work(
        lookup,
        edge_src,
        edge_coef,
        targets,
        area_weight,
        var_weight,
        b_hidden,
        w_out,
        b_out,
        mean_area,
    )
    slot_grad = (
        dtable[mesh_rows:].astype(jnp.bfloat16).reshape(shards, slot_count, members, hidden_width)
    )
    returned = lax.all_to_all(slot_grad, "space", split_axis=0, concat_axis=0, tiled=True)
    returned_rows = returned.reshape(shards * slot_count, flat_width)
    contribution = lax.dot_general(
        selector, returned_rows, (((0,), (0,)), ((), ())), preferred_element_type=jnp.float32
    )
    summed = dtable[:mesh_rows] + contribution
    dprojected = summed.astype(jnp.bfloat16).reshape(mesh_rows * members, hidden_width)
    grad_latent = jnp.dot(dprojected, w_src.T, preferred_element_type=jnp.float32).reshape(
        mesh_rows, members, hidden_width
    )
    grad_scale = WSCALE / (grid_dev * shards)
    own_rows = hidden_width // shards
    full_src = lax.dot_general(
        latent_flat, dprojected, (((0,), (0,)), ((), ())), preferred_element_type=jnp.float32
    )
    total_src, total_out, loss_total = lax.psum((full_src, dwout, loss_sum), "space")
    first_row = lax.axis_index("space") * own_rows
    grad_w_src = lax.dynamic_slice_in_dim(total_src, first_row, own_rows, 0) * grad_scale
    grad_w_out = lax.dynamic_slice_in_dim(total_out, first_row, own_rows, 0) * grad_scale
    loss = jnp.reshape(loss_total / (mean_area * grid_dev * shards), (1,))
    return (loss, grad_latent, grad_w_src, grad_w_out)


def solution(mesh):
    placed = (
        P(("groups", "space"), None, None),
        P(),
        P(),
        P(),
        P(),
        P(None, ("groups", "space")),
        P(),
        P("space"),
        P("space", None),
        P("space", None),
        P("space", None, None),
    )
    return jax.shard_map(
        per_device,
        mesh=mesh,
        in_specs=placed,
        out_specs=(
            P("groups"),
            P(("groups", "space"), None, None),
            P(("groups", "space"), None),
            P(("groups", "space"), None),
        ),
        check_vma=False,
    )
```

profile of v0, /device:TPU:0, one launch (start us, length us, event | category | flops | bytes accessed | tf_op | source)
XLA Modules:
  0.0 281.0 jit_solution(6711533754985055101)
XLA Ops:
  7.2 1.6 copy-done
  8.8 3.4 %convolution_convert_fusion.1 = bf16[512,1024]{1,0:T(8,128)(2,1)} fusion(bf16[1024,1024]{1,0:T(8,128)(2,1)S(1)} %copy-done, bf16[64,8,1024]{2,1,0:T(8,128)(2,1)} %param.13), kind=kOutput, calls=%fused_computation.59 | convolution fusion | flops 1074266112 | bytes 4194304 | tf_op jit(solution)/shard_map/dot_general | solution.py:108
  12.2 1.6 concatenate.8
  15.5 7.4 %all-to-all-start = ((bf16[16,2,8,1024]{3,2,1,0:T(8,128)(2,1)}), bf16[16,2,8,1024]{3,2,1,0:T(8,128)(2,1)}, u32[]{:S(2)}, u32[]{:S(2)}) async-start(bf16[16,2,8,1024]{3,2,1,0:T(8,128)(2,1)} %bitcast.118), calls=%async_computation | async-start | bytes 1048576 | tf_op jit(solution)/shard_map/all_to_all | solution.py:119
  23.5 36.7 %psum.28 = f32[]{:T(128)} all-reduce(f32[]{:T(128)} %reduce_sum.69), channel_id=1, replica_groups=mesh['groups'=2,'space'=16] {'space'}, use_global_device_ids=true, to_apply=%region_1.0 | all-reduce | flops 1 | bytes 8 | tf_op jit(solution)/shard_map/psum | solution.py:127
  60.9 1.3 copy.36
  62.3 2.6 pad_maximum_fusion
  64.9 58.8 %while.18 = (s32[]{:T(128)}, f32[]{:T(128)}, f32[1024,100]{0,1:T(8,128)S(1)}, f32[96,8192]{1,0:T(8,128)}, f32[100]{0:T(128)S(1)}, /*index=5*/s32[2]{0:T(128)S(1)...) while((s32[]{:T(128)}, f32[]{:T(128)}, ...), condition=%wide.region_8.9_spmd.clone.clone, body=%wide.region_2.8_spmd.clone.clone.sunk | while | flops 1478446336 | bytes 115948632 | solution.py:85
  66.2 2.2 fusion.79
  69.2 1.4 multiply_convert_fusion.4
  72.9 3.1 %fusion.81 = (f32[8,100,128]{2,1,0:T(8,128)S(1)}, f32[100,128]{1,0:T(8,128)S(1)}) fusion(f32[8,8]{1,0:T(8,128)S(1)} %convert_subtract_fusion.2, f32[8,100,128]{2,0,1:T(8,128)S(1)} %copy.57, f32[8,100,128]{2,1,0:T(8,128)S(1)} %fusion.80), kind=kLoop, calls=%fused_computation.27.clone.1 | loop fusion | flops 6438400 | bytes 1280256 | tf_op jit(solution)/shard_map/while/body/eval_jaxpr/reduce_sum | solution.py:61
  77.8 2.2 fusion.83
  80.6 4.2 %fusion.84 = bf16[128,8,1024]{2,0,1:T(8,128)(2,1)} fusion(f32[16,8,8,1024]{3,2,1,0:T(8,128)S(1)} %bitcast.116, bf16[8,100,128]{2,1,0:T(8,128)(2,1)S(1)} %get-tuple-element.463, f32[1024]{0:T(1024)S(1)} %get-tuple-element.512, bf16[1024,100]{0,1:T(8,128)(2,1)S(1)} %get-tuple-element.513), kind=kOutput, calls=%fused_computation.15.clone.1 | convolution fusion | flops 231735296 | bytes 6705152 | tf_op jit(solution)/shard_map/while/body/eval_jaxpr/mvg,hv->gmh/dot_general | solution.py:65
  84.9 3.9 %copy.58 = bf16[128,8,1024]{0,2,1:T(8,128)(2,1)} copy(bf16[128,8,1024]{2,0,1:T(8,128)(2,1)} %fusion.84) | data formatting | bytes 4194304 | tf_op jit(solution)/shard_map/while/body/eval_jaxpr/convert_element_type | solution.py:67
  88.8 2.5 convolution_add_fusion.9
  91.3 2.5 convolution_add_fusion.10
  95.1 2.2 fusion.79
  98.1 1.4 multiply_convert_fusion.4
  101.8 3.1 %fusion.81 = (f32[8,100,128]{2,1,0:T(8,128)S(1)}, f32[100,128]{1,0:T(8,128)S(1)}) fusion(f32[8,8]{1,0:T(8,128)S(1)} %convert_subtract_fusion.2, f32[8,100,128]{2,0,1:T(8,128)S(1)} %copy.57, f32[8,100,128]{2,1,0:T(8,128)S(1)} %fusion.80), kind=kLoop, calls=%fused_computation.27.clone.1 | loop fusion | flops 6438400 | bytes 1280256 | tf_op jit(solution)/shard_map/while/body/eval_jaxpr/reduce_sum | solution.py:61
  106.7 2.2 fusion.83
  109.5 4.2 %fusion.84 = bf16[128,8,1024]{2,0,1:T(8,128)(2,1)} fusion(f32[16,8,8,1024]{3,2,1,0:T(8,128)S(1)} %bitcast.116, bf16[8,100,128]{2,1,0:T(8,128)(2,1)S(1)} %get-tuple-element.463, f32[1024]{0:T(1024)S(1)} %get-tuple-element.512, bf16[1024,100]{0,1:T(8,128)(2,1)S(1)} %get-tuple-element.513), kind=kOutput, calls=%fused_computation.15.clone.1 | convolution fusion | flops 231735296 | bytes 6705152 | tf_op jit(solution)/shard_map/while/body/eval_jaxpr/mvg,hv->gmh/dot_general | solution.py:65
  113.8 3.9 %copy.58 = bf16[128,8,1024]{0,2,1:T(8,128)(2,1)} copy(bf16[128,8,1024]{2,0,1:T(8,128)(2,1)} %fusion.84) | data formatting | bytes 4194304 | tf_op jit(solution)/shard_map/while/body/eval_jaxpr/convert_element_type | solution.py:67
  117.7 3.5 %convolution_add_fusion.9 = f32[96,8192]{1,0:T(8,128)S(1)} fusion(bf16[128,8192]{0,1:T(8,128)(2,1)} %bitcast.113, f32[96,8192]{1,0:T(8,128)} %get-tuple-element.486, pred[]{:T(512)S(6)} %compare.3, f32[128,96]{0,1:T(8,128)S(1)} %select_reduce_fusion.2), kind=kOutput, calls=%fused_computation.4.clone.1 | convolution fusion | flops 202911744 | bytes 8437761 | tf_op jit(solution)/shard_map/while/body/eval_jaxpr/dot_general | solution.py:72
  121.2 2.5 convolution_add_fusion.10
  126.0 3.6 %all-to-all-start.1 = ((bf16[16,2,8,1024]{3,2,1,0:T(8,128)(2,1)}), bf16[16,2,8,1024]{3,2,1,0:T(8,128)(2,1)S(1)}, u32[]{:S(2)}, u32[]{:S(2)}) async-start(bf16[16,2,8,1024]{3,2,1,0:T(8,128)(2,1)} %bitcast.120), calls=%async_computation.1 | async-start | bytes 1048576 | tf_op jit(solution)/shard_map/all_to_all | solution.py:144
  130.9 13.1 %all-to-all-done.1 = bf16[16,2,8,1024]{3,2,1,0:T(8,128)(2,1)S(1)} async-done(((bf16[16,2,8,1024]{3,2,1,0:T(8,128)(2,1)}), bf16[16,2,8,1024]{3,2,1,0:T(8,128)(2,1)S(1)}, u32[]{:S(2)}, u32[]{:S(2)}) %all-to-all-start.1) | async-done | bytes 524320 | tf_op jit(solution)/shard_map/all_to_all | solution.py:144
  144.3 2.1 fusion.29
  147.8 4.8 %convolution_bitcast_fusion.1 = f32[1024,1024]{0,1:T(8,128)} fusion(bf16[512,1024]{1,0:T(8,128)(2,1)} %reshape.92, bf16[64,8,1024]{2,1,0:T(8,128)(2,1)} %param.13), kind=kOutput, calls=%fused_computation.55 | convolution fusion | flops 1073741824 | bytes 6291456 | tf_op jit(solution)/shard_map/dot_general | solution.py:156
  152.6 34.6 %psum.29 = f32[]{:T(128)} all-reduce(f32[]{:T(128)} %get-tuple-element.218), channel_id=1, replica_groups=mesh['groups'=2,'space'=16] {'space'}, use_global_device_ids=true, to_apply=%region_9.10 | all-reduce | flops 1 | bytes 8 | tf_op jit(solution)/shard_map/psum | solution.py:159
  189.1 2.6 fusion.30
  191.8 77.8 %all-reduce.3.cloned.1.call-done = (f32[1024,1024]{0,1:T(8,128)}, f32[1024,100]{1,0:T(8,128)}) async-done(((f32[1024,1024]{0,1:T(8,128)}, f32[1024,100]{1,0:T(8,128)}), (f32[1024,1024]{0,1:T(8,128)}, f32[1024,100]{1,0:T(8,128)})) %all-reduce.3.cloned.1.call-update) | async-done | bytes 4603920 | tf_op jit(solution)/shard_map/psum | solution.py:159
  271.7 1.4 dynamic-slice_multiply_fusion.1
  (84 shorter events, 20.9 us)
Async XLA Ops:
  7.2 1.6 copy-start
  7.2 6.6 %copy-start.14 = (s32[1,16,2]{1,2,0:T(2,128)S(1)}, s32[1,16,2]{1,2,0:T(2,128)}, u32[]{:S(2)}) copy-start(s32[1,16,2]{1,2,0:T(2,128)} %param.23) | copy-start | bytes 388
  12.2 10.7 %copy-start.15 = (f32[256]{0:T(256)S(1)}, f32[256]{0:T(256)}, u32[]{:S(2)}) copy-start(f32[256]{0:T(256)} %param.20) | copy-start | bytes 3076
  13.8 9.8 %copy-start.6 = (bf16[64,8192]{1,0:T(8,128)(2,1)}, bf16[64,8192]{1,0:T(8,128)(2,1)S(1)}, u32[]{:S(2)}) copy-start(bf16[64,8192]{1,0:T(8,128)(2,1)S(1)} %concatenate.8) | copy-start | bytes 3145732
  14.3 50.5 %copy-start.7 = (bf16[1024,100]{0,1:T(8,128)(2,1)S(1)}, bf16[1024,100]{0,1:T(8,128)(2,1)}, u32[]{:S(2)}) copy-start(bf16[1024,100]{0,1:T(8,128)(2,1)} %param.16) | copy-start | bytes 614404
  14.4 50.5 %copy-start.8 = (f32[100,256]{1,0:T(8,128)S(1)}, f32[100,256]{1,0:T(8,128)}, u32[]{:S(2)}) copy-start(f32[100,256]{1,0:T(8,128)} %param.18) | copy-start | bytes 307204
  14.4 50.5 %copy-start.9 = (f32[1024]{0:T(1024)S(1)}, f32[1024]{0:T(1024)}, u32[]{:S(2)}) copy-start(f32[1024]{0:T(1024)} %param.15) | copy-start | bytes 12292
  14.4 50.5 %copy-start.10 = (f32[100]{0:T(128)S(1)}, f32[100]{0:T(128)}, u32[]{:S(2)}) copy-start(f32[100]{0:T(128)} %param.19) | copy-start | bytes 1204
  14.4 50.5 %copy-start.11 = (s32[256,3]{0,1:T(4,128)S(1)}, s32[256,3]{0,1:T(4,128)}, u32[]{:S(2)}) copy-start(s32[256,3]{0,1:T(4,128)} %param.21) | copy-start | bytes 9220
  14.4 50.5 %copy-start.12 = (f32[256,3]{0,1:T(4,128)S(1)}, f32[256,3]{0,1:T(4,128)}, u32[]{:S(2)}) copy-start(f32[256,3]{0,1:T(4,128)} %param.22) | copy-start | bytes 9220
  14.4 50.5 %copy-start.13 = (f32[100]{0:T(128)S(1)}, f32[100]{0:T(128)}, u32[]{:S(2)}) copy-start(f32[100]{0:T(128)} %param.17) | copy-start | bytes 1204
  15.5 45.4 %all-to-all-start = ((bf16[16,2,8,1024]{3,2,1,0:T(8,128)(2,1)}), bf16[16,2,8,1024]{3,2,1,0:T(8,128)(2,1)}, u32[]{:S(2)}, u32[]{:S(2)}) async-start(bf16[16,2,8,1024]{3,2,1,0:T(8,128)(2,1)} %bitcast.118), calls=%async_computation | async-start | bytes 1048576 | tf_op jit(solution)/shard_map/all_to_all | solution.py:119
  66.2 2.3 copy-start.5
  69.2 3.6 %copy-start.3 = (f32[128,8192]{1,0:T(8,128)}, f32[128,8192]{1,0:T(8,128)S(1)}, u32[]{:S(2)}) copy-start(f32[128,8192]{1,0:T(8,128)S(1)} %convolution_add_fusion.8) | copy-start | bytes 12582916 | tf_op jit(solution)/shard_map/while
  70.7 1.3 copy-start.1
  77.8 2.8 %copy-start.4 = (f32[128,8192]{1,0:T(8,128)S(1)}, f32[128,8192]{1,0:T(8,128)}, u32[]{:S(2)}) copy-start(f32[128,8192]{1,0:T(8,128)} %copy-done.3) | copy-start | bytes 12582916 | tf_op jit(solution)/shard_map/while
  88.8 2.5 copy-start.2
  95.1 2.3 copy-start.5
  98.1 3.6 %copy-start.3 = (f32[128,8192]{1,0:T(8,128)}, f32[128,8192]{1,0:T(8,128)S(1)}, u32[]{:S(2)}) copy-start(f32[128,8192]{1,0:T(8,128)S(1)} %convolution_add_fusion.8) | copy-start | bytes 12582916 | tf_op jit(solution)/shard_map/while
  99.6 1.3 copy-start.1
  106.7 2.8 %copy-start.4 = (f32[128,8192]{1,0:T(8,128)S(1)}, f32[128,8192]{1,0:T(8,128)}, u32[]{:S(2)}) copy-start(f32[128,8192]{1,0:T(8,128)} %copy-done.3) | copy-start | bytes 12582916 | tf_op jit(solution)/shard_map/while
  117.7 3.5 %copy-start.2 = (bf16[128,8,1024]{0,2,1:T(8,128)(2,1)S(1)}, bf16[128,8,1024]{0,2,1:T(8,128)(2,1)}, u32[]{:S(2)}) copy-start(bf16[128,8,1024]{0,2,1:T(8,128)(2,1)} %copy.58) | copy-start | bytes 6291460 | tf_op jit(solution)/shard_map/while
  126.0 18.0 %all-to-all-start.1 = ((bf16[16,2,8,1024]{3,2,1,0:T(8,128)(2,1)}), bf16[16,2,8,1024]{3,2,1,0:T(8,128)(2,1)S(1)}, u32[]{:S(2)}, u32[]{:S(2)}) async-start(bf16[16,2,8,1024]{3,2,1,0:T(8,128)(2,1)} %bitcast.120), calls=%async_computation.1 | async-start | bytes 1048576 | tf_op jit(solution)/shard_map/all_to_all | solution.py:144
  129.6 139.9 %all-reduce.3.cloned.1.call-start = ((), (), s32[]{:S(2)}) async-start(), calls=%async_computation.2 | async-start | bytes 9437184 | tf_op jit(solution)/shard_map/psum | solution.py:159
Sparse Core Ops, SparseCore 0:
  152.7 116.7 all-reduce.2
where the time goes:
time: 282 us; the launch traced here: 281 us
  waiting for transfers between devices  90.9 us (32%)
  blocking collectives  71.3 us (25%)
  matrix products  44.8 us (16%)
  local copies, waits for them, and re-layouts  25.5 us (9%)
  between operations  17.4 us (6%)
  other arithmetic  17.1 us (6%)
  starting transfers between devices  11.2 us (4%)
  loops' own time  2.89 us (1%)
    psum x1, waiting for transfers between devices, per_device(): lax.psum((full_src, dwout, loss_sum), 'space')  77.8 us
    psum x1, blocking collectives, per_device(): area_total = lax.psum(jnp.sum(area_weight), 'space')  36.7 us
    psum x1, blocking collectives, per_device(): lax.psum((full_src, dwout, loss_sum), 'space')  34.6 us
    all_to_all x1, waiting for transfers between devices, per_device(): lax.all_to_all(slot_grad, 'space', split_axis=0, concat_axis=0, tiled=True)  13.1 us
    dot_general x2, matrix products, one_block(): jnp.einsum('mvg,hv->gmh', dpred, w_out, preferred_element_type=jnp.float32)  8.5 us
    convert_element_type x2, local copies, waits for them, and re-layouts, one_block(): gelu_back(dhidden)[0].astype(jnp.bfloat16)  7.82 us
    all_to_all x1, starting transfers between devices, per_device(): lax.all_to_all(outgoing, 'space', split_axis=0, concat_axis=0, tiled=True)  7.41 us
    unnamed x29, local copies, waits for them, and re-layouts  7.02 us
  transfers between devices with their start and end apart: 3, of which 2 were waited for; matrix products, arithmetic and copies ran while one was open for 2% of the time, Pallas kernels for 0%

commit v1 on v0

v1 whole, which is shorter than its diff:
```python
import functools
import math

import jax
import jax.numpy as jnp
from jax import lax
from jax.experimental import pallas as pl
from jax.experimental.pallas import tpu as pltpu
from jax.sharding import PartitionSpec as P

WSCALE = 2048
LANES = 128
ROWS = 16
alpha_fair = 0.95
smooth_sq = 0.01
VMEM_BYTES = 56 * 1024 * 1024

f32 = jnp.float32
bf16 = jnp.bfloat16
TN = (((0,), (0,)), ((), ()))
NT = (((1,), (1,)), ((), ()))
SMEM = pl.BlockSpec(memory_space=pltpu.SMEM)
VMEM = pl.BlockSpec(memory_space=pltpu.VMEM)


def spread_coef(members):
    return alpha_fair / (2.0 * members * (members - 1)) + (1.0 - alpha_fair) / (
        2.0 * members * members
    )


def mm(a, b, dims=(((1,), (0,)), ((), ()))):
    return lax.dot_general(a, b, dims, preferred_element_type=f32)


def round_up(value, multiple):
    return -(-value // multiple) * multiple


def split_sum(value):
    high = value.astype(bf16)
    rest = value - high.astype(f32)
    middle = rest.astype(bf16)
    return high, middle, (rest - middle.astype(f32)).astype(bf16)


def fill_selector(rows_ref, selector, shards, slots, members):
    lane = lax.broadcasted_iota(jnp.int32, (members, selector.shape[1]), 1)
    member = lax.broadcasted_iota(jnp.int32, (members, selector.shape[1]), 0)
    for s in range(shards):
        for b in range(slots):
            row = rows_ref[0, b, s]
            first = (s * slots + b) * members
            selector[first : first + members, :] = jnp.where(
                lane == row * members + member, 1.0, 0.0
            ).astype(f32)


def project(projected, rows, w_src):
    out = mm(rows, w_src[...])
    for c in range(projected.shape[0]):
        projected[c, : rows.shape[0], :] = out[:, c * LANES : (c + 1) * LANES]


def by_member(projected, table, first, count):
    members = table.shape[0]
    for m in range(members):
        for c in range(projected.shape[0]):
            block = projected[c, pl.ds(m, count, stride=members), :]
            table[m, first : first + count, c * LANES : (c + 1) * LANES] = block.astype(bf16)


def pack_kernel(rows_ref, latent, area, out, selector, *, members, slots):
    shards, per_pair, _ = out.shape
    width = latent.shape[1]
    fill_selector(rows_ref, selector, shards, slots, members)
    picked = mm(selector[...].astype(bf16), latent[...])
    out[:, :, :width] = picked.astype(bf16).reshape(shards, per_pair, width)
    total = jnp.sum(area[...], axis=1, keepdims=True) + jnp.zeros((per_pair, LANES), f32)
    lane = lax.broadcasted_iota(jnp.int32, (per_pair, LANES), 1)
    tail = jnp.zeros((per_pair, LANES), f32)
    for i, piece in enumerate(split_sum(total)):
        tail = jnp.where(lane == i, piece.astype(f32), tail)
    tail = tail.astype(bf16)
    for s in range(shards):
        out[s, :, width:] = tail


def local_kernel(
    latent, w_src, edge_src, edge_coef, table, edge_gr, edge_rg, projected, *, members
):
    mesh_rows = table.shape[1]
    project(projected, latent[...], w_src)
    by_member(projected, table, 0, mesh_rows)
    rows, points = edge_rg.shape
    row = lax.broadcasted_iota(jnp.int32, (rows, points), 0)
    matrix = jnp.zeros((rows, points), f32)
    for k in range(edge_src.shape[0]):
        matrix = matrix + jnp.where(
            row == edge_src[k : k + 1, :], edge_coef[k : k + 1, :], 0.0
        )
    edge_rg[...] = matrix.astype(bf16)
    edge_gr[...] = matrix.T.astype(bf16)


def decoder_kernel(
    me_ref,
    arrived,
    local,
    latent,
    w_src,
    edge_gr,
    edge_rg,
    b_hidden,
    w_out_t,
    b_out,
    targets,
    var_weight,
    area_weight,
    dlocal,
    slot_grad,
    keep_a,
    send_a,
    keep_b,
    send_b,
    table,
    hidden,
    slope,
    preact,
    pred,
    dpred,
    dtable,
    dtable_low,
    partial,
    *,
    points_all,
    variables,
):
    members, mesh_rows, width = local.shape
    shards, per_pair, _ = arrived.shape
    received = shards * per_pair
    rows, points = edge_rg.shape
    var_pad = w_out_t.shape[0]
    var_rows = round_up(variables, ROWS)
    me = me_ref[0]

    arrived_rows = arrived[:, :, :width].reshape(received, width)
    project(dtable, arrived_rows, w_src)
    table[:, :mesh_rows, :] = local[...]
    by_member(dtable, table, mesh_rows, received // members)

    tail = arrived[:, :, width:].astype(f32)
    at_row = lax.broadcasted_iota(jnp.int32, tail.shape, 1)
    at_lane = lax.broadcasted_iota(jnp.int32, tail.shape, 2)
    tail = jnp.where((at_row == 0) & (at_lane < 3), tail, 0.0)
    mean_area = jnp.sum(jnp.sum(tail, axis=0), keepdims=True) / points_all

    c0 = math.sqrt(2.0 / math.pi)
    c1 = c0 * 0.044715

    def forward(m, _):
        first = pl.multiple_of(m * points, points)
        preact[...] = mm(edge_gr[...], table[m])

        for r in range(0, points, ROWS):
            x = preact[r : r + ROWS, :] + b_hidden[...]
            x2 = x * x
            t = jnp.tanh(x * (c0 + c1 * x2))
            half = 0.5 * x
            hidden[pl.ds(first + r, ROWS), :] = (half + half * t).astype(bf16)
            bend = half * (1.0 - t * t) * (c0 + (3.0 * c1) * x2)
            slope[pl.ds(first + r, ROWS), :] = (0.5 + 0.5 * t + bend).astype(bf16)

        pred[m] = mm(w_out_t[...], hidden[pl.ds(first, points), :], NT) + b_out[...]
        return 0

    lax.fori_loop(0, members, forward, 0)

    spread = spread_coef(members)
    dpred[var_rows:, :] = jnp.zeros((var_pad - var_rows, members * points), bf16)
    loss_sum = jnp.zeros((ROWS, LANES), f32)
    inverse_mean = 1.0 / mean_area
    for g in range(0, points, LANES):
        area = area_weight[:, g : g + LANES]

        def score(block, loss_sum, g=g, area=area):
            v = pl.multiple_of(block * ROWS, ROWS)
            p = [pred[m, pl.ds(v, ROWS), g : g + LANES] for m in range(members)]
            truth = targets[pl.ds(v, ROWS), g : g + LANES]
            weighting = var_weight[pl.ds(v, ROWS), :] * area
            fit = jnp.zeros((ROWS, LANES), f32)
            grads = []
            for m in range(members):
                d = p[m] - truth
                q = d * d + smooth_sq
                r = lax.rsqrt(q)
                fit = fit + q * r
                grads.append(d * r * (1.0 / members))
            pairs = jnp.zeros((ROWS, LANES), f32)
            apart = [jnp.zeros((ROWS, LANES), f32) for _ in range(members)]
            for j in range(members):
                for k in range(j + 1, members):
                    d = p[j] - p[k]
                    q = d * d + smooth_sq
                    r = lax.rsqrt(q)
                    pairs = pairs + q * r
                    s = d * r
                    apart[j] = apart[j] + s
                    apart[k] = apart[k] - s
            scaled = weighting * inverse_mean
            for m in range(members):
                gradient = grads[m] - (2.0 * spread) * apart[m]
                dpred[pl.ds(v, ROWS), m * points + g : m * points + g + LANES] = (
                    gradient * scaled
                ).astype(bf16)
            return loss_sum + weighting * (
                fit * (1.0 / members) - (2.0 * spread) * pairs
            )

        loss_sum = lax.fori_loop(0, var_rows // ROWS, score, loss_sum)
    loss = jnp.sum(loss_sum, keepdims=True) * (inverse_mean / points_all)

    for m in range(members):
        first = m * points
        grad = mm(dpred[:, first : first + points], w_out_t[...], TN)
        grad = (grad * slope[first : first + points, :].astype(f32)).astype(bf16)
        grad = mm(edge_rg[...], grad)
        for c in range(width // LANES):
            dtable[c, pl.ds(m, rows, stride=members), :] = grad[:, c * LANES : (c + 1) * LANES]

    own = mesh_rows * members
    for c in range(width // LANES):
        left, right = c * LANES, (c + 1) * LANES
        dlocal[:, left:right] = dtable[c, :own, :]
        dtable_low[:, left:right] = dtable[c].astype(bf16)
    slot_grad[...] = dtable_low[own:, :].reshape(shards, per_pair, width)

    half_width = width // 2
    pairs, _, own_rows, columns = partial.shape
    core = lax.rem(me, 2)
    for c, (keep, send) in enumerate(((keep_a, send_a), (keep_b, send_b))):
        left, right = c * half_width, (c + 1) * half_width
        grad = mm(latent[...], dtable_low[:own, left:right], TN)
        grad = grad + mm(arrived_rows, dtable_low[own:, left:right], TN)
        partial[:, :, :, :half_width] = grad.astype(bf16).reshape(
            pairs, 2, own_rows, half_width
        )
        if c == 0:
            grad = mm(dpred[...], hidden[...]).T
            row = lax.broadcasted_iota(jnp.int32, grad.shape, 0)
            lane = lax.broadcasted_iota(jnp.int32, grad.shape, 1)
            row = lax.rem(row, own_rows)
            grad = jnp.where(lane < variables, grad, 0.0)
            for i, piece in enumerate(split_sum(loss)[:2]):
                place = me * 2 + i
                here = (row == lax.rem(place, own_rows)) & (
                    lane == variables + place // own_rows
                )
                grad = jnp.where(here, piece.astype(f32), grad)
            partial[:, :, :, half_width:] = grad.astype(bf16).reshape(
                pairs, 2, own_rows, columns - half_width
            )
            keep[...] = partial[:, core]
            send[...] = partial[:, 1 - core]
        else:
            keep[...] = partial[:, core, :, :half_width]
            send[...] = partial[:, 1 - core, :, :half_width]


def latent_grad_kernel(rows_ref, returned, dlocal, w_src, out, selector, *, members, slots):
    shards, per_pair, width = returned.shape
    fill_selector(rows_ref, selector, shards, slots, members)
    back = returned[...].reshape(shards * per_pair, width)
    total = dlocal[...] + mm(selector[...].astype(bf16), back, TN)
    out[...] = mm(total.astype(bf16), w_src[...], NT)


def call(kernel, out_shape, in_specs, scratch, cost, *args):
    single = not isinstance(out_shape, (list, tuple))
    return pl.pallas_call(
        kernel,
        out_shape=out_shape,
        in_specs=in_specs,
        out_specs=VMEM if single else [VMEM] * len(out_shape),
        scratch_shapes=scratch,
        compiler_params=pltpu.CompilerParams(vmem_limit_bytes=VMEM_BYTES),
        cost_estimate=pl.CostEstimate(flops=cost, bytes_accessed=4 << 20, transcendentals=0),
    )(*args)


def halve(summed, bits, bit, me, shards):
    place = bits.index(bit)
    shape = summed.shape
    split = summed.reshape(1 << place, 2, -1, *shape[1:])
    mine = (me // bit) % 2
    keep = lax.dynamic_index_in_dim(split, mine, 1, keepdims=False)
    send = lax.dynamic_index_in_dim(split, 1 - mine, 1, keepdims=False)
    flat = (-1, *shape[1:])
    return keep.reshape(flat), send.reshape(flat)


def swap(value, bit, shards):
    return lax.ppermute(value, "space", [(i, i ^ bit) for i in range(shards)])


def per_device(
    latent,
    w_src,
    b_hidden,
    w_out,
    b_out,
    targets,
    var_weight,
    area_weight,
    edge_src,
    edge_coef,
    send_rows,
):
    mesh_rows, members, width = latent.shape
    shards = lax.axis_size("space")
    slots = send_rows.shape[2]
    variables, points = targets.shape
    points_all = points * shards
    own_rows = width // shards
    per_pair = slots * members
    rows = mesh_rows + shards * slots
    loss_columns = round_up(2 * shards, own_rows) // own_rows
    var_pad = round_up(variables + loss_columns, LANES)
    var_rows = round_up(variables, ROWS)
    half_width = width // 2
    shape = jax.ShapeDtypeStruct
    me = lax.axis_index("space").astype(jnp.int32)

    latent_rows = latent.reshape(mesh_rows * members, width)
    slot_rows = jnp.swapaxes(send_rows, 1, 2)
    area_row = area_weight.reshape(1, points)
    selector = pltpu.VMEM((shards * per_pair, mesh_rows * members), f32)
    outgoing = call(
        functools.partial(pack_kernel, members=members, slots=slots),
        shape((shards, per_pair, width + LANES), bf16),
        [SMEM, VMEM, VMEM],
        [selector],
        1 << 29,
        slot_rows,
        latent_rows,
        area_row,
    )
    arrived = lax.all_to_all(outgoing, "space", split_axis=0, concat_axis=0, tiled=True)

    local, edge_gr, edge_rg = call(
        functools.partial(local_kernel, members=members),
        [
            shape((members, mesh_rows, width), bf16),
            shape((points, rows), bf16),
            shape((rows, points), bf16),
        ],
        [VMEM] * 4,
        [pltpu.VMEM((width // LANES, mesh_rows * members, LANES), f32)],
        1 << 31,
        latent_rows,
        w_src,
        edge_src.T,
        edge_coef.T,
    )
    w_out_t = jnp.pad(w_out.T, ((0, var_pad - variables), (0, 0)))
    b_out_column = jnp.pad(b_out, (0, var_pad - variables)).reshape(var_pad, 1)
    var_column = jnp.pad(var_weight, (0, var_rows - variables)).reshape(var_rows, 1)
    targets_pad = jnp.pad(targets, ((0, var_rows - variables), (0, 0)))

    dlocal, slot_grad, keep_a, send_a, keep_b, send_b = call(
        functools.partial(decoder_kernel, points_all=points_all, variables=variables),
        [
            shape((mesh_rows * members, width), f32),
            shape((shards, per_pair, width), bf16),
            shape((shards // 2, own_rows, half_width + var_pad), bf16),
            shape((shards // 2, own_rows, half_width + var_pad), bf16),
            shape((shards // 2, own_rows, half_width), bf16),
            shape((shards // 2, own_rows, half_width), bf16),
        ],
        [SMEM] + [VMEM] * 12,
        [
            pltpu.VMEM((members, rows, width), bf16),
            pltpu.VMEM((members * points, width), bf16),
            pltpu.VMEM((members * points, width), bf16),
            pltpu.VMEM((points, width), f32),
            pltpu.VMEM((members, var_pad, points), f32),
            pltpu.VMEM((var_pad, members * points), bf16),
            pltpu.VMEM((width // LANES, rows * members, LANES), f32),
            pltpu.VMEM((rows * members, width), bf16),
            pltpu.VMEM((shards // 2, 2, own_rows, half_width + var_pad), bf16),
        ],
        1 << 34,
        me.reshape(1),
        arrived,
        local,
        latent_rows,
        w_src,
        edge_gr,
        edge_rg,
        b_hidden.reshape(1, width),
        w_out_t,
        b_out_column,
        targets_pad,
        var_column,
        area_row,
    )

    returned = lax.all_to_all(slot_grad, "space", split_axis=0, concat_axis=0, tiled=True)

    levels = [1 << i for i in reversed(range(1, shards.bit_length() - 1))]
    order_a = levels[::-1]
    order_b = order_a[1:2] + order_a[:1] + order_a[2:]
    got_a, got_b = swap(send_a, 1, shards), swap(send_b, 1, shards)
    bits_a, bits_b = list(levels), list(levels)
    for bit_a, bit_b in zip(order_a, order_b, strict=True):
        sum_a = (keep_a.astype(f32) + got_a.astype(f32)).astype(bf16)
        sum_b = (keep_b.astype(f32) + got_b.astype(f32)).astype(bf16)
        keep_a, send_a = halve(sum_a, bits_a, bit_a, me, shards)
        keep_b, send_b = halve(sum_b, bits_b, bit_b, me, shards)
        got_a, got_b = swap(send_a, bit_a, shards), swap(send_b, bit_b, shards)
        bits_a.remove(bit_a)
        bits_b.remove(bit_b)
    total_a = (keep_a.astype(f32) + got_a.astype(f32))[0]
    total_b = (keep_b.astype(f32) + got_b.astype(f32))[0]

    grad_latent = call(
        functools.partial(latent_grad_kernel, members=members, slots=slots),
        shape((mesh_rows * members, width), f32),
        [SMEM] + [VMEM] * 3,
        [selector],
        1 << 31,
        slot_rows,
        returned,
        dlocal,
        w_src,
    ).reshape(mesh_rows, members, width)

    grad_scale = WSCALE / points_all
    grad_w_src = jnp.concatenate([total_a[:, :half_width], total_b], axis=1) * grad_scale
    grad_w_out = total_a[:, half_width : half_width + variables] * grad_scale
    loss = jnp.sum(total_a[:, half_width + variables :]).reshape(1)
    return (loss, grad_latent, grad_w_src, grad_w_out)


def solution(mesh):
    placed = (
        P(("groups", "space"), None, None),
        P(),
        P(),
        P(),
        P(),
        P(None, ("groups", "space")),
        P(),
        P("space"),
        P("space", None),
        P("space", None),
        P("space", None, None),
    )
    return jax.shard_map(
        per_device,
        mesh=mesh,
        in_specs=placed,
        out_specs=(
            P("groups"),
            P(("groups", "space"), None, None),
            P(("groups", "space"), None),
            P(("groups", "space"), None),
        ),
        check_vma=False,
    )
```

time: 282 us -> 93.3 us (0.33)
  blocking collectives: 71.3 us -> 0 us
  waiting for transfers between devices: 90.9 us -> 26 us
  matrix products: 44.8 us -> 0 us
  Pallas kernels: 0 us -> 34.2 us
  local copies, waits for them, and re-layouts: 25.5 us -> 4.67 us
  between operations: 17.4 us -> 0.83 us
  other arithmetic: 17.1 us -> 3.72 us
  starting transfers between devices: 11.2 us -> 23.5 us
  loops' own time: 2.89 us -> 0 us
    psum x1 -> x0, waiting for transfers between devices: 77.8 us -> none  [per_device(): lax.psum((full_src, dwout, loss_sum), 'space')]
    psum x2 -> x0, blocking collectives: 71.3 us -> none  [the longest x1 36.7 us: per_device(): area_total = lax.psum(jnp.sum(area_weight), 'space')]
    dot_general x19 -> x0, matrix products: 44.8 us -> none  [the longest x2 8.5 us: one_block(): jnp.einsum('mvg,hv->gmh', dpred, w_out, preferred_element_type=jnp.float32)]
    pallas_call x0 -> x4, Pallas kernels: none -> 34.2 us  [call(): pl.pallas_call(kernel, out_shape=out_shape, in_specs=in_specs, out_specs=...]
    ppermute x0 -> x8, waiting for transfers between devices: none -> 17.7 us  [swap(): return lax.ppermute(value, 'space', [(i, i ^ bit) for i in range(shards)])]
    all_to_all x1, waiting for transfers between devices: 13.1 us -> 0.01 us  [per_device(): lax.all_to_all(slot_grad, 'space', split_axis=0, concat_axis=0, tiled=True)]
    ppermute x0 -> x8, starting transfers between devices: none -> 12.4 us  [swap(): return lax.ppermute(value, 'space', [(i, i ^ bit) for i in range(shards)])]
    all_to_all x1, waiting for transfers between devices: 0.01 us -> 8.31 us  [per_device(): lax.all_to_all(outgoing, 'space', split_axis=0, concat_axis=0, tiled=True)]
  transfers between devices with their start and end apart: 3 -> 10, of which waited for: 2 -> 6; matrix products, arithmetic and copies ran while one was open for 2% -> 5% of each run, Pallas kernels for 0% -> 10%
where the time goes in v1:
time: 93.3 us; the launch traced here: 93 us
  Pallas kernels  34.2 us (37%)
  waiting for transfers between devices  26 us (28%)
  starting transfers between devices  23.5 us (25%)
  local copies, waits for them, and re-layouts  4.67 us (5%)
  other arithmetic  3.72 us (4%)
    pallas_call x4, Pallas kernels, call(): pl.pallas_call(kernel, out_shape=out_shape, in_specs=in_specs, out_specs=...  34.2 us
    ppermute x8, waiting for transfers between devices, swap(): return lax.ppermute(value, 'space', [(i, i ^ bit) for i in range(shards)])  17.7 us
    ppermute x8, starting transfers between devices, swap(): return lax.ppermute(value, 'space', [(i, i ^ bit) for i in range(shards)])  12.4 us
    all_to_all x1, waiting for transfers between devices, per_device(): lax.all_to_all(outgoing, 'space', split_axis=0, concat_axis=0, tiled=True)  8.31 us
    all_to_all x1, starting transfers between devices, per_device(): lax.all_to_all(outgoing, 'space', split_axis=0, concat_axis=0, tiled=True)  7.36 us
    all_to_all x1, starting transfers between devices, per_device(): lax.all_to_all(slot_grad, 'space', split_axis=0, concat_axis=0, tiled=True)  3.73 us
  transfers between devices with their start and end apart: 10, of which 6 were waited for; matrix products, arithmetic and copies ran while one was open for 5% of the time, Pallas kernels for 10%

profile of v1, /device:TPU:0, one launch (start us, length us, event | category | flops | bytes accessed | tf_op | source)
XLA Modules:
  0.0 93.0 jit_solution(1052367380891768069)
XLA Ops:
  0.7 2.5 %shard_map.138 = bf16[16,16,1152]{2,1,0:T(8,128)(2,1)} custom-call(s32[1,2,16]{2,1,0:T(2,128)} %bitcast.62, bf16[512,1024]{1,0:T(8,128)(2,1)} %bitcast.54, f32[1,256]{1,0:T(1,128)} %bitcast.60), custom_call_target="tpu_custom_call" | custom-call | flops 536870912 | bytes 4194304 | tf_op jit(solution)/shard_map/pallas_call | solution.py:280
  3.2 7.4 %all-to-all-start = ((bf16[16,16,1152]{2,1,0:T(8,128)(2,1)}), bf16[16,16,1152]{2,1,0:T(8,128)(2,1)S(1)}, u32[]{:S(2)}, u32[]{:S(2)}) async-start(bf16[16,16,1152]{2,1,0:T(8,128)(2,1)} %shard_map.138), calls=%async_computation | async-start | bytes 1179648 | tf_op jit(solution)/shard_map/all_to_all | solution.py:348
  10.6 0.8 copy.17.b_out
  11.4 0.7 copy.18.var_weight
  12.1 0.7 pad.16.w_out_t
  12.8 0.7 pad.18.targets
  13.5 4.3 %shard_map.139 = (bf16[8,64,1024]{2,1,0:T(8,128)(2,1)}, bf16[256,96]{1,0:T(8,128)(2,1)}, bf16[96,256]{1,0:T(8,128)(2,1)}) custom-call(bf16[512,1024]{1,0:T(8,128)(2,1)} %bitcast.55, bf16[1024,1024]{1,0:T(8,128)(2,1)} %w_src.5, s32[3,256]{1,0:T(4,128)} %bitcast.57, f32[3,256]{1,0:T(4,128)} %bitcast.58), custom_call_target="tpu_custom_call" | custom-call | flops 2147483648 | bytes 4194304 | tf_op jit(solution)/shard_map/pallas_call | solution.py:280
  17.8 8.3 %all-to-all-done.arrived = bf16[16,16,1152]{2,1,0:T(8,128)(2,1)S(1)} async-done(((bf16[16,16,1152]{2,1,0:T(8,128)(2,1)}), bf16[16,16,1152]{2,1,0:T(8,128)(2,1)S(1)}, u32[]{:S(2)}, u32[]{:S(2)}) %all-to-all-start) | async-done | bytes 589856 | tf_op jit(solution)/shard_map/all_to_all | solution.py:348
  26.1 0.8 copy-done.1
  26.9 22.1 %shard_map.140 = (f32[512,1024]{1,0:T(8,128)}, bf16[16,16,1024]{2,1,0:T(8,128)(2,1)}, bf16[8,64,640]{2,1,0:T(8,128)(2,1)}, bf16[8,64,640]{2,1,0:T(8,128)(2,1)}, ...) custom-call(s32[1]{0:T(128)} %bitcast.me_ref, bf16[16,16,1152]{2,1,0:T(8,128)(2,1)} %copy-done.1, ...), custom_call_target="tpu_custom_call" | custom-call | flops 17179869184 | bytes 4194304 | tf_op jit(solution)/shard_map/pallas_call | solution.py:280
  49.0 0.5 collective-permute-start
  49.5 1.6 %collective-permute-done.4 = bf16[8,64,512]{2,1,0:T(8,128)(2,1)S(1)} collective-permute-done((bf16[8,64,512]{2,1,0:T(8,128)(2,1)}, bf16[8,64,512]{2,1,0:T(8,128)(2,1)S(1)}, u32[]{:S(2)}, u32[]{:S(2)}) %collective-permute-start.4) | collective-permute-done | bytes 524320 | tf_op jit(solution)/shard_map/ppermute | solution.py:303
  51.1 1.2 %add_convert_fusion.1 = bf16[8,64,512]{2,1,0:T(8,128)(2,1)S(1)} fusion(bf16[8,64,512]{2,1,0:T(8,128)(2,1)S(1)} %collective-permute-done.4, bf16[8,64,512]{2,1,0:T(8,128)(2,1)} %get-tuple-element.20), kind=kLoop, calls=%fused_computation.1 | loop fusion | flops 1048576 | bytes 1572864 | tf_op jit(solution)/shard_map/convert_element_type | solution.py:417
  52.4 1.8 %collective-permute-start.5 = (bf16[4,64,512]{2,1,0:T(8,128)(2,1)S(1)}, bf16[4,64,512]{2,1,0:T(8,128)(2,1)S(1)}, u32[]{:S(2)}, u32[]{:S(2)}) collective-permute-start(bf16[4,64,512]{2,1,0:T(8,128)(2,1)S(1)} %bitcast.52), channel_id=1, source_target_pairs={{0,4},{1,5},{2,6},{3,7},{4,0},{5,1},{6,2},{7,3},{8,12},{9,13},{10,... | collective-permute-start | bytes 786440 | tf_op jit(solution)/shard_map/ppermute | solution.py:303
  54.2 3.7 %all-to-all-start.1 = ((bf16[16,16,1024]{2,1,0:T(8,128)(2,1)}), bf16[16,16,1024]{2,1,0:T(8,128)(2,1)S(1)}, u32[]{:S(2)}, u32[]{:S(2)}) async-start(bf16[16,16,1024]{2,1,0:T(8,128)(2,1)} %get-tuple-element.18), calls=%async_computation.1 | async-start | bytes 1048576 | tf_op jit(solution)/shard_map/all_to_all | solution.py:408
  57.9 3.1 %collective-permute-done.5 = bf16[4,64,512]{2,1,0:T(8,128)(2,1)S(1)} collective-permute-done((bf16[4,64,512]{2,1,0:T(8,128)(2,1)S(1)}, bf16[4,64,512]{2,1,0:T(8,128)(2,1)S(1)}, u32[]{:S(2)}, u32[]{:S(2)}) %collective-permute-start.5) | collective-permute-done | bytes 262176 | tf_op jit(solution)/shard_map/ppermute | solution.py:303
  61.0 0.1 fusion.1
  61.1 1.1 %collective-permute-start.6 = (bf16[2,64,512]{2,1,0:T(8,128)(2,1)S(1)}, bf16[2,64,512]{2,1,0:T(8,128)(2,1)S(1)}, u32[]{:S(2)}, u32[]{:S(2)}) collective-permute-start(bf16[2,64,512]{2,1,0:T(8,128)(2,1)S(1)} %dynamic-slice_bitcast_fusion.2), channel_id=1, source_target_pairs={{0,2},{1,3},{2,0},{3,1},{4,6},{5,7},{6,4},{7,5},{8,10},{9,11},{10,... | collective-permute-start | bytes 393224 | tf_op jit(solution)/shard_map/ppermute | solution.py:303
  62.2 0.2 add_convert_fusion
  62.4 1.1 %collective-permute-start.1 = (bf16[4,64,640]{2,1,0:T(8,128)(2,1)S(1)}, bf16[4,64,640]{2,1,0:T(8,128)(2,1)S(1)}, u32[]{:S(2)}, u32[]{:S(2)}) collective-permute-start(bf16[4,64,640]{2,1,0:T(8,128)(2,1)S(1)} %dynamic-slice_bitcast_fusion), channel_id=1, source_target_pairs={{0,2},{1,3},{2,0},{3,1},{4,6},{5,7},{6,4},{7,5},{8,10},{9,11},{10,... | collective-permute-start | bytes 983048 | tf_op jit(solution)/shard_map/ppermute | solution.py:303
  63.5 5.5 %collective-permute-done.6 = bf16[2,64,512]{2,1,0:T(8,128)(2,1)S(1)} collective-permute-done((bf16[2,64,512]{2,1,0:T(8,128)(2,1)S(1)}, bf16[2,64,512]{2,1,0:T(8,128)(2,1)S(1)}, u32[]{:S(2)}, u32[]{:S(2)}) %collective-permute-start.6) | collective-permute-done | bytes 131104 | tf_op jit(solution)/shard_map/ppermute | solution.py:303
  69.1 3.5 %collective-permute-start.7 = (bf16[1,64,512]{2,1,0:T(8,128)(2,1)S(1)}, bf16[1,64,512]{2,1,0:T(8,128)(2,1)S(1)}, u32[]{:S(2)}, u32[]{:S(2)}) collective-permute-start(bf16[1,64,512]{2,1,0:T(8,128)(2,1)S(1)} %constant_dynamic-slice_fusion), channel_id=1, source_target_pairs={{0,8},{1,9},{2,10},{3,11},{4,12},{5,13},{6,14},{7,15},{8,0},{9,1},... | collective-permute-start | bytes 196616 | tf_op jit(solution)/shard_map/ppermute | solution.py:303
  72.5 4.0 %collective-permute-done.1 = bf16[4,64,640]{2,1,0:T(8,128)(2,1)S(1)} collective-permute-done((bf16[4,64,640]{2,1,0:T(8,128)(2,1)S(1)}, bf16[4,64,640]{2,1,0:T(8,128)(2,1)S(1)}, u32[]{:S(2)}, u32[]{:S(2)}) %collective-permute-start.1) | collective-permute-done | bytes 327712 | tf_op jit(solution)/shard_map/ppermute | solution.py:303
  76.5 0.1 fusion
  76.6 2.4 %collective-permute-start.2 = (bf16[2,64,640]{2,1,0:T(8,128)(2,1)S(1)}, bf16[2,64,640]{2,1,0:T(8,128)(2,1)S(1)}, u32[]{:S(2)}, u32[]{:S(2)}) collective-permute-start(bf16[2,64,640]{2,1,0:T(8,128)(2,1)S(1)} %dynamic-slice_bitcast_fusion.1), channel_id=1, source_target_pairs={{0,4},{1,5},{2,6},{3,7},{4,0},{5,1},{6,2},{7,3},{8,12},{9,13},{10,... | collective-permute-start | bytes 491528 | tf_op jit(solution)/shard_map/ppermute | solution.py:303
  79.1 3.5 %collective-permute-done.2 = bf16[2,64,640]{2,1,0:T(8,128)(2,1)S(1)} collective-permute-done((bf16[2,64,640]{2,1,0:T(8,128)(2,1)S(1)}, bf16[2,64,640]{2,1,0:T(8,128)(2,1)S(1)}, u32[]{:S(2)}, u32[]{:S(2)}) %collective-permute-start.2) | collective-permute-done | bytes 163872 | tf_op jit(solution)/shard_map/ppermute | solution.py:303
  82.7 2.1 %collective-permute-start.3 = (bf16[1,64,640]{2,1,0:T(8,128)(2,1)S(1)}, bf16[1,64,640]{2,1,0:T(8,128)(2,1)S(1)}, u32[]{:S(2)}, u32[]{:S(2)}) collective-permute-start(bf16[1,64,640]{2,1,0:T(8,128)(2,1)S(1)} %constant_dynamic-slice_fusion.3), channel_id=1, source_target_pairs={{0,8},{1,9},{2,10},{3,11},{4,12},{5,13},{6,14},{7,15},{8,0},{9,1},... | collective-permute-start | bytes 245768 | tf_op jit(solution)/shard_map/ppermute | solution.py:303
  84.8 0.8 copy-done.2
  85.6 5.3 %shard_map.141 = f32[512,1024]{1,0:T(8,128)} custom-call(s32[1,2,16]{2,1,0:T(2,128)} %bitcast.63, bf16[16,16,1024]{2,1,0:T(8,128)(2,1)} %copy-done.2, f32[512,1024]{1,0:T(8,128)} %get-tuple-element.19.dlocal, bf16[1024,1024]{1,0:T(8,128)(2,1)} %w_src.5), custom_call_target="tpu_custom_call" | custom-call | flops 2147483648 | bytes 4194304 | tf_op jit(solution)/shard_map/pallas_call | solution.py:280
  90.9 0.7 slice_reduce_fusion
  91.6 0.6 slice_multiply_fusion
  92.2 0.7 maximum_multiply_fusion
  (30 shorter events, 0.3 us)
Async XLA Ops:
  0.6 10.0 %copy-start.5 = (f32[100]{0:T(128)S(1)}, f32[100]{0:T(128)}, u32[]{:S(2)}) copy-start(f32[100]{0:T(128)} %param.15) | copy-start | bytes 1204
  0.6 10.7 %copy-start.6 = (f32[100]{0:T(128)S(1)}, f32[100]{0:T(128)}, u32[]{:S(2)}) copy-start(f32[100]{0:T(128)} %param.17) | copy-start | bytes 1204
  0.7 11.5 %copy-start.3 = (bf16[1024,100]{0,1:T(8,128)(2,1)S(1)}, bf16[1024,100]{0,1:T(8,128)(2,1)}, u32[]{:S(2)}) copy-start(bf16[1024,100]{0,1:T(8,128)(2,1)} %param.14) | copy-start | bytes 614404
  0.7 12.2 %copy-start.4 = (f32[100,256]{1,0:T(8,128)S(1)}, f32[100,256]{1,0:T(8,128)}, u32[]{:S(2)}) copy-start(f32[100,256]{1,0:T(8,128)} %param.16) | copy-start | bytes 307204
  3.2 22.9 %all-to-all-start = ((bf16[16,16,1152]{2,1,0:T(8,128)(2,1)}), bf16[16,16,1152]{2,1,0:T(8,128)(2,1)S(1)}, u32[]{:S(2)}, u32[]{:S(2)}) async-start(bf16[16,16,1152]{2,1,0:T(8,128)(2,1)} %shard_map.138), calls=%async_computation | async-start | bytes 1179648 | tf_op jit(solution)/shard_map/all_to_all | solution.py:348
  26.1 0.8 copy-start.1
  49.0 2.1 %collective-permute-start.4 = (bf16[8,64,512]{2,1,0:T(8,128)(2,1)}, bf16[8,64,512]{2,1,0:T(8,128)(2,1)S(1)}, u32[]{:S(2)}, u32[]{:S(2)}) collective-permute-start(bf16[8,64,512]{2,1,0:T(8,128)(2,1)} %get-tuple-element.21), channel_id=1, source_target_pairs={{0,1},{1,0},{2,3},{3,2},{4,5},{5,4},{6,7},{7,6},{8,9},{9,8},{10,11... | collective-permute-start | bytes 1572872 | tf_op jit(solution)/shard_map/ppermute | solution.py:303
  49.0 13.2 %collective-permute-start = (bf16[8,64,640]{2,1,0:T(8,128)(2,1)}, bf16[8,64,640]{2,1,0:T(8,128)(2,1)S(1)}, u32[]{:S(2)}, u32[]{:S(2)}) collective-permute-start(bf16[8,64,640]{2,1,0:T(8,128)(2,1)} %get-tuple-element.17), channel_id=1, source_target_pairs={{0,1},{1,0},{2,3},{3,2},{4,5},{5,4},{6,7},{7,6},{8,9},{9,8},{10,11... | collective-permute-start | bytes 1966088 | tf_op jit(solution)/shard_map/ppermute | solution.py:303
  51.1 11.1 %copy-start = (bf16[8,64,640]{2,1,0:T(8,128)(2,1)S(1)}, bf16[8,64,640]{2,1,0:T(8,128)(2,1)}, u32[]{:S(2)}) copy-start(bf16[8,64,640]{2,1,0:T(8,128)(2,1)} %get-tuple-element.16) | copy-start | bytes 1966084
  52.4 8.6 %collective-permute-start.5 = (bf16[4,64,512]{2,1,0:T(8,128)(2,1)S(1)}, bf16[4,64,512]{2,1,0:T(8,128)(2,1)S(1)}, u32[]{:S(2)}, u32[]{:S(2)}) collective-permute-start(bf16[4,64,512]{2,1,0:T(8,128)(2,1)S(1)} %bitcast.52), channel_id=1, source_target_pairs={{0,4},{1,5},{2,6},{3,7},{4,0},{5,1},{6,2},{7,3},{8,12},{9,13},{10,... | collective-permute-start | bytes 786440 | tf_op jit(solution)/shard_map/ppermute | solution.py:303
  54.2 30.7 %all-to-all-start.1 = ((bf16[16,16,1024]{2,1,0:T(8,128)(2,1)}), bf16[16,16,1024]{2,1,0:T(8,128)(2,1)S(1)}, u32[]{:S(2)}, u32[]{:S(2)}) async-start(bf16[16,16,1024]{2,1,0:T(8,128)(2,1)} %get-tuple-element.18), calls=%async_computation.1 | async-start | bytes 1048576 | tf_op jit(solution)/shard_map/all_to_all | solution.py:408
  61.1 7.9 %collective-permute-start.6 = (bf16[2,64,512]{2,1,0:T(8,128)(2,1)S(1)}, bf16[2,64,512]{2,1,0:T(8,128)(2,1)S(1)}, u32[]{:S(2)}, u32[]{:S(2)}) collective-permute-start(bf16[2,64,512]{2,1,0:T(8,128)(2,1)S(1)} %dynamic-slice_bitcast_fusion.2), channel_id=1, source_target_pairs={{0,2},{1,3},{2,0},{3,1},{4,6},{5,7},{6,4},{7,5},{8,10},{9,11},{10,... | collective-permute-start | bytes 393224 | tf_op jit(solution)/shard_map/ppermute | solution.py:303
  62.4 14.1 %collective-permute-start.1 = (bf16[4,64,640]{2,1,0:T(8,128)(2,1)S(1)}, bf16[4,64,640]{2,1,0:T(8,128)(2,1)S(1)}, u32[]{:S(2)}, u32[]{:S(2)}) collective-permute-start(bf16[4,64,640]{2,1,0:T(8,128)(2,1)S(1)} %dynamic-slice_bitcast_fusion), channel_id=1, source_target_pairs={{0,2},{1,3},{2,0},{3,1},{4,6},{5,7},{6,4},{7,5},{8,10},{9,11},{10,... | collective-permute-start | bytes 983048 | tf_op jit(solution)/shard_map/ppermute | solution.py:303
  69.1 10.0 %collective-permute-start.7 = (bf16[1,64,512]{2,1,0:T(8,128)(2,1)S(1)}, bf16[1,64,512]{2,1,0:T(8,128)(2,1)S(1)}, u32[]{:S(2)}, u32[]{:S(2)}) collective-permute-start(bf16[1,64,512]{2,1,0:T(8,128)(2,1)S(1)} %constant_dynamic-slice_fusion), channel_id=1, source_target_pairs={{0,8},{1,9},{2,10},{3,11},{4,12},{5,13},{6,14},{7,15},{8,0},{9,1},... | collective-permute-start | bytes 196616 | tf_op jit(solution)/shard_map/ppermute | solution.py:303
  76.6 6.0 %collective-permute-start.2 = (bf16[2,64,640]{2,1,0:T(8,128)(2,1)S(1)}, bf16[2,64,640]{2,1,0:T(8,128)(2,1)S(1)}, u32[]{:S(2)}, u32[]{:S(2)}) collective-permute-start(bf16[2,64,640]{2,1,0:T(8,128)(2,1)S(1)} %dynamic-slice_bitcast_fusion.1), channel_id=1, source_target_pairs={{0,4},{1,5},{2,6},{3,7},{4,0},{5,1},{6,2},{7,3},{8,12},{9,13},{10,... | collective-permute-start | bytes 491528 | tf_op jit(solution)/shard_map/ppermute | solution.py:303
  82.7 8.2 %collective-permute-start.3 = (bf16[1,64,640]{2,1,0:T(8,128)(2,1)S(1)}, bf16[1,64,640]{2,1,0:T(8,128)(2,1)S(1)}, u32[]{:S(2)}, u32[]{:S(2)}) collective-permute-start(bf16[1,64,640]{2,1,0:T(8,128)(2,1)S(1)} %constant_dynamic-slice_fusion.3), channel_id=1, source_target_pairs={{0,8},{1,9},{2,10},{3,11},{4,12},{5,13},{6,14},{7,15},{8,0},{9,1},... | collective-permute-start | bytes 245768 | tf_op jit(solution)/shard_map/ppermute | solution.py:303
  84.8 0.8 copy-start.2

commit v2 on v1

v2 whole, which is shorter than its diff:
```python
import functools
import math

import jax
import jax.numpy as jnp
from jax import lax
from jax.experimental import pallas as pl
from jax.experimental.pallas import tpu as pltpu
from jax.sharding import PartitionSpec as P

WSCALE = 2048
LANES = 128
ROWS = 16
alpha_fair = 0.95
smooth_sq = 0.01
MIB = 1 << 20

f32 = jnp.float32
bf16 = jnp.bfloat16
NN = (((1,), (0,)), ((), ()))
TN = (((0,), (0,)), ((), ()))
NT = (((1,), (1,)), ((), ()))
SMEM = pl.BlockSpec(memory_space=pltpu.SMEM)
VMEM = pl.BlockSpec(memory_space=pltpu.VMEM)
ANY = pl.BlockSpec(memory_space=pl.ANY)
HBM = pl.BlockSpec(memory_space=pltpu.HBM)


def spread_coef(members):
    return alpha_fair / (2.0 * members * (members - 1)) + (1.0 - alpha_fair) / (
        2.0 * members * members
    )


def mm(a, b, dims=NN):
    return lax.dot_general(a, b, dims, preferred_element_type=f32)


def round_up(value, multiple):
    return -(-value // multiple) * multiple


def split_sum(value):
    high = value.astype(bf16)
    rest = value - high.astype(f32)
    middle = rest.astype(bf16)
    return high, middle, (rest - middle.astype(f32)).astype(bf16)


def project(projected, rows, w_src):
    out = mm(rows, w_src[...])
    for c in range(projected.shape[0]):
        projected[c, : rows.shape[0], :] = out[:, c * LANES : (c + 1) * LANES]


def by_member(projected, table, first, count):
    members = table.shape[0]
    for m in range(members):
        for c in range(projected.shape[0]):
            block = projected[c, pl.ds(m, count, stride=members), :]
            table[m, first : first + count, c * LANES : (c + 1) * LANES] = block.astype(bf16)


def pack_kernel(rows_ref, latent, area, out, zeros, sem):
    shards, slots, members, _ = out.shape
    width = zeros.shape[1]
    zeros[...] = jnp.zeros_like(zeros)
    for s in range(shards):
        for b in range(slots):
            row = rows_ref[0, b, s]
            target = out.at[s, b, :, pl.ds(0, width)]

            @pl.when(row >= 0)
            def _(row=row, target=target):
                pltpu.make_async_copy(latent.at[row], target, sem).start()

            @pl.when(row < 0)
            def _(target=target):
                pltpu.make_async_copy(zeros, target, sem).start()

    total = jnp.sum(area[...], axis=1, keepdims=True) + jnp.zeros((members, LANES), f32)
    lane = lax.broadcasted_iota(jnp.int32, (members, LANES), 1)
    tail = jnp.zeros((members, LANES), f32)
    for i, piece in enumerate(split_sum(total)):
        tail = jnp.where(lane == i, piece.astype(f32), tail)
    tail = tail.astype(bf16)
    for s in range(shards):
        for b in range(slots):
            out[s, b, :, width:] = tail
    for s in range(shards):
        for b in range(slots):
            pltpu.make_async_copy(zeros, out.at[s, b, :, pl.ds(0, width)], sem).wait()


def local_kernel(
    latent,
    w_src,
    edge_src,
    edge_coef,
    b_hidden,
    w_out_t,
    b_out,
    targets,
    var_weight,
    area_weight,
    table,
    edge_gr,
    edge_rg,
    w_out_pad,
    w_out_t_pad,
    b_out_pad,
    truth,
    weighting,
    w_src_t,
    projected,
    wide,
    tall,
):
    members, rows_pad, width = table.shape
    rows, points = edge_rg.shape
    mesh_rows = latent.shape[0] // members
    variables = w_out_t.shape[0]
    project(projected, latent[...], w_src)
    by_member(projected, table, 0, mesh_rows)

    row = lax.broadcasted_iota(jnp.int32, (rows_pad, points), 0)
    matrix = jnp.where((row >= rows) & (row < rows + 2), 1.0, 0.0).astype(f32)
    for k in range(edge_src.shape[0]):
        matrix = matrix + jnp.where(
            row == edge_src[k : k + 1, :], edge_coef[k : k + 1, :], 0.0
        )
    edge_rg[...] = matrix[:rows].astype(bf16)
    edge_gr[...] = matrix.T.astype(bf16)

    bias = b_hidden[...]
    high, low, _ = split_sum(bias)
    at = lax.broadcasted_iota(jnp.int32, (rows_pad - rows, width), 0)
    bias_rows = jnp.where(
        at == 0, high.astype(f32), jnp.where(at == 1, low.astype(f32), 0.0)
    ).astype(bf16)
    for m in range(members):
        table[m, rows:, :] = bias_rows

    wide[...] = jnp.zeros_like(wide)
    wide[:variables, :] = w_out_t[...].astype(f32)
    w_out_t_pad[...] = wide[...].astype(bf16)
    w_out_pad[...] = wide[...].T.astype(bf16)
    tall[...] = jnp.zeros_like(tall)
    tall[:variables, :] = targets[...]
    truth[...] = tall[...].T
    b_out_pad[...] = jnp.zeros_like(b_out_pad)
    b_out_pad[:, :variables] = b_out[...]
    weighting[...] = jnp.zeros_like(weighting)
    column = jnp.broadcast_to(area_weight[...], (LANES, points)).T
    w_src_t[...] = w_src[...].T
    weighting[:, :variables] = column[:, :variables] * var_weight[...]


def decoder_kernel(
    me_ref,
    arrived,
    w_src_hbm,
    table_hbm,
    edge_gr_hbm,
    w_out_hbm,
    b_out_hbm,
    truth_hbm,
    weighting_hbm,
    w_out_t_hbm,
    edge_rg_hbm,
    latent_hbm,
    dlocal_hbm,
    slot_grad_hbm,
    keep_a,
    send_a,
    keep_b,
    send_b,
    w_src,
    table,
    edge_gr,
    w_out_pad,
    b_out_pad,
    truth,
    weighting,
    w_out_t_pad,
    edge_rg,
    latent,
    hidden,
    slope,
    preact,
    pred,
    dpred,
    dtable,
    dlocal,
    slot_grad,
    partial,
    partial_b,
    sem,
    *,
    points_all,
    variables,
):
    members, rows_pad, width = table.shape
    shards, per_pair, _ = arrived.shape
    received = shards * per_pair
    rows, points = edge_rg.shape
    own = latent.shape[0]
    mesh_rows = own // members
    var_pad = w_out_pad.shape[1]
    me = me_ref[0]

    sources = (
        w_src_hbm,
        table_hbm,
        edge_gr_hbm,
        w_out_hbm,
        b_out_hbm,
        truth_hbm,
        weighting_hbm,
        w_out_t_hbm,
        edge_rg_hbm,
        latent_hbm,
    )
    targets = (
        w_src,
        table,
        edge_gr,
        w_out_pad,
        b_out_pad,
        truth,
        weighting,
        w_out_t_pad,
        edge_rg,
        latent,
    )
    loads = [
        pltpu.make_async_copy(source, target, sem.at[i])
        for i, (source, target) in enumerate(zip(sources, targets, strict=True))
    ]
    loads[0].start()

    loads[0].wait()
    for load in loads[1:]:
        load.start()
    arrived_rows = arrived[:, :, :width].reshape(received, width)
    project(dtable, arrived_rows, w_src)
    loads[1].wait()
    by_member(dtable, table, mesh_rows, received // members)
    for load in loads[2:]:
        load.wait()

    tail = arrived[:, :, width:].astype(f32)
    at_row = lax.broadcasted_iota(jnp.int32, tail.shape, 1)
    at_lane = lax.broadcasted_iota(jnp.int32, tail.shape, 2)
    tail = jnp.where((at_row == 0) & (at_lane < 3), tail, 0.0)
    mean_area = jnp.sum(jnp.sum(tail, axis=0), keepdims=True) / points_all

    c0 = math.sqrt(2.0 / math.pi)
    c1 = c0 * 0.044715
    quarter = width // 4

    def gather(m, slot, c):
        left, right = c * quarter, (c + 1) * quarter
        preact[slot, :, left:right] = mm(edge_gr[...], table[m, :, left:right])

    for c in range(4):
        gather(0, 0, c)

    def forward(pair, _):
        for slot in range(2):
            m = pair * 2 + slot
            first = pl.multiple_of(m * points, points)
            following = jnp.minimum(m + 1, members - 1)
            for c in range(4):
                left, right = c * quarter, (c + 1) * quarter
                gather(following, 1 - slot, c)
                for r in range(0, points, ROWS):
                    x = preact[slot, r : r + ROWS, left:right]
                    x2 = x * x
                    t = jnp.tanh(x * (c0 + c1 * x2))
                    cdf = 0.5 + 0.5 * t
                    hidden[pl.ds(first + r, ROWS), left:right] = (x * cdf).astype(bf16)
                    bend = (1.0 - t) * (x * (c0 + (3.0 * c1) * x2)) + 1.0
                    slope[pl.ds(first + r, ROWS), left:right] = (cdf * bend).astype(bf16)
            pred[m] = mm(hidden[pl.ds(first, points), :], w_out_pad[...]) + b_out_pad[...]
        return 0

    lax.fori_loop(0, members // 2, forward, 0)

    spread = spread_coef(members)
    inverse_mean = 1.0 / mean_area
    loss_sum = jnp.zeros((ROWS, LANES), f32)
    for left in range(0, var_pad, LANES):

        def score(block, loss_sum, left=left):
            at = pl.ds(pl.multiple_of(block * ROWS, ROWS), ROWS)
            p = [pred[m, at, left : left + LANES] for m in range(members)]
            true = truth[at, left : left + LANES]
            weight = weighting[at, left : left + LANES]
            fit = jnp.zeros((ROWS, LANES), f32)
            grads = []
            for m in range(members):
                d = p[m] - true
                q = d * d + smooth_sq
                r = lax.rsqrt(q)
                fit = fit + q * r
                grads.append(d * r * (1.0 / members))
            pairs = jnp.zeros((ROWS, LANES), f32)
            apart = [jnp.zeros((ROWS, LANES), f32) for _ in range(members)]
            for j in range(members):
                for k in range(j + 1, members):
                    d = p[j] - p[k]
                    q = d * d + smooth_sq
                    r = lax.rsqrt(q)
                    pairs = pairs + q * r
                    s = d * r
                    apart[j] = apart[j] + s
                    apart[k] = apart[k] - s
            scaled = weight * inverse_mean
            for m in range(members):
                gradient = grads[m] - (2.0 * spread) * apart[m]
                dpred[m, at, left : left + LANES] = (gradient * scaled).astype(bf16)
            return loss_sum + weight * (fit * (1.0 / members) - (2.0 * spread) * pairs)

        loss_sum = lax.fori_loop(0, points // ROWS, score, loss_sum)
    loss = jnp.sum(loss_sum, keepdims=True) * (inverse_mean / points_all)

    for m in range(members):
        first = m * points
        grad = mm(dpred[m], w_out_t_pad[...])
        grad = (grad * slope[first : first + points, :].astype(f32)).astype(bf16)
        grad = mm(edge_rg[...], grad)
        for c in range(width // LANES):
            dtable[c, pl.ds(m, rows, stride=members), :] = grad[:, c * LANES : (c + 1) * LANES]

    for c in range(width // LANES):
        left, right = c * LANES, (c + 1) * LANES
        dlocal[:, left:right] = dtable[c, :own, :].astype(bf16)
        slot_grad[:, :, left:right] = (
            dtable[c, own:, :].astype(bf16).reshape(shards, per_pair, LANES)
        )
    stores = [
        pltpu.make_async_copy(slot_grad, slot_grad_hbm, sem.at[0]),
        pltpu.make_async_copy(dlocal, dlocal_hbm, sem.at[1]),
    ]
    for store in stores:
        store.start()

    half_width = width // 2
    pairs, _, own_rows, columns = partial.shape
    core = lax.rem(me, 2)
    grad = mm(dpred[...].reshape(members * points, var_pad), hidden[...], TN).T
    row = lax.broadcasted_iota(jnp.int32, grad.shape, 0)
    lane = lax.broadcasted_iota(jnp.int32, grad.shape, 1)
    row = row & (own_rows - 1)
    grad = jnp.where(lane < variables, grad, 0.0)
    for i, piece in enumerate(split_sum(loss)[:2]):
        place = me * 2 + i
        here = (row == lax.rem(place, own_rows)) & (lane == variables + place // own_rows)
        grad = jnp.where(here, piece.astype(f32), grad)
    partial[:, :, :, half_width:] = grad.astype(bf16).reshape(
        pairs, 2, own_rows, columns - half_width
    )
    back = slot_grad[...].reshape(received, width)
    for c, (keep, send) in enumerate(((keep_a, send_a), (keep_b, send_b))):
        left, right = c * half_width, (c + 1) * half_width
        grad = mm(latent[...], dlocal[:, left:right], TN)
        grad = grad + mm(arrived_rows, back[:, left:right], TN)
        part = partial if c == 0 else partial_b
        part[:, :, :, :half_width] = grad.astype(bf16).reshape(
            pairs, 2, own_rows, half_width
        )
        for i, (half, target) in enumerate(((1 - core, send), (core, keep))):
            stores.append(pltpu.make_async_copy(part.at[:, half], target, sem.at[2 + 2 * c + i]))
            stores[-1].start()
    for store in stores:
        store.wait()


def halve_kernel(me_ref, keep_a, got_a, keep_b, got_b, *rest, bits):
    outs = rest[-4:]
    for i, (keep, got, bit) in enumerate(
        ((keep_a, got_a, bits[0]), (keep_b, got_b, bits[1]))
    ):
        mine = lax.rem(me_ref[0] // bit, 2)
        for out, half in ((outs[2 * i + 1], 1 - mine), (outs[2 * i], mine)):
            total = keep[:, half].astype(f32) + got[:, half].astype(f32)
            out[...] = total.astype(bf16)


def final_kernel(keep_a, got_a, keep_b, got_b, grad_w_src, grad_w_out, loss, *, scale):
    variables = grad_w_out.shape[1]
    half_width = grad_w_src.shape[1] // 2
    total = keep_a[0].astype(f32) + got_a[0].astype(f32)
    grad_w_src[:, :half_width] = total[:, :half_width] * scale
    grad_w_src[:, half_width:] = (keep_b[0].astype(f32) + got_b[0].astype(f32)) * scale
    out = total[:, half_width:]
    grad_w_out[...] = out[:, :variables] * scale
    lane = lax.broadcasted_iota(jnp.int32, out.shape, 1)
    loss[...] = jnp.sum(jnp.where(lane >= variables, out, 0.0), keepdims=True)


def latent_grad_kernel(
    rows_ref, returned, dlocal_hbm, w_src_t_hbm, _, out_hbm, selector, dlocal, w_src_t, out, sem
):
    shards, per_pair, width = returned.shape
    _, slots, _ = rows_ref.shape
    members = per_pair // slots
    loads = [
        pltpu.make_async_copy(w_src_t_hbm, w_src_t, sem.at[0]),
        pltpu.make_async_copy(dlocal_hbm, dlocal, sem.at[1]),
    ]
    for load in loads:
        load.start()
    lane = lax.broadcasted_iota(jnp.int32, (members, selector.shape[1]), 1)
    member = lax.broadcasted_iota(jnp.int32, (members, selector.shape[1]), 0)
    for s in range(shards):
        for b in range(slots):
            first = (s * slots + b) * members
            selector[first : first + members, :] = jnp.where(
                lane == rows_ref[0, b, s] * members + member, 1.0, 0.0
            ).astype(f32)
    back = returned[...].reshape(shards * per_pair, width)
    spread = mm(selector[...].astype(bf16), back, TN)
    for load in loads:
        load.wait()
    total = (dlocal[...].astype(f32) + spread).astype(bf16)
    stores = []
    chunk = width // 4
    for i in range(4):
        part = pl.ds(i * chunk, chunk)
        out[:, part] = mm(total, w_src_t[:, part])
        stores.append(
            pltpu.make_async_copy(out.at[:, part], out_hbm.at[:, part], sem.at[2 + i])
        )
        stores[-1].start()
    for store in stores:
        store.wait()


def size_of(x):
    return math.prod(x.shape) * jnp.dtype(x.dtype).itemsize


def call(kernel, out_shape, in_specs, scratch, cost, *args, out_specs=None, limit=None):
    single = not isinstance(out_shape, (list, tuple))
    outs = [out_shape] if single else list(out_shape)
    specs = out_specs or [VMEM] * len(outs)
    used = sum(size_of(x) for x, s in zip(args, in_specs, strict=True) if s is VMEM)
    used += sum(size_of(x) for x, s in zip(outs, specs, strict=True) if s is VMEM)
    used += sum(size_of(x) for x in scratch if getattr(x, "dtype", None) in (f32, bf16))
    limit = min(limit or used + used // 4 + 6 * MIB, 60 * MIB)
    return pl.pallas_call(
        kernel,
        out_shape=out_shape,
        in_specs=in_specs,
        out_specs=specs[0] if single else specs,
        scratch_shapes=scratch,
        compiler_params=pltpu.CompilerParams(vmem_limit_bytes=limit),
        cost_estimate=pl.CostEstimate(flops=cost, bytes_accessed=used, transcendentals=0),
    )(*args)


def swap(value, bit, shards):
    return lax.ppermute(value, "space", [(i, i ^ bit) for i in range(shards)])


def per_device(
    latent,
    w_src,
    b_hidden,
    w_out,
    b_out,
    targets,
    var_weight,
    area_weight,
    edge_src,
    edge_coef,
    send_rows,
):
    mesh_rows, members, width = latent.shape
    shards = lax.axis_size("space")
    slots = send_rows.shape[2]
    variables, points = targets.shape
    points_all = points * shards
    own_rows = width // shards
    per_pair = slots * members
    rows = mesh_rows + shards * slots
    rows_pad = round_up(rows + 2, ROWS)
    loss_columns = round_up(2 * shards, own_rows) // own_rows
    var_pad = round_up(variables + loss_columns, LANES)
    half_width = width // 2
    shape = jax.ShapeDtypeStruct
    me = lax.axis_index("space").astype(jnp.int32).reshape(1)

    latent_rows = latent.reshape(mesh_rows * members, width)
    slot_rows = jnp.swapaxes(send_rows, 1, 2)
    area_row = area_weight.reshape(1, points)
    outgoing = call(
        pack_kernel,
        shape((shards, slots, members, width + LANES), bf16),
        [SMEM, ANY, VMEM],
        [pltpu.VMEM((members, width), bf16), pltpu.SemaphoreType.DMA],
        1 << 24,
        slot_rows,
        latent,
        area_row,
        limit=56 * MIB,
    )
    arrived = lax.all_to_all(outgoing, "space", split_axis=0, concat_axis=0, tiled=True)
    arrived = arrived.reshape(shards, per_pair, width + LANES)

    columns = (half_width + var_pad, half_width)
    table, edge_gr, edge_rg, w_out_pad, w_out_t_pad, b_out_pad, truth, weighting, w_src_t = call(
        local_kernel,
        [
            shape((members, rows_pad, width), bf16),
            shape((points, rows_pad), bf16),
            shape((rows, points), bf16),
            shape((width, var_pad), bf16),
            shape((var_pad, width), bf16),
            shape((1, var_pad), f32),
            shape((points, var_pad), f32),
            shape((points, var_pad), f32),
            shape((width, width), bf16),
        ],
        [VMEM] * 10,
        [
            pltpu.VMEM((width // LANES, mesh_rows * members, LANES), f32),
            pltpu.VMEM((var_pad, width), f32),
            pltpu.VMEM((var_pad, points), f32),
        ],
        1 << 31,
        latent_rows,
        w_src,
        edge_src.T,
        edge_coef.T,
        b_hidden.reshape(1, width),
        w_out.T,
        b_out.reshape(1, variables),
        targets,
        var_weight.reshape(1, variables),
        area_row,
        limit=56 * MIB,
    )

    operands = (
        w_src,
        table,
        edge_gr,
        w_out_pad,
        b_out_pad,
        truth,
        weighting,
        w_out_t_pad,
        edge_rg,
        latent_rows,
    )
    dlocal, slot_grad, *pieces = call(
        functools.partial(decoder_kernel, points_all=points_all, variables=variables),
        [
            shape((mesh_rows * members, width), bf16),
            shape((shards, per_pair, width), bf16),
            *[shape((shards // 2, own_rows, n), bf16) for n in columns for _ in range(2)],
        ],
        [SMEM, VMEM] + [HBM] * len(operands),
        [
            *[pltpu.VMEM(x.shape, x.dtype) for x in operands],
            pltpu.VMEM((members * points, width), bf16),
            pltpu.VMEM((members * points, width), bf16),
            pltpu.VMEM((2, points, width), f32),
            pltpu.VMEM((members, points, var_pad), f32),
            pltpu.VMEM((members, points, var_pad), bf16),
            pltpu.VMEM((width // LANES, rows * members, LANES), f32),
            pltpu.VMEM((mesh_rows * members, width), bf16),
            pltpu.VMEM((shards, per_pair, width), bf16),
            pltpu.VMEM((shards // 2, 2, own_rows, columns[0]), bf16),
            pltpu.VMEM((shards // 2, 2, own_rows, columns[1]), bf16),
            pltpu.SemaphoreType.DMA((len(operands),)),
        ],
        1 << 34,
        me,
        arrived,
        *operands,
        out_specs=[HBM] * 6,
        limit=56 * MIB,
    )

    returned = lax.all_to_all(slot_grad, "space", split_axis=0, concat_axis=0, tiled=True)

    levels = [1 << i for i in reversed(range(1, shards.bit_length() - 1))]
    order_a = levels[::-1]
    order_b = order_a[1:2] + order_a[:1] + order_a[2:]
    left = [list(levels), list(levels)]
    count = shards // 2
    got = [swap(pieces[1], 1, shards), swap(pieces[3], 1, shards)]
    for step, bits in enumerate(zip(order_a, order_b, strict=True)):
        views = []
        for i, bit in enumerate(bits):
            place = left[i].index(bit)
            left[i].remove(bit)
            split = (1 << place, 2, count >> (place + 1), own_rows, columns[i])
            views += [pieces[2 * i].reshape(split), got[i].reshape(split)]
        count //= 2
        halves = [(x.shape[0], *x.shape[2:]) for x in views[::2] for _ in range(2)]
        pieces = call(
            functools.partial(halve_kernel, bits=bits),
            [shape(x, bf16) for x in halves],
            [SMEM] + [VMEM] * len(views),
            [],
            1 << 24,
            me,
            *views,
        )
        pieces = [x.reshape(count, *x.shape[2:]) for x in pieces]
        got = [swap(pieces[2 * i + 1], bit, shards) for i, bit in enumerate(bits)]

    grad_latent = call(
        latent_grad_kernel,
        shape((mesh_rows * members, width), f32),
        [SMEM, VMEM, HBM, HBM, ANY],
        [
            pltpu.VMEM((shards * per_pair, mesh_rows * members), f32),
            pltpu.VMEM((mesh_rows * members, width), bf16),
            pltpu.VMEM((width, width), bf16),
            pltpu.VMEM((mesh_rows * members, width), f32),
            pltpu.SemaphoreType.DMA((6,)),
        ],
        1 << 32,
        slot_rows,
        returned,
        dlocal,
        w_src_t,
        pieces[0],
        out_specs=[HBM],
        limit=56 * MIB,
    )
    grad_w_src, grad_w_out, loss = call(
        functools.partial(final_kernel, scale=WSCALE / points_all),
        [
            shape((own_rows, width), f32),
            shape((own_rows, variables), f32),
            shape((1, 1), f32),
        ],
        [VMEM] * 4,
        [],
        1 << 24,
        pieces[0],
        got[0],
        pieces[2],
        got[1],
    )
    return (
        loss.reshape(1),
        grad_latent.reshape(mesh_rows, members, width),
        grad_w_src,
        grad_w_out,
    )


def solution(mesh):
    placed = (
        P(("groups", "space"), None, None),
        P(),
        P(),
        P(),
        P(),
        P(None, ("groups", "space")),
        P(),
        P("space"),
        P("space", None),
        P("space", None),
        P("space", None, None),
    )
    return jax.shard_map(
        per_device,
        mesh=mesh,
        in_specs=placed,
        out_specs=(
            P("groups"),
            P(("groups", "space"), None, None),
            P(("groups", "space"), None),
            P(("groups", "space"), None),
        ),
        check_vma=False,
    )
```

time: 93.3 us -> 87.4 us (0.937)
  other arithmetic: 3.72 us -> 0 us
  starting transfers between devices: 23.5 us -> 20.8 us
  Pallas kernels: 34.2 us -> 35.7 us
    ppermute x8, starting transfers between devices: 12.4 us -> 9.08 us  [swap(): return lax.ppermute(value, 'space', [(i, i ^ bit) for i in range(shards)])]
    unnamed x14 -> x12, local copies, waits for them, and re-layouts: 1.62 us -> 4.37 us
    ppermute x8, waiting for transfers between devices: 17.7 us -> 15.3 us  [swap(): return lax.ppermute(value, 'space', [(i, i ^ bit) for i in range(shards)])]
    convert_element_type x6 -> x0, other arithmetic: 1.66 us -> none  [the longest x3 1.36 us: per_device(): sum_b = (keep_b.astype(f32) + got_b.astype(f32)).astype(bf16)]
    reshape x7 -> x0, local copies, waits for them, and re-layouts: 1.57 us -> none  [the longest x2 0.76 us: per_device(): b_out_column = jnp.pad(b_out, (0, var_pad - variables)).reshape(var_pad, 1)]
    all_to_all x1, waiting for transfers between devices: 8.31 us -> 9.85 us  [per_device(): lax.all_to_all(outgoing, 'space', split_axis=0, concat_axis=0, tiled=True)]
    pallas_call x4 -> x8, Pallas kernels: 34.2 us -> 35.7 us  [call(): pl.pallas_call(kernel, out_shape=out_shape, in_specs=in_specs, out_specs=...]
    pad x2 -> x0, local copies, waits for them, and re-layouts: 1.39 us -> none  [the longest x1 0.73 us: per_device(): w_out_t = jnp.pad(w_out.T, ((0, var_pad - variables), (0, 0)))]
  transfers between devices with their start and end apart: 10 -> 10, of which waited for: 6 -> 4; matrix products, arithmetic and copies ran while one was open for 5% -> 0% of each run, Pallas kernels for 10% -> 13%
where the time goes in v2:
time: 87.4 us; the launch traced here: 86.8 us
  Pallas kernels  35.7 us (41%)
  waiting for transfers between devices  25.2 us (29%)
  starting transfers between devices  20.8 us (24%)
  local copies, waits for them, and re-layouts  4.37 us (5%)
    pallas_call x8, Pallas kernels, call(): pl.pallas_call(kernel, out_shape=out_shape, in_specs=in_specs, out_specs=...  35.7 us
    ppermute x8, waiting for transfers between devices, swap(): return lax.ppermute(value, 'space', [(i, i ^ bit) for i in range(shards)])  15.3 us
    all_to_all x1, waiting for transfers between devices, per_device(): lax.all_to_all(outgoing, 'space', split_axis=0, concat_axis=0, tiled=True)  9.85 us
    ppermute x8, starting transfers between devices, swap(): return lax.ppermute(value, 'space', [(i, i ^ bit) for i in range(shards)])  9.08 us
    all_to_all x1, starting transfers between devices, per_device(): lax.all_to_all(outgoing, 'space', split_axis=0, concat_axis=0, tiled=True)  7.33 us
    all_to_all x1, starting transfers between devices, per_device(): lax.all_to_all(slot_grad, 'space', split_axis=0, concat_axis=0, tiled=True)  4.43 us
    unnamed x12, local copies, waits for them, and re-layouts  4.37 us
  transfers between devices with their start and end apart: 10, of which 4 were waited for; matrix products, arithmetic and copies ran while one was open for 0% of the time, Pallas kernels for 13%

profile of v2, /device:TPU:0, one launch (start us, length us, event | category | flops | bytes accessed | tf_op | source)
XLA Modules:
  0.0 86.8 jit_solution(5817391867847068398)
XLA Ops:
  0.6 2.7 %shard_map.138 = bf16[16,2,8,1152]{3,2,1,0:T(8,128)(2,1)} custom-call(s32[1,2,16]{2,1,0:T(2,128)} %bitcast.59, bf16[64,8,1024]{2,1,0:T(8,128)(2,1)} %latent.1, f32[1,256]{1,0:T(1,128)} %bitcast.57), custom_call_target="tpu_custom_call" | custom-call | flops 16777216 | bytes 607232 | tf_op jit(solution)/shard_map/pallas_call | solution.py:453
  3.3 7.3 %all-to-all-start = ((bf16[16,2,8,1152]{3,2,1,0:T(8,128)(2,1)}), bf16[16,2,8,1152]{3,2,1,0:T(8,128)(2,1)S(1)}, u32[]{:S(2)}, u32[]{:S(2)}) async-start(bf16[16,2,8,1152]{3,2,1,0:T(8,128)(2,1)} %shard_map.138), calls=%async_computation | async-start | bytes 1179648 | tf_op jit(solution)/shard_map/all_to_all | solution.py:510
  10.7 5.7 %shard_map.139 = (bf16[8,112,1024]{2,1,0:T(8,128)(2,1)}, bf16[256,112]{1,0:T(8,128)(2,1)}, bf16[96,256]{1,0:T(8,128)(2,1)}, bf16[1024,128]{1,0:T(8,128)(2,1)}, b...) custom-call(bf16[512,1024]{1,0:T(8,128)(2,1)} %bitcast.54, ...), custom_call_target="tpu_custom_call" | custom-call | flops 2147483648 | bytes 11043104 | tf_op jit(solution)/shard_map/pallas_call | solution.py:453
  16.4 9.9 %all-to-all-done = bf16[16,2,8,1152]{3,2,1,0:T(8,128)(2,1)S(1)} async-done(((bf16[16,2,8,1152]{3,2,1,0:T(8,128)(2,1)}), bf16[16,2,8,1152]{3,2,1,0:T(8,128)(2,1)S(1)}, u32[]{:S(2)}, u32[]{:S(2)}) %all-to-all-start) | async-done | bytes 589856 | tf_op jit(solution)/shard_map/all_to_all | solution.py:510
  26.2 0.8 copy-done.4
  27.0 20.8 %shard_map.140 = (bf16[512,1024]{1,0:T(8,128)(2,1)}, bf16[16,16,1024]{2,1,0:T(8,128)(2,1)}, bf16[8,64,640]{2,1,0:T(8,128)(2,1)}, bf16[8,64,640]{2,1,0:T(8,128)(2...) custom-call(s32[1]{0:T(128)} %bitcast.me_ref, bf16[16,16,1152]{2,1,0:T(8,128)(2,1)} %bitcast.56, ...), custom_call_target="tpu_custom_call" | custom-call | flops 17179869184 | bytes 25600512 | tf_op jit(solution)/shard_map/pallas_call | solution.py:453
  47.8 0.1 collective-permute-start
  47.9 0.5 collective-permute-start.1
  48.4 4.4 %all-to-all-start.1 = ((bf16[16,16,1024]{2,1,0:T(8,128)(2,1)}), bf16[16,16,1024]{2,1,0:T(8,128)(2,1)S(1)}, u32[]{:S(2)}, u32[]{:S(2)}) async-start(bf16[16,16,1024]{2,1,0:T(8,128)(2,1)} %get-tuple-element.59), calls=%async_computation.1 | async-start | bytes 1048576 | tf_op jit(solution)/shard_map/all_to_all | solution.py:589
  52.8 0.0 collective-permute-done.1
  52.9 0.0 collective-permute-done
  52.9 1.1 %copy-done = bf16[8,64,640]{2,1,0:T(8,128)(2,1)S(1)} copy-done((bf16[8,64,640]{2,1,0:T(8,128)(2,1)S(1)}, bf16[8,64,640]{2,1,0:T(8,128)(2,1)}, u32[]{:S(2)}) %copy-start) | copy-done | bytes 655384
  54.0 1.0 %copy-done.1 = bf16[8,64,512]{2,1,0:T(8,128)(2,1)S(1)} copy-done((bf16[8,64,512]{2,1,0:T(8,128)(2,1)S(1)}, bf16[8,64,512]{2,1,0:T(8,128)(2,1)}, u32[]{:S(2)}) %copy-start.1) | copy-done | bytes 524312
  55.0 0.3 shard_map.141
  55.3 2.0 %collective-permute-start.2 = (bf16[4,64,640]{2,1,0:T(8,128)(2,1)S(1)}, bf16[4,64,640]{2,1,0:T(8,128)(2,1)S(1)}, u32[]{:S(2)}, u32[]{:S(2)}) collective-permute-start(bf16[4,64,640]{2,1,0:T(8,128)(2,1)S(1)} %bitcast.48), channel_id=1, source_target_pairs={{0,2},{1,3},{2,0},{3,1},{4,6},{5,7},{6,4},{7,5},{8,10},{9,11},{10,... | collective-permute-start | bytes 983048 | tf_op jit(solution)/shard_map/ppermute | solution.py:465
  57.3 1.5 %collective-permute-start.3 = (bf16[4,64,512]{2,1,0:T(8,128)(2,1)S(1)}, bf16[4,64,512]{2,1,0:T(8,128)(2,1)S(1)}, u32[]{:S(2)}, u32[]{:S(2)}) collective-permute-start(bf16[4,64,512]{2,1,0:T(8,128)(2,1)S(1)} %bitcast.49), channel_id=1, source_target_pairs={{0,4},{1,5},{2,6},{3,7},{4,0},{5,1},{6,2},{7,3},{8,12},{9,13},{10,... | collective-permute-start | bytes 786440 | tf_op jit(solution)/shard_map/ppermute | solution.py:465
  58.7 11.3 %collective-permute-done.3 = bf16[4,64,512]{2,1,0:T(8,128)(2,1)S(1)} collective-permute-done((bf16[4,64,512]{2,1,0:T(8,128)(2,1)S(1)}, bf16[4,64,512]{2,1,0:T(8,128)(2,1)S(1)}, u32[]{:S(2)}, u32[]{:S(2)}) %collective-permute-start.3) | collective-permute-done | bytes 262176 | tf_op jit(solution)/shard_map/ppermute | solution.py:465
  70.0 0.0 collective-permute-done.2
  70.0 0.1 shard_map.142
  70.2 1.0 %collective-permute-start.4 = (bf16[2,64,640]{2,1,0:T(8,128)(2,1)S(1)}, bf16[2,64,640]{2,1,0:T(8,128)(2,1)S(1)}, u32[]{:S(2)}, u32[]{:S(2)}) collective-permute-start(bf16[2,64,640]{2,1,0:T(8,128)(2,1)S(1)} %bitcast.50), channel_id=1, source_target_pairs={{0,4},{1,5},{2,6},{3,7},{4,0},{5,1},{6,2},{7,3},{8,12},{9,13},{10,... | collective-permute-start | bytes 491528 | tf_op jit(solution)/shard_map/ppermute | solution.py:465
  71.2 1.1 %collective-permute-start.5 = (bf16[2,64,512]{2,1,0:T(8,128)(2,1)S(1)}, bf16[2,64,512]{2,1,0:T(8,128)(2,1)S(1)}, u32[]{:S(2)}, u32[]{:S(2)}) collective-permute-start(bf16[2,64,512]{2,1,0:T(8,128)(2,1)S(1)} %bitcast.51), channel_id=1, source_target_pairs={{0,2},{1,3},{2,0},{3,1},{4,6},{5,7},{6,4},{7,5},{8,10},{9,11},{10,... | collective-permute-start | bytes 393224 | tf_op jit(solution)/shard_map/ppermute | solution.py:465
  72.3 3.9 %collective-permute-done.5 = bf16[2,64,512]{2,1,0:T(8,128)(2,1)S(1)} collective-permute-done((bf16[2,64,512]{2,1,0:T(8,128)(2,1)S(1)}, bf16[2,64,512]{2,1,0:T(8,128)(2,1)S(1)}, u32[]{:S(2)}, u32[]{:S(2)}) %collective-permute-start.5) | collective-permute-done | bytes 131104 | tf_op jit(solution)/shard_map/ppermute | solution.py:465
  76.2 0.0 collective-permute-done.4
  76.2 0.1 shard_map.143
  76.3 0.0 copy-start.2
  76.3 0.6 copy-done.2
  76.9 2.3 %collective-permute-start.7 = (bf16[1,64,512]{2,1,0:T(8,128)(2,1)S(1)}, bf16[1,64,512]{2,1,0:T(8,128)(2,1)S(1)}, u32[]{:S(2)}, u32[]{:S(2)}) collective-permute-start(bf16[1,64,512]{2,1,0:T(8,128)(2,1)S(1)} %bitcast.53), channel_id=1, source_target_pairs={{0,8},{1,9},{2,10},{3,11},{4,12},{5,13},{6,14},{7,15},{8,0},{9,1},... | collective-permute-start | bytes 196616 | tf_op jit(solution)/shard_map/ppermute | solution.py:465
  79.2 0.6 collective-permute-start.6
  79.8 0.8 copy-done.5
  80.6 5.3 %shard_map.145 = f32[512,1024]{1,0:T(8,128)} custom-call(s32[1,2,16]{2,1,0:T(2,128)} %bitcast.60, bf16[16,16,1024]{2,1,0:T(8,128)(2,1)} %copy-done.5, bf16[512,1024]{1,0:T(8,128)(2,1)} %get-tuple-element.60.dlocal_hbm, bf16[1024,1024]{1,0:T(8,128)(2,1)} %get-tuple-element.61.w_src_t_hbm, bf16[1,64,640]{2,1,0:T(8,128)(2,1)} %bitcast.45), custom_call_target="tpu_custom_call" | custom-call | flops 4294967296 | bytes 6291456 | tf_op jit(solution)/shard_map/pallas_call | solution.py:453
  85.9 0.1 collective-permute-done.6.got_a
  86.0 0.8 shard_map.144
  (8 shorter events, 0.0 us)
Async XLA Ops:
  3.3 22.9 %all-to-all-start = ((bf16[16,2,8,1152]{3,2,1,0:T(8,128)(2,1)}), bf16[16,2,8,1152]{3,2,1,0:T(8,128)(2,1)S(1)}, u32[]{:S(2)}, u32[]{:S(2)}) async-start(bf16[16,2,8,1152]{3,2,1,0:T(8,128)(2,1)} %shard_map.138), calls=%async_computation | async-start | bytes 1179648 | tf_op jit(solution)/shard_map/all_to_all | solution.py:510
  26.2 0.8 copy-start.4
  47.8 5.0 %collective-permute-start = (bf16[8,64,640]{2,1,0:T(8,128)(2,1)}, bf16[8,64,640]{2,1,0:T(8,128)(2,1)S(1)}, u32[]{:S(2)}, u32[]{:S(2)}) collective-permute-start(bf16[8,64,640]{2,1,0:T(8,128)(2,1)} %get-tuple-element.43), channel_id=1, source_target_pairs={{0,1},{1,0},{2,3},{3,2},{4,5},{5,4},{6,7},{7,6},{8,9},{9,8},{10,11... | collective-permute-start | bytes 1966088 | tf_op jit(solution)/shard_map/ppermute | solution.py:465
  47.9 4.9 %collective-permute-start.1 = (bf16[8,64,512]{2,1,0:T(8,128)(2,1)}, bf16[8,64,512]{2,1,0:T(8,128)(2,1)S(1)}, u32[]{:S(2)}, u32[]{:S(2)}) collective-permute-start(bf16[8,64,512]{2,1,0:T(8,128)(2,1)} %get-tuple-element.45), channel_id=1, source_target_pairs={{0,1},{1,0},{2,3},{3,2},{4,5},{5,4},{6,7},{7,6},{8,9},{9,8},{10,11... | collective-permute-start | bytes 1572872 | tf_op jit(solution)/shard_map/ppermute | solution.py:465
  48.4 31.4 %all-to-all-start.1 = ((bf16[16,16,1024]{2,1,0:T(8,128)(2,1)}), bf16[16,16,1024]{2,1,0:T(8,128)(2,1)S(1)}, u32[]{:S(2)}, u32[]{:S(2)}) async-start(bf16[16,16,1024]{2,1,0:T(8,128)(2,1)} %get-tuple-element.59), calls=%async_computation.1 | async-start | bytes 1048576 | tf_op jit(solution)/shard_map/all_to_all | solution.py:589
  52.9 1.1 %copy-start = (bf16[8,64,640]{2,1,0:T(8,128)(2,1)S(1)}, bf16[8,64,640]{2,1,0:T(8,128)(2,1)}, u32[]{:S(2)}) copy-start(bf16[8,64,640]{2,1,0:T(8,128)(2,1)} %get-tuple-element.42) | copy-start | bytes 1966084
  54.0 1.0 %copy-start.1 = (bf16[8,64,512]{2,1,0:T(8,128)(2,1)S(1)}, bf16[8,64,512]{2,1,0:T(8,128)(2,1)}, u32[]{:S(2)}) copy-start(bf16[8,64,512]{2,1,0:T(8,128)(2,1)} %get-tuple-element.44) | copy-start | bytes 1572868
  55.3 14.7 %collective-permute-start.2 = (bf16[4,64,640]{2,1,0:T(8,128)(2,1)S(1)}, bf16[4,64,640]{2,1,0:T(8,128)(2,1)S(1)}, u32[]{:S(2)}, u32[]{:S(2)}) collective-permute-start(bf16[4,64,640]{2,1,0:T(8,128)(2,1)S(1)} %bitcast.48), channel_id=1, source_target_pairs={{0,2},{1,3},{2,0},{3,1},{4,6},{5,7},{6,4},{7,5},{8,10},{9,11},{10,... | collective-permute-start | bytes 983048 | tf_op jit(solution)/shard_map/ppermute | solution.py:465
  57.3 12.8 %collective-permute-start.3 = (bf16[4,64,512]{2,1,0:T(8,128)(2,1)S(1)}, bf16[4,64,512]{2,1,0:T(8,128)(2,1)S(1)}, u32[]{:S(2)}, u32[]{:S(2)}) collective-permute-start(bf16[4,64,512]{2,1,0:T(8,128)(2,1)S(1)} %bitcast.49), channel_id=1, source_target_pairs={{0,4},{1,5},{2,6},{3,7},{4,0},{5,1},{6,2},{7,3},{8,12},{9,13},{10,... | collective-permute-start | bytes 786440 | tf_op jit(solution)/shard_map/ppermute | solution.py:465
  70.2 6.0 %collective-permute-start.4 = (bf16[2,64,640]{2,1,0:T(8,128)(2,1)S(1)}, bf16[2,64,640]{2,1,0:T(8,128)(2,1)S(1)}, u32[]{:S(2)}, u32[]{:S(2)}) collective-permute-start(bf16[2,64,640]{2,1,0:T(8,128)(2,1)S(1)} %bitcast.50), channel_id=1, source_target_pairs={{0,4},{1,5},{2,6},{3,7},{4,0},{5,1},{6,2},{7,3},{8,12},{9,13},{10,... | collective-permute-start | bytes 491528 | tf_op jit(solution)/shard_map/ppermute | solution.py:465
  71.2 5.0 %collective-permute-start.5 = (bf16[2,64,512]{2,1,0:T(8,128)(2,1)S(1)}, bf16[2,64,512]{2,1,0:T(8,128)(2,1)S(1)}, u32[]{:S(2)}, u32[]{:S(2)}) collective-permute-start(bf16[2,64,512]{2,1,0:T(8,128)(2,1)S(1)} %bitcast.51), channel_id=1, source_target_pairs={{0,2},{1,3},{2,0},{3,1},{4,6},{5,7},{6,4},{7,5},{8,10},{9,11},{10,... | collective-permute-start | bytes 393224 | tf_op jit(solution)/shard_map/ppermute | solution.py:465
  76.3 0.6 copy-start.2
  76.9 9.0 %collective-permute-start.7 = (bf16[1,64,512]{2,1,0:T(8,128)(2,1)S(1)}, bf16[1,64,512]{2,1,0:T(8,128)(2,1)S(1)}, u32[]{:S(2)}, u32[]{:S(2)}) collective-permute-start(bf16[1,64,512]{2,1,0:T(8,128)(2,1)S(1)} %bitcast.53), channel_id=1, source_target_pairs={{0,8},{1,9},{2,10},{3,11},{4,12},{5,13},{6,14},{7,15},{8,0},{9,1},... | collective-permute-start | bytes 196616 | tf_op jit(solution)/shard_map/ppermute | solution.py:465
  79.2 6.9 %collective-permute-start.6 = (bf16[1,64,640]{2,1,0:T(8,128)(2,1)S(1)}, bf16[1,64,640]{2,1,0:T(8,128)(2,1)S(1)}, u32[]{:S(2)}, u32[]{:S(2)}) collective-permute-start(bf16[1,64,640]{2,1,0:T(8,128)(2,1)S(1)} %bitcast.52), channel_id=1, source_target_pairs={{0,8},{1,9},{2,10},{3,11},{4,12},{5,13},{6,14},{7,15},{8,0},{9,1},... | collective-permute-start | bytes 245768 | tf_op jit(solution)/shard_map/ppermute | solution.py:465
  79.8 0.8 copy-start.5
  80.6 5.4 %copy-start.3 = (bf16[1,1,64,640]{3,2,1,0:T(8,128)(2,1)S(1)}, bf16[1,1,64,640]{3,2,1,0:T(8,128)(2,1)}, u32[]{:S(2)}) copy-start(bf16[1,1,64,640]{3,2,1,0:T(8,128)(2,1)} %copy-done.2) | copy-start | bytes 245764

commit v3 on v2

--- a/solution.py
+++ b/solution.py
@@ -14,6 +14,9 @@
 alpha_fair = 0.95
 smooth_sq = 0.01
 MIB = 1 << 20
+KEEP = 50
+PACK = 56
+UNROLL = 2
 
 f32 = jnp.float32
 bf16 = jnp.bfloat16
@@ -53,12 +56,12 @@
         projected[c, : rows.shape[0], :] = out[:, c * LANES : (c + 1) * LANES]
 
 
-def by_member(projected, table, first, count):
-    members = table.shape[0]
+def by_member(projected, table, members, rows_pad, first, count):
     for m in range(members):
+        at = m * rows_pad + first
         for c in range(projected.shape[0]):
             block = projected[c, pl.ds(m, count, stride=members), :]
-            table[m, first : first + count, c * LANES : (c + 1) * LANES] = block.astype(bf16)
+            table[at : at + count, c * LANES : (c + 1) * LANES] = block.astype(bf16)
 
 
 def pack_kernel(rows_ref, latent, area, out, zeros, sem):
@@ -92,6 +95,33 @@
             pltpu.make_async_copy(zeros, out.at[s, b, :, pl.ds(0, width)], sem).wait()
 
 
+def strips(widths, width):
+    places, strip, first = [], 0, 0
+    for w in widths:
+        if first + w > width:
+            strip, first = strip + 1, 0
+        places.append((strip, first))
+        first += w
+    return places, strip + 1
+
+
+class Layout:
+    def __init__(self, members, rows, points, var_pad, width):
+        self.rows_pad = round_up(rows + 2, ROWS)
+        self.out_first = members * self.rows_pad
+        self.point_first = self.out_first + var_pad
+        widths = [var_pad] * 6 + [round_up(self.rows_pad, LANES)]
+        self.places, count = strips(widths, width)
+        self.points = points
+        self.edge_first = self.point_first + count * points
+        self.shape = (self.edge_first + rows, width)
+
+    def point_block(self, ref, i, columns):
+        strip, first = self.places[i]
+        at = self.point_first + strip * self.points
+        return ref.at[pl.ds(at, self.points), pl.ds(first, columns)]
+
+
 def local_kernel(
     latent,
     w_src,
@@ -103,71 +133,58 @@
     targets,
     var_weight,
     area_weight,
-    table,
-    edge_gr,
-    edge_rg,
-    w_out_pad,
-    w_out_t_pad,
-    b_out_pad,
-    truth,
-    weighting,
+    prepared,
     w_src_t,
     projected,
     wide,
     tall,
+    *,
+    layout,
+    rows,
 ):
-    members, rows_pad, width = table.shape
-    rows, points = edge_rg.shape
+    variables, width = w_out_t.shape
+    points = edge_src.shape[1]
+    rows_pad = layout.rows_pad
+    members = layout.out_first // rows_pad
     mesh_rows = latent.shape[0] // members
-    variables = w_out_t.shape[0]
+    var_pad = wide.shape[0]
     project(projected, latent[...], w_src)
-    by_member(projected, table, 0, mesh_rows)
+    by_member(projected, prepared, members, rows_pad, 0, mesh_rows)
 
     row = lax.broadcasted_iota(jnp.int32, (rows_pad, points), 0)
-    matrix = jnp.where((row >= rows) & (row < rows + 2), 1.0, 0.0).astype(f32)
+    matrix = jnp.where((row >= rows) & (row < rows + 2), 0.5, 0.0).astype(f32)
     for k in range(edge_src.shape[0]):
         matrix = matrix + jnp.where(
-            row == edge_src[k : k + 1, :], edge_coef[k : k + 1, :], 0.0
+            row == edge_src[k : k + 1, :], 0.5 * edge_coef[k : k + 1, :], 0.0
         )
-    edge_rg[...] = matrix[:rows].astype(bf16)
-    edge_gr[...] = matrix.T.astype(bf16)
-
-    bias = b_hidden[...]
-    high, low, _ = split_sum(bias)
+    prepared[layout.edge_first :, :points] = matrix[:rows].astype(bf16)
+    layout.point_block(prepared, 6, rows_pad)[...] = matrix.T.astype(bf16)
+
+    high, low, _ = split_sum(b_hidden[...])
     at = lax.broadcasted_iota(jnp.int32, (rows_pad - rows, width), 0)
     bias_rows = jnp.where(
         at == 0, high.astype(f32), jnp.where(at == 1, low.astype(f32), 0.0)
     ).astype(bf16)
     for m in range(members):
-        table[m, rows:, :] = bias_rows
+        prepared[m * rows_pad + rows : (m + 1) * rows_pad, :] = bias_rows
 
     wide[...] = jnp.zeros_like(wide)
     wide[:variables, :] = w_out_t[...].astype(f32)
-    w_out_t_pad[...] = wide[...].astype(bf16)
-    w_out_pad[...] = wide[...].T.astype(bf16)
-    tall[...] = jnp.zeros_like(tall)
-    tall[:variables, :] = targets[...]
-    truth[...] = tall[...].T
-    b_out_pad[...] = jnp.zeros_like(b_out_pad)
-    b_out_pad[:, :variables] = b_out[...]
-    weighting[...] = jnp.zeros_like(weighting)
-    column = jnp.broadcast_to(area_weight[...], (LANES, points)).T
+    prepared[layout.out_first : layout.point_first, :] = wide[...].astype(bf16)
+
+    for i, value in ((0, targets[...] - b_out[...]), (3, var_weight[...] * area_weight[...])):
+        tall[...] = jnp.zeros_like(tall)
+        tall[:variables, :] = value
+        for j, piece in enumerate(split_sum(tall[...].T)):
+            layout.point_block(prepared, i + j, var_pad)[...] = piece
     w_src_t[...] = w_src[...].T
-    weighting[:, :variables] = column[:, :variables] * var_weight[...]
 
 
 def decoder_kernel(
     me_ref,
     arrived,
     w_src_hbm,
-    table_hbm,
-    edge_gr_hbm,
-    w_out_hbm,
-    b_out_hbm,
-    truth_hbm,
-    weighting_hbm,
-    w_out_t_hbm,
-    edge_rg_hbm,
+    prepared_hbm,
     latent_hbm,
     dlocal_hbm,
     slot_grad_hbm,
@@ -176,78 +193,54 @@
     keep_b,
     send_b,
     w_src,
-    table,
-    edge_gr,
-    w_out_pad,
-    b_out_pad,
-    truth,
-    weighting,
-    w_out_t_pad,
-    edge_rg,
+    prepared,
     latent,
     hidden,
     slope,
     preact,
     pred,
     dpred,
+    truth,
+    weighting,
+    w_out_pad,
     dtable,
     dlocal,
     slot_grad,
-    partial,
-    partial_b,
     sem,
     *,
+    layout,
     points_all,
     variables,
 ):
-    members, rows_pad, width = table.shape
     shards, per_pair, _ = arrived.shape
     received = shards * per_pair
-    rows, points = edge_rg.shape
-    own = latent.shape[0]
+    own, width = latent.shape
+    members, points, var_pad = pred.shape
     mesh_rows = own // members
-    var_pad = w_out_pad.shape[1]
+    rows = mesh_rows + received // members
+    rows_pad = layout.rows_pad
     me = me_ref[0]
 
-    sources = (
-        w_src_hbm,
-        table_hbm,
-        edge_gr_hbm,
-        w_out_hbm,
-        b_out_hbm,
-        truth_hbm,
-        weighting_hbm,
-        w_out_t_hbm,
-        edge_rg_hbm,
-        latent_hbm,
-    )
-    targets = (
-        w_src,
-        table,
-        edge_gr,
-        w_out_pad,
-        b_out_pad,
-        truth,
-        weighting,
-        w_out_t_pad,
-        edge_rg,
-        latent,
-    )
     loads = [
         pltpu.make_async_copy(source, target, sem.at[i])
-        for i, (source, target) in enumerate(zip(sources, targets, strict=True))
+        for i, (source, target) in enumerate(
+            ((w_src_hbm, w_src), (prepared_hbm, prepared), (latent_hbm, latent))
+        )
     ]
-    loads[0].start()
+    for load in loads:
+        load.start()
 
     loads[0].wait()
-    for load in loads[1:]:
-        load.start()
     arrived_rows = arrived[:, :, :width].reshape(received, width)
     project(dtable, arrived_rows, w_src)
     loads[1].wait()
-    by_member(dtable, table, mesh_rows, received // members)
-    for load in loads[2:]:
-        load.wait()
+    by_member(dtable, prepared, members, rows_pad, mesh_rows, received // members)
+    w_out_t_pad = prepared[layout.out_first : layout.point_first, :]
+    w_out_pad[...] = w_out_t_pad.T
+    for i, target in ((0, truth), (3, weighting)):
+        target[...] = sum(
+            layout.point_block(prepared, i + j, var_pad)[...].astype(f32) for j in range(3)
+        )
 
     tail = arrived[:, :, width:].astype(f32)
     at_row = lax.broadcasted_iota(jnp.int32, tail.shape, 1)
@@ -261,7 +254,8 @@
 
     def gather(m, slot, c):
         left, right = c * quarter, (c + 1) * quarter
-        preact[slot, :, left:right] = mm(edge_gr[...], table[m, :, left:right])
+        table = prepared[pl.ds(pl.multiple_of(m * rows_pad, ROWS), rows_pad), left:right]
+        preact[slot, :, left:right] = mm(layout.point_block(prepared, 6, rows_pad)[...], table)
 
     for c in range(4):
         gather(0, 0, c)
@@ -275,14 +269,15 @@
                 left, right = c * quarter, (c + 1) * quarter
                 gather(following, 1 - slot, c)
                 for r in range(0, points, ROWS):
-                    x = preact[slot, r : r + ROWS, left:right]
-                    x2 = x * x
-                    t = jnp.tanh(x * (c0 + c1 * x2))
-                    cdf = 0.5 + 0.5 * t
-                    hidden[pl.ds(first + r, ROWS), left:right] = (x * cdf).astype(bf16)
-                    bend = (1.0 - t) * (x * (c0 + (3.0 * c1) * x2)) + 1.0
-                    slope[pl.ds(first + r, ROWS), left:right] = (cdf * bend).astype(bf16)
-            pred[m] = mm(hidden[pl.ds(first, points), :], w_out_pad[...]) + b_out_pad[...]
+                    y = preact[slot, r : r + ROWS, left:right]
+                    y2 = y * y
+                    t = jnp.tanh(y * (2.0 * c0 + (8.0 * c1) * y2))
+                    p = 1.0 + t
+                    gelu = y * p
+                    hidden[pl.ds(first + r, ROWS), left:right] = gelu.astype(bf16)
+                    bend = (gelu * (1.0 - t)) * (2.0 * c0 + (24.0 * c1) * y2)
+                    slope[pl.ds(first + r, ROWS), left:right] = (p + bend).astype(bf16)
+            pred[m] = mm(hidden[pl.ds(first, points), :], w_out_pad[...])
         return 0
 
     lax.fori_loop(0, members // 2, forward, 0)
@@ -322,14 +317,14 @@
                 dpred[m, at, left : left + LANES] = (gradient * scaled).astype(bf16)
             return loss_sum + weight * (fit * (1.0 / members) - (2.0 * spread) * pairs)
 
-        loss_sum = lax.fori_loop(0, points // ROWS, score, loss_sum)
+        loss_sum = lax.fori_loop(0, points // ROWS, score, loss_sum, unroll=UNROLL)
     loss = jnp.sum(loss_sum, keepdims=True) * (inverse_mean / points_all)
 
     for m in range(members):
         first = m * points
-        grad = mm(dpred[m], w_out_t_pad[...])
+        grad = mm(dpred[m], w_out_t_pad)
         grad = (grad * slope[first : first + points, :].astype(f32)).astype(bf16)
-        grad = mm(edge_rg[...], grad)
+        grad = mm(prepared[layout.edge_first :, :points], grad)
         for c in range(width // LANES):
             dtable[c, pl.ds(m, rows, stride=members), :] = grad[:, c * LANES : (c + 1) * LANES]
 
@@ -347,7 +342,7 @@
         store.start()
 
     half_width = width // 2
-    pairs, _, own_rows, columns = partial.shape
+    pairs, own_rows, columns = keep_a.shape
     core = lax.rem(me, 2)
     grad = mm(dpred[...].reshape(members * points, var_pad), hidden[...], TN).T
     row = lax.broadcasted_iota(jnp.int32, grad.shape, 0)
@@ -358,21 +353,18 @@
         place = me * 2 + i
         here = (row == lax.rem(place, own_rows)) & (lane == variables + place // own_rows)
         grad = jnp.where(here, piece.astype(f32), grad)
-    partial[:, :, :, half_width:] = grad.astype(bf16).reshape(
-        pairs, 2, own_rows, columns - half_width
-    )
+    out = grad.astype(bf16).reshape(pairs, 2, own_rows, columns - half_width)
+    keep_a[:, :, half_width:] = jnp.where(core == 0, out[:, 0], out[:, 1])
+    send_a[:, :, half_width:] = jnp.where(core == 0, out[:, 1], out[:, 0])
+    loads[2].wait()
     back = slot_grad[...].reshape(received, width)
     for c, (keep, send) in enumerate(((keep_a, send_a), (keep_b, send_b))):
         left, right = c * half_width, (c + 1) * half_width
         grad = mm(latent[...], dlocal[:, left:right], TN)
         grad = grad + mm(arrived_rows, back[:, left:right], TN)
-        part = partial if c == 0 else partial_b
-        part[:, :, :, :half_width] = grad.astype(bf16).reshape(
-            pairs, 2, own_rows, half_width
-        )
-        for i, (half, target) in enumerate(((1 - core, send), (core, keep))):
-            stores.append(pltpu.make_async_copy(part.at[:, half], target, sem.at[2 + 2 * c + i]))
-            stores[-1].start()
+        grad = grad.astype(bf16).reshape(pairs, 2, own_rows, half_width)
+        keep[:, :, :half_width] = jnp.where(core == 0, grad[:, 0], grad[:, 1])
+        send[:, :, :half_width] = jnp.where(core == 0, grad[:, 1], grad[:, 0])
     for store in stores:
         store.wait()
 
@@ -449,7 +441,9 @@
     used = sum(size_of(x) for x, s in zip(args, in_specs, strict=True) if s is VMEM)
     used += sum(size_of(x) for x, s in zip(outs, specs, strict=True) if s is VMEM)
     used += sum(size_of(x) for x in scratch if getattr(x, "dtype", None) in (f32, bf16))
-    limit = min(limit or used + used // 4 + 6 * MIB, 60 * MIB)
+    limit = limit or used + used // 4 + 6 * MIB
+    if used > limit * 4 // 5:
+        limit = 60 * MIB
     return pl.pallas_call(
         kernel,
         out_shape=out_shape,
@@ -486,7 +480,6 @@
     own_rows = width // shards
     per_pair = slots * members
     rows = mesh_rows + shards * slots
-    rows_pad = round_up(rows + 2, ROWS)
     loss_columns = round_up(2 * shards, own_rows) // own_rows
     var_pad = round_up(variables + loss_columns, LANES)
     half_width = width // 2
@@ -505,25 +498,16 @@
         slot_rows,
         latent,
         area_row,
-        limit=56 * MIB,
+        limit=PACK * MIB,
     )
     arrived = lax.all_to_all(outgoing, "space", split_axis=0, concat_axis=0, tiled=True)
     arrived = arrived.reshape(shards, per_pair, width + LANES)
 
     columns = (half_width + var_pad, half_width)
-    table, edge_gr, edge_rg, w_out_pad, w_out_t_pad, b_out_pad, truth, weighting, w_src_t = call(
-        local_kernel,
-        [
-            shape((members, rows_pad, width), bf16),
-            shape((points, rows_pad), bf16),
-            shape((rows, points), bf16),
-            shape((width, var_pad), bf16),
-            shape((var_pad, width), bf16),
-            shape((1, var_pad), f32),
-            shape((points, var_pad), f32),
-            shape((points, var_pad), f32),
-            shape((width, width), bf16),
-        ],
+    layout = Layout(members, rows, points, var_pad, width)
+    prepared, w_src_t = call(
+        functools.partial(local_kernel, layout=layout, rows=rows),
+        [shape(layout.shape, bf16), shape((width, width), bf16)],
         [VMEM] * 10,
         [
             pltpu.VMEM((width // LANES, mesh_rows * members, LANES), f32),
@@ -537,27 +521,18 @@
         edge_coef.T,
         b_hidden.reshape(1, width),
         w_out.T,
-        b_out.reshape(1, variables),
+        b_out.reshape(variables, 1),
         targets,
-        var_weight.reshape(1, variables),
+        var_weight.reshape(variables, 1),
         area_row,
         limit=56 * MIB,
     )
 
-    operands = (
-        w_src,
-        table,
-        edge_gr,
-        w_out_pad,
-        b_out_pad,
-        truth,
-        weighting,
-        w_out_t_pad,
-        edge_rg,
-        latent_rows,
-    )
+    operands = (w_src, prepared, latent_rows)
     dlocal, slot_grad, *pieces = call(
-        functools.partial(decoder_kernel, points_all=points_all, variables=variables),
+        functools.partial(
+            decoder_kernel, layout=layout, points_all=points_all, variables=variables
+        ),
         [
             shape((mesh_rows * members, width), bf16),
             shape((shards, per_pair, width), bf16),
@@ -571,19 +546,20 @@
             pltpu.VMEM((2, points, width), f32),
             pltpu.VMEM((members, points, var_pad), f32),
             pltpu.VMEM((members, points, var_pad), bf16),
+            pltpu.VMEM((points, var_pad), f32),
+            pltpu.VMEM((points, var_pad), f32),
+            pltpu.VMEM((width, var_pad), bf16),
             pltpu.VMEM((width // LANES, rows * members, LANES), f32),
             pltpu.VMEM((mesh_rows * members, width), bf16),
             pltpu.VMEM((shards, per_pair, width), bf16),
-            pltpu.VMEM((shards // 2, 2, own_rows, columns[0]), bf16),
-            pltpu.VMEM((shards // 2, 2, own_rows, columns[1]), bf16),
-            pltpu.SemaphoreType.DMA((len(operands),)),
+            pltpu.SemaphoreType.DMA((3,)),
         ],
         1 << 34,
         me,
         arrived,
         *operands,
-        out_specs=[HBM] * 6,
-        limit=56 * MIB,
+        out_specs=[HBM] * 2 + [VMEM] * 4,
+        limit=KEEP * MIB,
     )
 
     returned = lax.all_to_all(slot_grad, "space", split_axis=0, concat_axis=0, tiled=True)

time: 87.4 us -> 82.6 us (0.945)
  Pallas kernels: 35.7 us -> 31.9 us
  local copies, waits for them, and re-layouts: 4.37 us -> 2.11 us
  waiting for transfers between devices: 25.2 us -> 26.6 us
    pallas_call x8, Pallas kernels: 35.7 us -> 31.9 us  [call(): pl.pallas_call(kernel, out_shape=out_shape, in_specs=in_specs, out_specs=...]
    unnamed x12 -> x8, local copies, waits for them, and re-layouts: 4.37 us -> 0.64 us
    ppermute x8, waiting for transfers between devices: 15.3 us -> 18.2 us  [swap(): return lax.ppermute(value, 'space', [(i, i ^ bit) for i in range(shards)])]
    all_to_all x1, waiting for transfers between devices: 9.85 us -> 8.37 us  [per_device(): lax.all_to_all(outgoing, 'space', split_axis=0, concat_axis=0, tiled=True)]
    reshape x0 -> x2, local copies, waits for them, and re-layouts: none -> 1.47 us  [the longest x1 0.73 us: per_device(): var_weight.reshape(variables, 1)]
  transfers between devices with their start and end apart: 10 -> 10, of which waited for: 4 -> 5; matrix products, arithmetic and copies ran while one was open for 0% -> 2% of each run, Pallas kernels for 13% -> 14%
where the time goes in v3:
time: 82.6 us; the launch traced here: 82.1 us
  Pallas kernels  31.9 us (39%)
  waiting for transfers between devices  26.6 us (32%)
  starting transfers between devices  20.9 us (25%)
  local copies, waits for them, and re-layouts  2.11 us (3%)
    pallas_call x8, Pallas kernels, call(): pl.pallas_call(kernel, out_shape=out_shape, in_specs=in_specs, out_specs=...  31.9 us
    ppermute x8, waiting for transfers between devices, swap(): return lax.ppermute(value, 'space', [(i, i ^ bit) for i in range(shards)])  18.2 us
    ppermute x8, starting transfers between devices, swap(): return lax.ppermute(value, 'space', [(i, i ^ bit) for i in range(shards)])  9.02 us
    all_to_all x1, waiting for transfers between devices, per_device(): lax.all_to_all(outgoing, 'space', split_axis=0, concat_axis=0, tiled=True)  8.37 us
    all_to_all x1, starting transfers between devices, per_device(): lax.all_to_all(outgoing, 'space', split_axis=0, concat_axis=0, tiled=True)  7.35 us
    all_to_all x1, starting transfers between devices, per_device(): lax.all_to_all(slot_grad, 'space', split_axis=0, concat_axis=0, tiled=True)  4.49 us
  transfers between devices with their start and end apart: 10, of which 5 were waited for; matrix products, arithmetic and copies ran while one was open for 2% of the time, Pallas kernels for 14%

profile of v3, /device:TPU:0, one launch (start us, length us, event | category | flops | bytes accessed | tf_op | source)
XLA Modules:
  0.0 82.1 jit_solution(783820212271306090)
XLA Ops:
  0.7 2.8 %shard_map.138 = bf16[16,2,8,1152]{3,2,1,0:T(8,128)(2,1)} custom-call(s32[1,2,16]{2,1,0:T(2,128)} %bitcast.59, bf16[64,8,1024]{2,1,0:T(8,128)(2,1)} %latent.1, f32[1,256]{1,0:T(1,128)} %bitcast.57), custom_call_target="tpu_custom_call" | custom-call | flops 16777216 | bytes 607232 | tf_op jit(solution)/shard_map/pallas_call | solution.py:447
  3.5 7.3 %all-to-all-start = ((bf16[16,2,8,1152]{3,2,1,0:T(8,128)(2,1)}), bf16[16,2,8,1152]{3,2,1,0:T(8,128)(2,1)S(1)}, u32[]{:S(2)}, u32[]{:S(2)}) async-start(bf16[16,2,8,1152]{3,2,1,0:T(8,128)(2,1)} %shard_map.138), calls=%async_computation | async-start | bytes 1179648 | tf_op jit(solution)/shard_map/all_to_all | solution.py:503
  10.9 0.7 copy.15.b_out
  11.6 0.7 copy.16.var_weight
  12.3 5.7 %shard_map.139 = (bf16[1376,1024]{1,0:T(8,128)(2,1)}, bf16[1024,1024]{1,0:T(8,128)(2,1)}) custom-call(bf16[512,1024]{1,0:T(8,128)(2,1)} %bitcast.55, bf16[1024,1024]{1,0:T(8,128)(2,1)} %w_src_hbm.1, s32[3,256]{1,0:T(4,128)} %bitcast.64, f32[3,256]{1,0:T(4,128)} %bitcast.65, f32[1,1024]{1,0:T(1,128)} %bitcast.66, bf16[100,1024]{1,0:T(8,128)(2,1)} %bitcast.63, ...), custom_call_target="tpu_custom_call" | custom-call | flops 2147483648 | bytes 11132704 | tf_op jit(solution)/shard_map/pallas_call | solution.py:447
  18.0 8.4 %all-to-all-done = bf16[16,2,8,1152]{3,2,1,0:T(8,128)(2,1)S(1)} async-done(((bf16[16,2,8,1152]{3,2,1,0:T(8,128)(2,1)}), bf16[16,2,8,1152]{3,2,1,0:T(8,128)(2,1)S(1)}, u32[]{:S(2)}, u32[]{:S(2)}) %all-to-all-start) | async-done | bytes 589856 | tf_op jit(solution)/shard_map/all_to_all | solution.py:503
  26.4 16.8 %shard_map.140 = (bf16[512,1024]{1,0:T(8,128)(2,1)}, bf16[16,16,1024]{2,1,0:T(8,128)(2,1)}, bf16[8,64,640]{2,1,0:T(8,128)(2,1)S(1)}, bf16[8,64,640]{2,1,0:T(8,12...) custom-call(s32[1]{0:T(128)} %bitcast.me_ref, bf16[16,16,1152]{2,1,0:T(8,128)(2,1)S(1)} %bitcast.35, ...), custom_call_target="tpu_custom_call" | custom-call | flops 17179869184 | bytes 26214400 | tf_op jit(solution)/shard_map/pallas_call | solution.py:447
  43.2 0.1 collective-permute-start
  43.3 0.5 collective-permute-start.1
  43.8 4.5 %all-to-all-start.1 = ((bf16[16,16,1024]{2,1,0:T(8,128)(2,1)}), bf16[16,16,1024]{2,1,0:T(8,128)(2,1)}, u32[]{:S(2)}, u32[]{:S(2)}) async-start(bf16[16,16,1024]{2,1,0:T(8,128)(2,1)} %get-tuple-element.45), calls=%async_computation.1 | async-start | bytes 1048576 | tf_op jit(solution)/shard_map/all_to_all | solution.py:565
  48.3 0.0 collective-permute-done.1
  48.3 0.0 collective-permute-done
  48.3 0.3 shard_map.141
  48.6 1.9 %collective-permute-start.2 = (bf16[4,64,640]{2,1,0:T(8,128)(2,1)S(1)}, bf16[4,64,640]{2,1,0:T(8,128)(2,1)S(1)}, u32[]{:S(2)}, u32[]{:S(2)}) collective-permute-start(bf16[4,64,640]{2,1,0:T(8,128)(2,1)S(1)} %bitcast.49), channel_id=1, source_target_pairs={{0,2},{1,3},{2,0},{3,1},{4,6},{5,7},{6,4},{7,5},{8,10},{9,11},{10,... | collective-permute-start | bytes 983048 | tf_op jit(solution)/shard_map/ppermute | solution.py:459
  50.5 1.5 %collective-permute-start.3 = (bf16[4,64,512]{2,1,0:T(8,128)(2,1)S(1)}, bf16[4,64,512]{2,1,0:T(8,128)(2,1)S(1)}, u32[]{:S(2)}, u32[]{:S(2)}) collective-permute-start(bf16[4,64,512]{2,1,0:T(8,128)(2,1)S(1)} %bitcast.50), channel_id=1, source_target_pairs={{0,4},{1,5},{2,6},{3,7},{4,0},{5,1},{6,2},{7,3},{8,12},{9,13},{10,... | collective-permute-start | bytes 786440 | tf_op jit(solution)/shard_map/ppermute | solution.py:459
  52.0 13.4 %collective-permute-done.3 = bf16[4,64,512]{2,1,0:T(8,128)(2,1)S(1)} collective-permute-done((bf16[4,64,512]{2,1,0:T(8,128)(2,1)S(1)}, bf16[4,64,512]{2,1,0:T(8,128)(2,1)S(1)}, u32[]{:S(2)}, u32[]{:S(2)}) %collective-permute-start.3) | collective-permute-done | bytes 262176 | tf_op jit(solution)/shard_map/ppermute | solution.py:459
  65.4 0.0 collective-permute-done.2
  65.4 0.1 shard_map.142
  65.5 0.5 collective-permute-start.4
  66.0 1.6 %collective-permute-start.5 = (bf16[2,64,512]{2,1,0:T(8,128)(2,1)S(1)}, bf16[2,64,512]{2,1,0:T(8,128)(2,1)S(1)}, u32[]{:S(2)}, u32[]{:S(2)}) collective-permute-start(bf16[2,64,512]{2,1,0:T(8,128)(2,1)S(1)} %bitcast.52), channel_id=1, source_target_pairs={{0,2},{1,3},{2,0},{3,1},{4,6},{5,7},{6,4},{7,5},{8,10},{9,11},{10,... | collective-permute-start | bytes 393224 | tf_op jit(solution)/shard_map/ppermute | solution.py:459
  67.7 3.4 %collective-permute-done.5 = bf16[2,64,512]{2,1,0:T(8,128)(2,1)S(1)} collective-permute-done((bf16[2,64,512]{2,1,0:T(8,128)(2,1)S(1)}, bf16[2,64,512]{2,1,0:T(8,128)(2,1)S(1)}, u32[]{:S(2)}, u32[]{:S(2)}) %collective-permute-start.5) | collective-permute-done | bytes 131104 | tf_op jit(solution)/shard_map/ppermute | solution.py:459
  71.1 0.2 collective-permute-done.4
  71.3 0.1 shard_map.143
  71.4 0.0 copy-start
  71.4 0.6 copy-done
  72.0 2.5 %collective-permute-start.7 = (bf16[1,64,512]{2,1,0:T(8,128)(2,1)S(1)}, bf16[1,64,512]{2,1,0:T(8,128)(2,1)S(1)}, u32[]{:S(2)}, u32[]{:S(2)}) collective-permute-start(bf16[1,64,512]{2,1,0:T(8,128)(2,1)S(1)} %bitcast.54), channel_id=1, source_target_pairs={{0,8},{1,9},{2,10},{3,11},{4,12},{5,13},{6,14},{7,15},{8,0},{9,1},... | collective-permute-start | bytes 196616 | tf_op jit(solution)/shard_map/ppermute | solution.py:459
  74.5 0.4 collective-permute-start.6
  75.0 0.0 all-to-all-done.1.returned
  75.0 5.3 %shard_map.145 = f32[512,1024]{1,0:T(8,128)} custom-call(s32[1,2,16]{2,1,0:T(2,128)} %bitcast.60, bf16[16,16,1024]{2,1,0:T(8,128)(2,1)} %all-to-all-done.1.returned, bf16[512,1024]{1,0:T(8,128)(2,1)} %get-tuple-element.46.dlocal_hbm, bf16[1024,1024]{1,0:T(8,128)(2,1)} %get-tuple-element.47.w_src_t_hbm, bf16[1,64,640]{2,1,0:T(8,128)(2,1)} %bitcast.46), custom_call_target="tpu_custom_call" | custom-call | flops 4294967296 | bytes 6291456 | tf_op jit(solution)/shard_map/pallas_call | solution.py:447
  80.3 0.0 collective-permute-done.7.got_b
  80.3 1.1 %collective-permute-done.6.got_a = bf16[1,64,640]{2,1,0:T(8,128)(2,1)S(1)} collective-permute-done((bf16[1,64,640]{2,1,0:T(8,128)(2,1)S(1)}, bf16[1,64,640]{2,1,0:T(8,128)(2,1)S(1)}, u32[]{:S(2)}, u32[]{:S(2)}) %collective-permute-start.6) | collective-permute-done | bytes 81952 | tf_op jit(solution)/shard_map/ppermute | solution.py:459
  81.4 0.8 shard_map.144
  (6 shorter events, 0.0 us)
Async XLA Ops:
  0.6 10.2 %copy-start.2 = (f32[100]{0:T(128)S(1)}, f32[100]{0:T(128)}, u32[]{:S(2)}) copy-start(f32[100]{0:T(128)} %param.15) | copy-start | bytes 1204
  0.6 11.0 %copy-start.3 = (f32[100]{0:T(128)S(1)}, f32[100]{0:T(128)}, u32[]{:S(2)}) copy-start(f32[100]{0:T(128)} %param.17) | copy-start | bytes 1204
  3.5 22.9 %all-to-all-start = ((bf16[16,2,8,1152]{3,2,1,0:T(8,128)(2,1)}), bf16[16,2,8,1152]{3,2,1,0:T(8,128)(2,1)S(1)}, u32[]{:S(2)}, u32[]{:S(2)}) async-start(bf16[16,2,8,1152]{3,2,1,0:T(8,128)(2,1)} %shard_map.138), calls=%async_computation | async-start | bytes 1179648 | tf_op jit(solution)/shard_map/all_to_all | solution.py:503
  43.2 5.1 %collective-permute-start = (bf16[8,64,640]{2,1,0:T(8,128)(2,1)S(1)}, bf16[8,64,640]{2,1,0:T(8,128)(2,1)S(1)}, u32[]{:S(2)}, u32[]{:S(2)}) collective-permute-start(bf16[8,64,640]{2,1,0:T(8,128)(2,1)S(1)} %get-tuple-element.29), channel_id=1, source_target_pairs={{0,1},{1,0},{2,3},{3,2},{4,5},{5,4},{6,7},{7,6},{8,9},{9,8},{10,11... | collective-permute-start | bytes 1966088 | tf_op jit(solution)/shard_map/ppermute | solution.py:459
  43.3 5.0 %collective-permute-start.1 = (bf16[8,64,512]{2,1,0:T(8,128)(2,1)S(1)}, bf16[8,64,512]{2,1,0:T(8,128)(2,1)S(1)}, u32[]{:S(2)}, u32[]{:S(2)}) collective-permute-start(bf16[8,64,512]{2,1,0:T(8,128)(2,1)S(1)} %get-tuple-element.31), channel_id=1, source_target_pairs={{0,1},{1,0},{2,3},{3,2},{4,5},{5,4},{6,7},{7,6},{8,9},{9,8},{10,11... | collective-permute-start | bytes 1572872 | tf_op jit(solution)/shard_map/ppermute | solution.py:459
  43.8 31.2 %all-to-all-start.1 = ((bf16[16,16,1024]{2,1,0:T(8,128)(2,1)}), bf16[16,16,1024]{2,1,0:T(8,128)(2,1)}, u32[]{:S(2)}, u32[]{:S(2)}) async-start(bf16[16,16,1024]{2,1,0:T(8,128)(2,1)} %get-tuple-element.45), calls=%async_computation.1 | async-start | bytes 1048576 | tf_op jit(solution)/shard_map/all_to_all | solution.py:565
  48.6 16.8 %collective-permute-start.2 = (bf16[4,64,640]{2,1,0:T(8,128)(2,1)S(1)}, bf16[4,64,640]{2,1,0:T(8,128)(2,1)S(1)}, u32[]{:S(2)}, u32[]{:S(2)}) collective-permute-start(bf16[4,64,640]{2,1,0:T(8,128)(2,1)S(1)} %bitcast.49), channel_id=1, source_target_pairs={{0,2},{1,3},{2,0},{3,1},{4,6},{5,7},{6,4},{7,5},{8,10},{9,11},{10,... | collective-permute-start | bytes 983048 | tf_op jit(solution)/shard_map/ppermute | solution.py:459
  50.5 14.9 %collective-permute-start.3 = (bf16[4,64,512]{2,1,0:T(8,128)(2,1)S(1)}, bf16[4,64,512]{2,1,0:T(8,128)(2,1)S(1)}, u32[]{:S(2)}, u32[]{:S(2)}) collective-permute-start(bf16[4,64,512]{2,1,0:T(8,128)(2,1)S(1)} %bitcast.50), channel_id=1, source_target_pairs={{0,4},{1,5},{2,6},{3,7},{4,0},{5,1},{6,2},{7,3},{8,12},{9,13},{10,... | collective-permute-start | bytes 786440 | tf_op jit(solution)/shard_map/ppermute | solution.py:459
  65.5 5.8 %collective-permute-start.4 = (bf16[2,64,640]{2,1,0:T(8,128)(2,1)S(1)}, bf16[2,64,640]{2,1,0:T(8,128)(2,1)S(1)}, u32[]{:S(2)}, u32[]{:S(2)}) collective-permute-start(bf16[2,64,640]{2,1,0:T(8,128)(2,1)S(1)} %bitcast.51), channel_id=1, source_target_pairs={{0,4},{1,5},{2,6},{3,7},{4,0},{5,1},{6,2},{7,3},{8,12},{9,13},{10,... | collective-permute-start | bytes 491528 | tf_op jit(solution)/shard_map/ppermute | solution.py:459
  66.0 5.0 %collective-permute-start.5 = (bf16[2,64,512]{2,1,0:T(8,128)(2,1)S(1)}, bf16[2,64,512]{2,1,0:T(8,128)(2,1)S(1)}, u32[]{:S(2)}, u32[]{:S(2)}) collective-permute-start(bf16[2,64,512]{2,1,0:T(8,128)(2,1)S(1)} %bitcast.52), channel_id=1, source_target_pairs={{0,2},{1,3},{2,0},{3,1},{4,6},{5,7},{6,4},{7,5},{8,10},{9,11},{10,... | collective-permute-start | bytes 393224 | tf_op jit(solution)/shard_map/ppermute | solution.py:459
  71.4 0.6 copy-start
  72.0 8.2 %collective-permute-start.7 = (bf16[1,64,512]{2,1,0:T(8,128)(2,1)S(1)}, bf16[1,64,512]{2,1,0:T(8,128)(2,1)S(1)}, u32[]{:S(2)}, u32[]{:S(2)}) collective-permute-start(bf16[1,64,512]{2,1,0:T(8,128)(2,1)S(1)} %bitcast.54), channel_id=1, source_target_pairs={{0,8},{1,9},{2,10},{3,11},{4,12},{5,13},{6,14},{7,15},{8,0},{9,1},... | collective-permute-start | bytes 196616 | tf_op jit(solution)/shard_map/ppermute | solution.py:459
  74.5 6.9 %collective-permute-start.6 = (bf16[1,64,640]{2,1,0:T(8,128)(2,1)S(1)}, bf16[1,64,640]{2,1,0:T(8,128)(2,1)S(1)}, u32[]{:S(2)}, u32[]{:S(2)}) collective-permute-start(bf16[1,64,640]{2,1,0:T(8,128)(2,1)S(1)} %bitcast.53), channel_id=1, source_target_pairs={{0,8},{1,9},{2,10},{3,11},{4,12},{5,13},{6,14},{7,15},{8,0},{9,1},... | collective-permute-start | bytes 245768 | tf_op jit(solution)/shard_map/ppermute | solution.py:459
  75.0 6.4 %copy-start.1 = (bf16[1,1,64,640]{3,2,1,0:T(8,128)(2,1)S(1)}, bf16[1,1,64,640]{3,2,1,0:T(8,128)(2,1)}, u32[]{:S(2)}) copy-start(bf16[1,1,64,640]{3,2,1,0:T(8,128)(2,1)} %copy-done) | copy-start | bytes 245764

commit v4 on v3

--- a/solution.py
+++ b/solution.py
@@ -17,6 +17,7 @@
 KEEP = 50
 PACK = 56
 UNROLL = 2
+LAST = 54
 
 f32 = jnp.float32
 bf16 = jnp.bfloat16
@@ -198,6 +199,7 @@
     hidden,
     slope,
     preact,
+    dpreact,
     pred,
     dpred,
     truth,
@@ -254,33 +256,29 @@
 
     def gather(m, slot, c):
         left, right = c * quarter, (c + 1) * quarter
-        table = prepared[pl.ds(pl.multiple_of(m * rows_pad, ROWS), rows_pad), left:right]
+        table = prepared[m * rows_pad : (m + 1) * rows_pad, left:right]
         preact[slot, :, left:right] = mm(layout.point_block(prepared, 6, rows_pad)[...], table)
 
     for c in range(4):
         gather(0, 0, c)
 
-    def forward(pair, _):
-        for slot in range(2):
-            m = pair * 2 + slot
-            first = pl.multiple_of(m * points, points)
-            following = jnp.minimum(m + 1, members - 1)
-            for c in range(4):
-                left, right = c * quarter, (c + 1) * quarter
-                gather(following, 1 - slot, c)
-                for r in range(0, points, ROWS):
-                    y = preact[slot, r : r + ROWS, left:right]
-                    y2 = y * y
-                    t = jnp.tanh(y * (2.0 * c0 + (8.0 * c1) * y2))
-                    p = 1.0 + t
-                    gelu = y * p
-                    hidden[pl.ds(first + r, ROWS), left:right] = gelu.astype(bf16)
-                    bend = (gelu * (1.0 - t)) * (2.0 * c0 + (24.0 * c1) * y2)
-                    slope[pl.ds(first + r, ROWS), left:right] = (p + bend).astype(bf16)
-            pred[m] = mm(hidden[pl.ds(first, points), :], w_out_pad[...])
-        return 0
-
-    lax.fori_loop(0, members // 2, forward, 0)
+    for m in range(members):
+        slot = m % 2
+        first = m * points
+        for c in range(4):
+            left, right = c * quarter, (c + 1) * quarter
+            if m + 1 < members:
+                gather(m + 1, 1 - slot, c)
+            for r in range(0, points, ROWS):
+                y = preact[slot, r : r + ROWS, left:right]
+                y2 = y * y
+                t = jnp.tanh(y * (2.0 * c0 + (8.0 * c1) * y2))
+                p = 1.0 + t
+                gelu = y * p
+                hidden[first + r : first + r + ROWS, left:right] = gelu.astype(bf16)
+                bend = (gelu * (1.0 - t)) * (2.0 * c0 + (24.0 * c1) * y2)
+                slope[first + r : first + r + ROWS, left:right] = (p + bend).astype(bf16)
+        pred[m] = mm(hidden[first : first + points, :], w_out_pad[...])
 
     spread = spread_coef(members)
     inverse_mean = 1.0 / mean_area
@@ -320,13 +318,22 @@
         loss_sum = lax.fori_loop(0, points // ROWS, score, loss_sum, unroll=UNROLL)
     loss = jnp.sum(loss_sum, keepdims=True) * (inverse_mean / points_all)
 
-    for m in range(members):
-        first = m * points
-        grad = mm(dpred[m], w_out_t_pad)
-        grad = (grad * slope[first : first + points, :].astype(f32)).astype(bf16)
-        grad = mm(prepared[layout.edge_first :, :points], grad)
-        for c in range(width // LANES):
-            dtable[c, pl.ds(m, rows, stride=members), :] = grad[:, c * LANES : (c + 1) * LANES]
+    edge_back = prepared[layout.edge_first :, :points]
+    preact[0] = mm(dpred[0], w_out_t_pad)
+    for m in range(members + 1):
+        if m + 1 < members:
+            preact[(m + 1) % 2] = mm(dpred[m + 1], w_out_t_pad)
+        if m < members:
+            for r in range(0, points, ROWS):
+                at = m * points + r
+                grad = preact[m % 2, r : r + ROWS, :] * slope[at : at + ROWS, :].astype(f32)
+                dpreact[m % 2, r : r + ROWS, :] = grad.astype(bf16)
+        if m >= 1:
+            grad = mm(edge_back, dpreact[(m - 1) % 2])
+            for c in range(width // LANES):
+                dtable[c, pl.ds(m - 1, rows, stride=members), :] = grad[
+                    :, c * LANES : (c + 1) * LANES
+                ]
 
     for c in range(width // LANES):
         left, right = c * LANES, (c + 1) * LANES
@@ -342,7 +349,7 @@
         store.start()
 
     half_width = width // 2
-    pairs, own_rows, columns = keep_a.shape
+    pairs, own_rows, _ = keep_a.shape
     core = lax.rem(me, 2)
     grad = mm(dpred[...].reshape(members * points, var_pad), hidden[...], TN).T
     row = lax.broadcasted_iota(jnp.int32, grad.shape, 0)
@@ -353,13 +360,13 @@
         place = me * 2 + i
         here = (row == lax.rem(place, own_rows)) & (lane == variables + place // own_rows)
         grad = jnp.where(here, piece.astype(f32), grad)
-    out = grad.astype(bf16).reshape(pairs, 2, own_rows, columns - half_width)
-    keep_a[:, :, half_width:] = jnp.where(core == 0, out[:, 0], out[:, 1])
-    send_a[:, :, half_width:] = jnp.where(core == 0, out[:, 1], out[:, 0])
+    grad = grad.astype(bf16).reshape(pairs, 2, own_rows, var_pad)
+    keep_a[:, :, half_width:] = jnp.where(core == 0, grad[:, 0], grad[:, 1])
+    send_a[:, :, half_width:] = jnp.where(core == 0, grad[:, 1], grad[:, 0])
     loads[2].wait()
     back = slot_grad[...].reshape(received, width)
-    for c, (keep, send) in enumerate(((keep_a, send_a), (keep_b, send_b))):
-        left, right = c * half_width, (c + 1) * half_width
+    for left, keep, send in ((0, keep_a, send_a), (half_width, keep_b, send_b)):
+        right = left + half_width
         grad = mm(latent[...], dlocal[:, left:right], TN)
         grad = grad + mm(arrived_rows, back[:, left:right], TN)
         grad = grad.astype(bf16).reshape(pairs, 2, own_rows, half_width)
@@ -369,24 +376,25 @@
         store.wait()
 
 
-def halve_kernel(me_ref, keep_a, got_a, keep_b, got_b, *rest, bits):
-    outs = rest[-4:]
-    for i, (keep, got, bit) in enumerate(
-        ((keep_a, got_a, bits[0]), (keep_b, got_b, bits[1]))
-    ):
+def halve_kernel(me_ref, *refs, parts):
+    outs = refs[2 * len(parts) :]
+    for i, (bit, (first, last), place, (left, right)) in enumerate(parts):
+        keep, got = refs[2 * i], refs[2 * i + 1]
         mine = lax.rem(me_ref[0] // bit, 2)
-        for out, half in ((outs[2 * i + 1], 1 - mine), (outs[2 * i], mine)):
-            total = keep[:, half].astype(f32) + got[:, half].astype(f32)
-            out[...] = total.astype(bf16)
-
-
-def final_kernel(keep_a, got_a, keep_b, got_b, grad_w_src, grad_w_out, loss, *, scale):
+        for out, half in ((outs[2 * place + 1], 1 - mine), (outs[2 * place], mine)):
+            total = keep[:, half, :, :, first:last].astype(f32)
+            total = total + got[:, half, :, :, first:last].astype(f32)
+            out[:, :, :, left:right] = total.astype(bf16)
+
+
+def final_kernel(keep, got, grad_w_src, grad_w_out, loss, *, scale):
     variables = grad_w_out.shape[1]
     half_width = grad_w_src.shape[1] // 2
-    total = keep_a[0].astype(f32) + got_a[0].astype(f32)
+    second = keep.shape[2] - half_width
+    total = keep[0].astype(f32) + got[0].astype(f32)
     grad_w_src[:, :half_width] = total[:, :half_width] * scale
-    grad_w_src[:, half_width:] = (keep_b[0].astype(f32) + got_b[0].astype(f32)) * scale
-    out = total[:, half_width:]
+    grad_w_src[:, half_width:] = total[:, second:] * scale
+    out = total[:, half_width:second]
     grad_w_out[...] = out[:, :variables] * scale
     lane = lax.broadcasted_iota(jnp.int32, out.shape, 1)
     loss[...] = jnp.sum(jnp.where(lane >= variables, out, 0.0), keepdims=True)
@@ -503,7 +511,8 @@
     arrived = lax.all_to_all(outgoing, "space", split_axis=0, concat_axis=0, tiled=True)
     arrived = arrived.reshape(shards, per_pair, width + LANES)
 
-    columns = (half_width + var_pad, half_width)
+    columns = width + var_pad
+    cut = half_width + var_pad
     layout = Layout(members, rows, points, var_pad, width)
     prepared, w_src_t = call(
         functools.partial(local_kernel, layout=layout, rows=rows),
@@ -536,7 +545,7 @@
         [
             shape((mesh_rows * members, width), bf16),
             shape((shards, per_pair, width), bf16),
-            *[shape((shards // 2, own_rows, n), bf16) for n in columns for _ in range(2)],
+            *[shape((shards // 2, own_rows, n), bf16) for n in (cut, half_width) for _ in range(2)],
         ],
         [SMEM, VMEM] + [HBM] * len(operands),
         [
@@ -544,6 +553,7 @@
             pltpu.VMEM((members * points, width), bf16),
             pltpu.VMEM((members * points, width), bf16),
             pltpu.VMEM((2, points, width), f32),
+            pltpu.VMEM((2, points, width), bf16),
             pltpu.VMEM((members, points, var_pad), f32),
             pltpu.VMEM((members, points, var_pad), bf16),
             pltpu.VMEM((points, var_pad), f32),
@@ -568,28 +578,45 @@
     order_a = levels[::-1]
     order_b = order_a[1:2] + order_a[:1] + order_a[2:]
     left = [list(levels), list(levels)]
+    held = [(pieces[i], swap(pieces[i + 1], 1, shards)) for i in (0, 2)]
     count = shards // 2
-    got = [swap(pieces[1], 1, shards), swap(pieces[3], 1, shards)]
     for step, bits in enumerate(zip(order_a, order_b, strict=True)):
-        views = []
+        views, parts = [], []
         for i, bit in enumerate(bits):
             place = left[i].index(bit)
             left[i].remove(bit)
-            split = (1 << place, 2, count >> (place + 1), own_rows, columns[i])
-            views += [pieces[2 * i].reshape(split), got[i].reshape(split)]
+            if step > 2 and i == 1:
+                break
+            pair = held[i]
+            split = (1 << place, 2, count >> (place + 1), own_rows)
+            views += [x.reshape(*split, x.shape[2]) for x in pair]
+            mine = (0, cut) if i == 0 else (cut, columns)
+            alone = (0, mine[1] - mine[0])
+            if step < 2:
+                parts.append((bit, alone, i, alone))
+            elif step == 2:
+                parts.append((bit, alone, 0, mine))
+            else:
+                parts.append((bit, (0, columns), 0, (0, columns)))
+        widths = (cut, columns - cut) if step < 2 else (columns,)
         count //= 2
-        halves = [(x.shape[0], *x.shape[2:]) for x in views[::2] for _ in range(2)]
+        outs = []
+        for i, w in enumerate(widths):
+            hi, _, lo = views[2 * i].shape[:3]
+            outs += [shape((hi, lo, own_rows, w), bf16)] * 2
         pieces = call(
-            functools.partial(halve_kernel, bits=bits),
-            [shape(x, bf16) for x in halves],
+            functools.partial(halve_kernel, parts=tuple(parts)),
+            outs,
             [SMEM] + [VMEM] * len(views),
             [],
             1 << 24,
             me,
             *views,
         )
-        pieces = [x.reshape(count, *x.shape[2:]) for x in pieces]
-        got = [swap(pieces[2 * i + 1], bit, shards) for i, bit in enumerate(bits)]
+        pieces = [x.reshape(count, own_rows, x.shape[3]) for x in pieces]
+        held = [
+            (pieces[2 * i], swap(pieces[2 * i + 1], bits[i], shards)) for i in range(len(widths))
+        ]
 
     grad_latent = call(
         latent_grad_kernel,
@@ -607,9 +634,9 @@
         returned,
         dlocal,
         w_src_t,
-        pieces[0],
+        held[0][0],
         out_specs=[HBM],
-        limit=56 * MIB,
+        limit=LAST * MIB,
     )
     grad_w_src, grad_w_out, loss = call(
         functools.partial(final_kernel, scale=WSCALE / points_all),
@@ -618,13 +645,10 @@
             shape((own_rows, variables), f32),
             shape((1, 1), f32),
         ],
-        [VMEM] * 4,
+        [VMEM] * 2,
         [],
         1 << 24,
-        pieces[0],
-        got[0],
-        pieces[2],
-        got[1],
+        *held[0],
     )
     return (
         loss.reshape(1),

time: 82.6 us -> 80.5 us (0.975)
  Pallas kernels: 31.9 us -> 30.5 us
    pallas_call x8, Pallas kernels: 31.9 us -> 30.5 us  [call(): pl.pallas_call(kernel, out_shape=out_shape, in_specs=in_specs, out_specs=...]
    ppermute x8 -> x7, starting transfers between devices: 9.02 us -> 8.59 us  [swap(): return lax.ppermute(value, 'space', [(i, i ^ bit) for i in range(shards)])]
    ppermute x8 -> x7, waiting for transfers between devices: 18.2 us -> 17.9 us  [swap(): return lax.ppermute(value, 'space', [(i, i ^ bit) for i in range(shards)])]
  transfers between devices with their start and end apart: 10 -> 9, of which waited for: 5 -> 5; matrix products, arithmetic and copies ran while one was open for 2% -> 2% of each run, Pallas kernels for 14% -> 14%
where the time goes in v4:
time: 80.5 us; the launch traced here: 80 us
  Pallas kernels  30.5 us (38%)
  waiting for transfers between devices  26.2 us (33%)
  starting transfers between devices  20.4 us (25%)
  local copies, waits for them, and re-layouts  2.12 us (3%)
    pallas_call x8, Pallas kernels, call(): pl.pallas_call(kernel, out_shape=out_shape, in_specs=in_specs, out_specs=...  30.5 us
    ppermute x7, waiting for transfers between devices, swap(): return lax.ppermute(value, 'space', [(i, i ^ bit) for i in range(shards)])  17.9 us
    ppermute x7, starting transfers between devices, swap(): return lax.ppermute(value, 'space', [(i, i ^ bit) for i in range(shards)])  8.59 us
    all_to_all x1, waiting for transfers between devices, per_device(): lax.all_to_all(outgoing, 'space', split_axis=0, concat_axis=0, tiled=True)  8.38 us
    all_to_all x1, starting transfers between devices, per_device(): lax.all_to_all(outgoing, 'space', split_axis=0, concat_axis=0, tiled=True)  7.35 us
    all_to_all x1, starting transfers between devices, per_device(): lax.all_to_all(slot_grad, 'space', split_axis=0, concat_axis=0, tiled=True)  4.47 us
  transfers between devices with their start and end apart: 9, of which 5 were waited for; matrix products, arithmetic and copies ran while one was open for 2% of the time, Pallas kernels for 14%

profile of v4, /device:TPU:0, one launch (start us, length us, event | category | flops | bytes accessed | tf_op | source)
XLA Modules:
  0.0 80.0 jit_solution(14589086730313505266)
XLA Ops:
  0.6 0.0 copy-start.2
  0.7 2.8 %shard_map.138 = bf16[16,2,8,1152]{3,2,1,0:T(8,128)(2,1)} custom-call(s32[1,2,16]{2,1,0:T(2,128)} %bitcast.55, bf16[64,8,1024]{2,1,0:T(8,128)(2,1)} %latent.1, f32[1,256]{1,0:T(1,128)} %bitcast.53), custom_call_target="tpu_custom_call" | custom-call | flops 16777216 | bytes 607232 | tf_op jit(solution)/shard_map/pallas_call | solution.py:455
  3.5 7.4 %all-to-all-start = ((bf16[16,2,8,1152]{3,2,1,0:T(8,128)(2,1)}), bf16[16,2,8,1152]{3,2,1,0:T(8,128)(2,1)S(1)}, u32[]{:S(2)}, u32[]{:S(2)}) async-start(bf16[16,2,8,1152]{3,2,1,0:T(8,128)(2,1)} %shard_map.138), calls=%async_computation | async-start | bytes 1179648 | tf_op jit(solution)/shard_map/all_to_all | solution.py:511
  10.8 0.0 copy-done.2
  10.8 0.7 copy.15.b_out
  11.6 0.7 copy.16.var_weight
  12.3 5.7 %shard_map.139 = (bf16[1376,1024]{1,0:T(8,128)(2,1)}, bf16[1024,1024]{1,0:T(8,128)(2,1)}) custom-call(bf16[512,1024]{1,0:T(8,128)(2,1)} %bitcast.51, bf16[1024,1024]{1,0:T(8,128)(2,1)} %w_src_hbm.1, s32[3,256]{1,0:T(4,128)} %bitcast.60, f32[3,256]{1,0:T(4,128)} %bitcast.61, f32[1,1024]{1,0:T(1,128)} %bitcast.62, bf16[100,1024]{1,0:T(8,128)(2,1)} %bitcast.59, ...), custom_call_target="tpu_custom_call" | custom-call | flops 2147483648 | bytes 11132704 | tf_op jit(solution)/shard_map/pallas_call | solution.py:455
  18.0 8.4 %all-to-all-done = bf16[16,2,8,1152]{3,2,1,0:T(8,128)(2,1)S(1)} async-done(((bf16[16,2,8,1152]{3,2,1,0:T(8,128)(2,1)}), bf16[16,2,8,1152]{3,2,1,0:T(8,128)(2,1)S(1)}, u32[]{:S(2)}, u32[]{:S(2)}) %all-to-all-start) | async-done | bytes 589856 | tf_op jit(solution)/shard_map/all_to_all | solution.py:511
  26.4 15.5 %shard_map.140 = (bf16[512,1024]{1,0:T(8,128)(2,1)}, bf16[16,16,1024]{2,1,0:T(8,128)(2,1)}, bf16[8,64,640]{2,1,0:T(8,128)(2,1)S(1)}, bf16[8,64,640]{2,1,0:T(8,12...) custom-call(s32[1]{0:T(128)} %bitcast.me_ref, bf16[16,16,1152]{2,1,0:T(8,128)(2,1)S(1)} %bitcast.33, ...), custom_call_target="tpu_custom_call" | custom-call | flops 17179869184 | bytes 27262976 | tf_op jit(solution)/shard_map/pallas_call | solution.py:455
  41.8 0.1 collective-permute-start
  41.9 0.5 collective-permute-start.1
  42.4 4.5 %all-to-all-start.1 = ((bf16[16,16,1024]{2,1,0:T(8,128)(2,1)}), bf16[16,16,1024]{2,1,0:T(8,128)(2,1)}, u32[]{:S(2)}, u32[]{:S(2)}) async-start(bf16[16,16,1024]{2,1,0:T(8,128)(2,1)} %get-tuple-element.41), calls=%async_computation.1 | async-start | bytes 1048576 | tf_op jit(solution)/shard_map/all_to_all | solution.py:575
  46.9 0.0 collective-permute-done.1
  46.9 0.0 collective-permute-done
  46.9 0.3 shard_map.141
  47.2 1.9 %collective-permute-start.2 = (bf16[4,64,640]{2,1,0:T(8,128)(2,1)S(1)}, bf16[4,64,640]{2,1,0:T(8,128)(2,1)S(1)}, u32[]{:S(2)}, u32[]{:S(2)}) collective-permute-start(bf16[4,64,640]{2,1,0:T(8,128)(2,1)S(1)} %bitcast.46), channel_id=1, source_target_pairs={{0,2},{1,3},{2,0},{3,1},{4,6},{5,7},{6,4},{7,5},{8,10},{9,11},{10,... | collective-permute-start | bytes 983048 | tf_op jit(solution)/shard_map/ppermute | solution.py:467
  49.1 1.5 %collective-permute-start.3 = (bf16[4,64,512]{2,1,0:T(8,128)(2,1)S(1)}, bf16[4,64,512]{2,1,0:T(8,128)(2,1)S(1)}, u32[]{:S(2)}, u32[]{:S(2)}) collective-permute-start(bf16[4,64,512]{2,1,0:T(8,128)(2,1)S(1)} %bitcast.47), channel_id=1, source_target_pairs={{0,4},{1,5},{2,6},{3,7},{4,0},{5,1},{6,2},{7,3},{8,12},{9,13},{10,... | collective-permute-start | bytes 786440 | tf_op jit(solution)/shard_map/ppermute | solution.py:467
  50.6 13.4 %collective-permute-done.3 = bf16[4,64,512]{2,1,0:T(8,128)(2,1)S(1)} collective-permute-done((bf16[4,64,512]{2,1,0:T(8,128)(2,1)S(1)}, bf16[4,64,512]{2,1,0:T(8,128)(2,1)S(1)}, u32[]{:S(2)}, u32[]{:S(2)}) %collective-permute-start.3) | collective-permute-done | bytes 262176 | tf_op jit(solution)/shard_map/ppermute | solution.py:467
  64.0 0.0 collective-permute-done.2
  64.0 0.1 shard_map.142
  64.2 0.5 collective-permute-start.4
  64.7 1.6 %collective-permute-start.5 = (bf16[2,64,512]{2,1,0:T(8,128)(2,1)S(1)}, bf16[2,64,512]{2,1,0:T(8,128)(2,1)S(1)}, u32[]{:S(2)}, u32[]{:S(2)}) collective-permute-start(bf16[2,64,512]{2,1,0:T(8,128)(2,1)S(1)} %bitcast.50), channel_id=1, source_target_pairs={{0,2},{1,3},{2,0},{3,1},{4,6},{5,7},{6,4},{7,5},{8,10},{9,11},{10,... | collective-permute-start | bytes 393224 | tf_op jit(solution)/shard_map/ppermute | solution.py:467
  66.3 3.4 %collective-permute-done.5 = bf16[2,64,512]{2,1,0:T(8,128)(2,1)S(1)} collective-permute-done((bf16[2,64,512]{2,1,0:T(8,128)(2,1)S(1)}, bf16[2,64,512]{2,1,0:T(8,128)(2,1)S(1)}, u32[]{:S(2)}, u32[]{:S(2)}) %collective-permute-start.5) | collective-permute-done | bytes 131104 | tf_op jit(solution)/shard_map/ppermute | solution.py:467
  69.7 0.2 collective-permute-done.4
  70.0 0.1 shard_map.143
  70.0 0.0 copy-start
  70.1 0.7 copy-done
  70.7 2.5 %collective-permute-start.6 = (bf16[1,64,1152]{2,1,0:T(8,128)(2,1)S(1)}, bf16[1,64,1152]{2,1,0:T(8,128)(2,1)S(1)}, u32[]{:S(2)}, u32[]{:S(2)}) collective-permute-start(bf16[1,64,1152]{2,1,0:T(8,128)(2,1)S(1)} %bitcast.49), channel_id=1, source_target_pairs={{0,8},{1,9},{2,10},{3,11},{4,12},{5,13},{6,14},{7,15},{8,0},{9,1},... | collective-permute-start | bytes 442376 | tf_op jit(solution)/shard_map/ppermute | solution.py:467
  73.2 0.0 all-to-all-done.1.returned
  73.2 5.3 %shard_map.145 = f32[512,1024]{1,0:T(8,128)} custom-call(s32[1,2,16]{2,1,0:T(2,128)} %bitcast.56, bf16[16,16,1024]{2,1,0:T(8,128)(2,1)} %all-to-all-done.1.returned, bf16[512,1024]{1,0:T(8,128)(2,1)} %get-tuple-element.42.dlocal_hbm, bf16[1024,1024]{1,0:T(8,128)(2,1)} %get-tuple-element.43.w_src_t_hbm, bf16[1,64,1152]{2,1,0:T(8,128)(2,1)} %bitcast.42), custom_call_target="tpu_custom_call" | custom-call | flops 4294967296 | bytes 6291456 | tf_op jit(solution)/shard_map/pallas_call | solution.py:455
  78.5 0.8 collective-permute-done.6.got
  79.3 0.8 shard_map.144
  (4 shorter events, 0.0 us)
Async XLA Ops:
  0.6 10.2 %copy-start.2 = (f32[100]{0:T(128)S(1)}, f32[100]{0:T(128)}, u32[]{:S(2)}) copy-start(f32[100]{0:T(128)} %param.15) | copy-start | bytes 1204
  0.6 10.9 %copy-start.3 = (f32[100]{0:T(128)S(1)}, f32[100]{0:T(128)}, u32[]{:S(2)}) copy-start(f32[100]{0:T(128)} %param.17) | copy-start | bytes 1204
  3.5 22.9 %all-to-all-start = ((bf16[16,2,8,1152]{3,2,1,0:T(8,128)(2,1)}), bf16[16,2,8,1152]{3,2,1,0:T(8,128)(2,1)S(1)}, u32[]{:S(2)}, u32[]{:S(2)}) async-start(bf16[16,2,8,1152]{3,2,1,0:T(8,128)(2,1)} %shard_map.138), calls=%async_computation | async-start | bytes 1179648 | tf_op jit(solution)/shard_map/all_to_all | solution.py:511
  41.8 5.1 %collective-permute-start = (bf16[8,64,640]{2,1,0:T(8,128)(2,1)S(1)}, bf16[8,64,640]{2,1,0:T(8,128)(2,1)S(1)}, u32[]{:S(2)}, u32[]{:S(2)}) collective-permute-start(bf16[8,64,640]{2,1,0:T(8,128)(2,1)S(1)} %get-tuple-element.27), channel_id=1, source_target_pairs={{0,1},{1,0},{2,3},{3,2},{4,5},{5,4},{6,7},{7,6},{8,9},{9,8},{10,11... | collective-permute-start | bytes 1966088 | tf_op jit(solution)/shard_map/ppermute | solution.py:467
  41.9 5.0 %collective-permute-start.1 = (bf16[8,64,512]{2,1,0:T(8,128)(2,1)S(1)}, bf16[8,64,512]{2,1,0:T(8,128)(2,1)S(1)}, u32[]{:S(2)}, u32[]{:S(2)}) collective-permute-start(bf16[8,64,512]{2,1,0:T(8,128)(2,1)S(1)} %get-tuple-element.29), channel_id=1, source_target_pairs={{0,1},{1,0},{2,3},{3,2},{4,5},{5,4},{6,7},{7,6},{8,9},{9,8},{10,11... | collective-permute-start | bytes 1572872 | tf_op jit(solution)/shard_map/ppermute | solution.py:467
  42.4 30.8 %all-to-all-start.1 = ((bf16[16,16,1024]{2,1,0:T(8,128)(2,1)}), bf16[16,16,1024]{2,1,0:T(8,128)(2,1)}, u32[]{:S(2)}, u32[]{:S(2)}) async-start(bf16[16,16,1024]{2,1,0:T(8,128)(2,1)} %get-tuple-element.41), calls=%async_computation.1 | async-start | bytes 1048576 | tf_op jit(solution)/shard_map/all_to_all | solution.py:575
  47.2 16.8 %collective-permute-start.2 = (bf16[4,64,640]{2,1,0:T(8,128)(2,1)S(1)}, bf16[4,64,640]{2,1,0:T(8,128)(2,1)S(1)}, u32[]{:S(2)}, u32[]{:S(2)}) collective-permute-start(bf16[4,64,640]{2,1,0:T(8,128)(2,1)S(1)} %bitcast.46), channel_id=1, source_target_pairs={{0,2},{1,3},{2,0},{3,1},{4,6},{5,7},{6,4},{7,5},{8,10},{9,11},{10,... | collective-permute-start | bytes 983048 | tf_op jit(solution)/shard_map/ppermute | solution.py:467
  49.1 14.9 %collective-permute-start.3 = (bf16[4,64,512]{2,1,0:T(8,128)(2,1)S(1)}, bf16[4,64,512]{2,1,0:T(8,128)(2,1)S(1)}, u32[]{:S(2)}, u32[]{:S(2)}) collective-permute-start(bf16[4,64,512]{2,1,0:T(8,128)(2,1)S(1)} %bitcast.47), channel_id=1, source_target_pairs={{0,4},{1,5},{2,6},{3,7},{4,0},{5,1},{6,2},{7,3},{8,12},{9,13},{10,... | collective-permute-start | bytes 786440 | tf_op jit(solution)/shard_map/ppermute | solution.py:467
  64.2 5.8 %collective-permute-start.4 = (bf16[2,64,640]{2,1,0:T(8,128)(2,1)S(1)}, bf16[2,64,640]{2,1,0:T(8,128)(2,1)S(1)}, u32[]{:S(2)}, u32[]{:S(2)}) collective-permute-start(bf16[2,64,640]{2,1,0:T(8,128)(2,1)S(1)} %bitcast.48), channel_id=1, source_target_pairs={{0,4},{1,5},{2,6},{3,7},{4,0},{5,1},{6,2},{7,3},{8,12},{9,13},{10,... | collective-permute-start | bytes 491528 | tf_op jit(solution)/shard_map/ppermute | solution.py:467
  64.7 5.0 %collective-permute-start.5 = (bf16[2,64,512]{2,1,0:T(8,128)(2,1)S(1)}, bf16[2,64,512]{2,1,0:T(8,128)(2,1)S(1)}, u32[]{:S(2)}, u32[]{:S(2)}) collective-permute-start(bf16[2,64,512]{2,1,0:T(8,128)(2,1)S(1)} %bitcast.50), channel_id=1, source_target_pairs={{0,2},{1,3},{2,0},{3,1},{4,6},{5,7},{6,4},{7,5},{8,10},{9,11},{10,... | collective-permute-start | bytes 393224 | tf_op jit(solution)/shard_map/ppermute | solution.py:467
  70.0 0.7 copy-start
  70.7 8.6 %collective-permute-start.6 = (bf16[1,64,1152]{2,1,0:T(8,128)(2,1)S(1)}, bf16[1,64,1152]{2,1,0:T(8,128)(2,1)S(1)}, u32[]{:S(2)}, u32[]{:S(2)}) collective-permute-start(bf16[1,64,1152]{2,1,0:T(8,128)(2,1)S(1)} %bitcast.49), channel_id=1, source_target_pairs={{0,8},{1,9},{2,10},{3,11},{4,12},{5,13},{6,14},{7,15},{8,0},{9,1},... | collective-permute-start | bytes 442376 | tf_op jit(solution)/shard_map/ppermute | solution.py:467
  73.2 6.1 %copy-start.1 = (bf16[1,1,64,1152]{3,2,1,0:T(8,128)(2,1)S(1)}, bf16[1,1,64,1152]{3,2,1,0:T(8,128)(2,1)}, u32[]{:S(2)}) copy-start(bf16[1,1,64,1152]{3,2,1,0:T(8,128)(2,1)} %copy-done) | copy-start | bytes 442372

commit v5 on v4

--- a/solution.py
+++ b/solution.py
@@ -65,35 +65,32 @@
             table[at : at + count, c * LANES : (c + 1) * LANES] = block.astype(bf16)
 
 
-def pack_kernel(rows_ref, latent, area, out, zeros, sem):
-    shards, slots, members, _ = out.shape
-    width = zeros.shape[1]
-    zeros[...] = jnp.zeros_like(zeros)
+def fill_selector(selector, rows_ref, members):
+    _, slots, shards = rows_ref.shape
+    lane = lax.broadcasted_iota(jnp.int32, (members, selector.shape[1]), 1)
+    member = lax.broadcasted_iota(jnp.int32, (members, selector.shape[1]), 0)
     for s in range(shards):
         for b in range(slots):
-            row = rows_ref[0, b, s]
-            target = out.at[s, b, :, pl.ds(0, width)]
-
-            @pl.when(row >= 0)
-            def _(row=row, target=target):
-                pltpu.make_async_copy(latent.at[row], target, sem).start()
-
-            @pl.when(row < 0)
-            def _(target=target):
-                pltpu.make_async_copy(zeros, target, sem).start()
-
-    total = jnp.sum(area[...], axis=1, keepdims=True) + jnp.zeros((members, LANES), f32)
-    lane = lax.broadcasted_iota(jnp.int32, (members, LANES), 1)
-    tail = jnp.zeros((members, LANES), f32)
+            first = (s * slots + b) * members
+            selector[first : first + members, :] = jnp.where(
+                lane == rows_ref[0, b, s] * members + member, 1.0, 0.0
+            ).astype(f32)
+
+
+def pack_kernel(rows_ref, latent, area, out, selector, *, members):
+    shards, per_pair, _ = out.shape
+    width = latent.shape[1]
+    fill_selector(selector, rows_ref, members)
+    picked = mm(selector[...].astype(bf16), latent[...])
+    out[:, :, :width] = picked.astype(bf16).reshape(shards, per_pair, width)
+    total = jnp.sum(area[...], axis=1, keepdims=True) + jnp.zeros((per_pair, LANES), f32)
+    lane = lax.broadcasted_iota(jnp.int32, (per_pair, LANES), 1)
+    tail = jnp.zeros((per_pair, LANES), f32)
     for i, piece in enumerate(split_sum(total)):
         tail = jnp.where(lane == i, piece.astype(f32), tail)
     tail = tail.astype(bf16)
     for s in range(shards):
-        for b in range(slots):
-            out[s, b, :, width:] = tail
-    for s in range(shards):
-        for b in range(slots):
-            pltpu.make_async_copy(zeros, out.at[s, b, :, pl.ds(0, width)], sem).wait()
+        out[s, :, width:] = tail
 
 
 def strips(widths, width):
@@ -401,7 +398,7 @@
 
 
 def latent_grad_kernel(
-    rows_ref, returned, dlocal_hbm, w_src_t_hbm, _, out_hbm, selector, dlocal, w_src_t, out, sem
+    rows_ref, returned, dlocal_hbm, w_src_t_hbm, out_hbm, selector, dlocal, w_src_t, out, sem
 ):
     shards, per_pair, width = returned.shape
     _, slots, _ = rows_ref.shape
@@ -412,14 +409,7 @@
     ]
     for load in loads:
         load.start()
-    lane = lax.broadcasted_iota(jnp.int32, (members, selector.shape[1]), 1)
-    member = lax.broadcasted_iota(jnp.int32, (members, selector.shape[1]), 0)
-    for s in range(shards):
-        for b in range(slots):
-            first = (s * slots + b) * members
-            selector[first : first + members, :] = jnp.where(
-                lane == rows_ref[0, b, s] * members + member, 1.0, 0.0
-            ).astype(f32)
+    fill_selector(selector, rows_ref, members)
     back = returned[...].reshape(shards * per_pair, width)
     spread = mm(selector[...].astype(bf16), back, TN)
     for load in loads:
@@ -497,19 +487,19 @@
     latent_rows = latent.reshape(mesh_rows * members, width)
     slot_rows = jnp.swapaxes(send_rows, 1, 2)
     area_row = area_weight.reshape(1, points)
+    selector = pltpu.VMEM((shards * per_pair, mesh_rows * members), f32)
     outgoing = call(
-        pack_kernel,
-        shape((shards, slots, members, width + LANES), bf16),
-        [SMEM, ANY, VMEM],
-        [pltpu.VMEM((members, width), bf16), pltpu.SemaphoreType.DMA],
+        functools.partial(pack_kernel, members=members),
+        shape((shards, per_pair, width + LANES), bf16),
+        [SMEM, VMEM, VMEM],
+        [selector],
         1 << 24,
         slot_rows,
-        latent,
+        latent_rows,
         area_row,
         limit=PACK * MIB,
     )
     arrived = lax.all_to_all(outgoing, "space", split_axis=0, concat_axis=0, tiled=True)
-    arrived = arrived.reshape(shards, per_pair, width + LANES)
 
     columns = width + var_pad
     cut = half_width + var_pad
@@ -621,9 +611,9 @@
     grad_latent = call(
         latent_grad_kernel,
         shape((mesh_rows * members, width), f32),
-        [SMEM, VMEM, HBM, HBM, ANY],
+        [SMEM, VMEM, HBM, HBM],
         [
-            pltpu.VMEM((shards * per_pair, mesh_rows * members), f32),
+            selector,
             pltpu.VMEM((mesh_rows * members, width), bf16),
             pltpu.VMEM((width, width), bf16),
             pltpu.VMEM((mesh_rows * members, width), f32),
@@ -634,7 +624,6 @@
         returned,
         dlocal,
         w_src_t,
-        held[0][0],
         out_specs=[HBM],
         limit=LAST * MIB,
     )

time: 80.5 us -> 79.5 us (0.988)
  no operation moved by 1% of the time
where the time goes in v5:
time: 79.5 us; the launch traced here: 79.1 us
  Pallas kernels  30.2 us (38%)
  waiting for transfers between devices  26.3 us (33%)
  starting transfers between devices  20.5 us (26%)
  local copies, waits for them, and re-layouts  1.47 us (2%)
    pallas_call x8, Pallas kernels, call(): pl.pallas_call(kernel, out_shape=out_shape, in_specs=in_specs, out_specs=...  30.2 us
    ppermute x7, waiting for transfers between devices, swap(): return lax.ppermute(value, 'space', [(i, i ^ bit) for i in range(shards)])  17.9 us
    ppermute x7, starting transfers between devices, swap(): return lax.ppermute(value, 'space', [(i, i ^ bit) for i in range(shards)])  8.65 us
    all_to_all x1, waiting for transfers between devices, per_device(): lax.all_to_all(outgoing, 'space', split_axis=0, concat_axis=0, tiled=True)  8.36 us
    all_to_all x1, starting transfers between devices, per_device(): lax.all_to_all(outgoing, 'space', split_axis=0, concat_axis=0, tiled=True)  7.36 us
    all_to_all x1, starting transfers between devices, per_device(): lax.all_to_all(slot_grad, 'space', split_axis=0, concat_axis=0, tiled=True)  4.47 us
  transfers between devices with their start and end apart: 9, of which 5 were waited for; matrix products, arithmetic and copies ran while one was open for 2% of the time, Pallas kernels for 14%

profile of v5, /device:TPU:0, one launch (start us, length us, event | category | flops | bytes accessed | tf_op | source)
XLA Modules:
  0.0 79.1 jit_solution(7399171831772603916)
XLA Ops:
  0.6 0.0 copy-start
  0.6 0.0 copy-start.1
  0.7 2.5 %shard_map.138 = bf16[16,16,1152]{2,1,0:T(8,128)(2,1)} custom-call(s32[1,2,16]{2,1,0:T(2,128)} %bitcast.53, bf16[512,1024]{1,0:T(8,128)(2,1)} %bitcast.48, f32[1,256]{1,0:T(1,128)} %bitcast.51), custom_call_target="tpu_custom_call" | custom-call | flops 16777216 | bytes 2163712 | tf_op jit(solution)/shard_map/pallas_call | solution.py:445
  3.2 7.4 %all-to-all-start = ((bf16[16,16,1152]{2,1,0:T(8,128)(2,1)}), bf16[16,16,1152]{2,1,0:T(8,128)(2,1)S(1)}, u32[]{:S(2)}, u32[]{:S(2)}) async-start(bf16[16,16,1152]{2,1,0:T(8,128)(2,1)} %shard_map.138), calls=%async_computation | async-start | bytes 1179648 | tf_op jit(solution)/shard_map/all_to_all | solution.py:502
  10.5 0.0 copy-done
  10.5 0.7 copy.15.b_out
  11.3 0.0 copy-done.1
  11.3 0.7 copy.16.var_weight
  12.0 5.7 %shard_map.139 = (bf16[1376,1024]{1,0:T(8,128)(2,1)}, bf16[1024,1024]{1,0:T(8,128)(2,1)}) custom-call(bf16[512,1024]{1,0:T(8,128)(2,1)} %bitcast.49, bf16[1024,1024]{1,0:T(8,128)(2,1)} %w_src_hbm.1, s32[3,256]{1,0:T(4,128)} %bitcast.58, f32[3,256]{1,0:T(4,128)} %bitcast.59, f32[1,1024]{1,0:T(1,128)} %bitcast.60, bf16[100,1024]{1,0:T(8,128)(2,1)} %bitcast.57, ...), custom_call_target="tpu_custom_call" | custom-call | flops 2147483648 | bytes 11132704 | tf_op jit(solution)/shard_map/pallas_call | solution.py:445
  17.7 8.4 %all-to-all-done.arrived = bf16[16,16,1152]{2,1,0:T(8,128)(2,1)S(1)} async-done(((bf16[16,16,1152]{2,1,0:T(8,128)(2,1)}), bf16[16,16,1152]{2,1,0:T(8,128)(2,1)S(1)}, u32[]{:S(2)}, u32[]{:S(2)}) %all-to-all-start) | async-done | bytes 589856 | tf_op jit(solution)/shard_map/all_to_all | solution.py:502
  26.1 15.5 %shard_map.140 = (bf16[512,1024]{1,0:T(8,128)(2,1)}, bf16[16,16,1024]{2,1,0:T(8,128)(2,1)}, bf16[8,64,640]{2,1,0:T(8,128)(2,1)S(1)}, bf16[8,64,640]{2,1,0:T(8,12...) custom-call(s32[1]{0:T(128)} %bitcast.me_ref, ...), custom_call_target="tpu_custom_call" | custom-call | flops 17179869184 | bytes 27262976 | tf_op jit(solution)/shard_map/pallas_call | solution.py:445
  41.5 0.1 collective-permute-start
  41.6 0.5 collective-permute-start.1
  42.1 4.5 %all-to-all-start.1 = ((bf16[16,16,1024]{2,1,0:T(8,128)(2,1)}), bf16[16,16,1024]{2,1,0:T(8,128)(2,1)}, u32[]{:S(2)}, u32[]{:S(2)}) async-start(bf16[16,16,1024]{2,1,0:T(8,128)(2,1)} %get-tuple-element.41), calls=%async_computation.1 | async-start | bytes 1048576 | tf_op jit(solution)/shard_map/all_to_all | solution.py:565
  46.6 0.0 collective-permute-done.1
  46.6 0.0 collective-permute-done
  46.6 0.3 shard_map.141
  46.9 1.9 %collective-permute-start.2 = (bf16[4,64,640]{2,1,0:T(8,128)(2,1)S(1)}, bf16[4,64,640]{2,1,0:T(8,128)(2,1)S(1)}, u32[]{:S(2)}, u32[]{:S(2)}) collective-permute-start(bf16[4,64,640]{2,1,0:T(8,128)(2,1)S(1)} %bitcast.43), channel_id=1, source_target_pairs={{0,2},{1,3},{2,0},{3,1},{4,6},{5,7},{6,4},{7,5},{8,10},{9,11},{10,... | collective-permute-start | bytes 983048 | tf_op jit(solution)/shard_map/ppermute | solution.py:457
  48.8 1.5 %collective-permute-start.3 = (bf16[4,64,512]{2,1,0:T(8,128)(2,1)S(1)}, bf16[4,64,512]{2,1,0:T(8,128)(2,1)S(1)}, u32[]{:S(2)}, u32[]{:S(2)}) collective-permute-start(bf16[4,64,512]{2,1,0:T(8,128)(2,1)S(1)} %bitcast.44), channel_id=1, source_target_pairs={{0,4},{1,5},{2,6},{3,7},{4,0},{5,1},{6,2},{7,3},{8,12},{9,13},{10,... | collective-permute-start | bytes 786440 | tf_op jit(solution)/shard_map/ppermute | solution.py:457
  50.3 13.4 %collective-permute-done.3 = bf16[4,64,512]{2,1,0:T(8,128)(2,1)S(1)} collective-permute-done((bf16[4,64,512]{2,1,0:T(8,128)(2,1)S(1)}, bf16[4,64,512]{2,1,0:T(8,128)(2,1)S(1)}, u32[]{:S(2)}, u32[]{:S(2)}) %collective-permute-start.3) | collective-permute-done | bytes 262176 | tf_op jit(solution)/shard_map/ppermute | solution.py:457
  63.7 0.0 collective-permute-done.2
  63.7 0.1 shard_map.142
  63.8 0.5 collective-permute-start.4
  64.4 1.6 %collective-permute-start.5 = (bf16[2,64,512]{2,1,0:T(8,128)(2,1)S(1)}, bf16[2,64,512]{2,1,0:T(8,128)(2,1)S(1)}, u32[]{:S(2)}, u32[]{:S(2)}) collective-permute-start(bf16[2,64,512]{2,1,0:T(8,128)(2,1)S(1)} %bitcast.47), channel_id=1, source_target_pairs={{0,2},{1,3},{2,0},{3,1},{4,6},{5,7},{6,4},{7,5},{8,10},{9,11},{10,... | collective-permute-start | bytes 393224 | tf_op jit(solution)/shard_map/ppermute | solution.py:457
  66.0 3.4 %collective-permute-done.5 = bf16[2,64,512]{2,1,0:T(8,128)(2,1)S(1)} collective-permute-done((bf16[2,64,512]{2,1,0:T(8,128)(2,1)S(1)}, bf16[2,64,512]{2,1,0:T(8,128)(2,1)S(1)}, u32[]{:S(2)}, u32[]{:S(2)}) %collective-permute-start.5) | collective-permute-done | bytes 131104 | tf_op jit(solution)/shard_map/ppermute | solution.py:457
  69.4 0.2 collective-permute-done.4
  69.7 0.1 shard_map.143
  69.7 2.5 %collective-permute-start.6 = (bf16[1,64,1152]{2,1,0:T(8,128)(2,1)S(1)}, bf16[1,64,1152]{2,1,0:T(8,128)(2,1)S(1)}, u32[]{:S(2)}, u32[]{:S(2)}) collective-permute-start(bf16[1,64,1152]{2,1,0:T(8,128)(2,1)S(1)} %bitcast.46), channel_id=1, source_target_pairs={{0,8},{1,9},{2,10},{3,11},{4,12},{5,13},{6,14},{7,15},{8,0},{9,1},... | collective-permute-start | bytes 442376 | tf_op jit(solution)/shard_map/ppermute | solution.py:457
  72.3 0.0 all-to-all-done.1.returned
  72.3 5.3 %shard_map.145 = f32[512,1024]{1,0:T(8,128)} custom-call(s32[1,2,16]{2,1,0:T(2,128)} %bitcast.54, bf16[16,16,1024]{2,1,0:T(8,128)(2,1)} %all-to-all-done.1.returned, bf16[512,1024]{1,0:T(8,128)(2,1)} %get-tuple-element.42.dlocal_hbm, bf16[1024,1024]{1,0:T(8,128)(2,1)} %get-tuple-element.43.w_src_t_hbm), custom_call_target="tpu_custom_call" | custom-call | flops 4294967296 | bytes 6291456 | tf_op jit(solution)/shard_map/pallas_call | solution.py:445
  77.5 0.8 %collective-permute-done.6.got = bf16[1,64,1152]{2,1,0:T(8,128)(2,1)S(1)} collective-permute-done((bf16[1,64,1152]{2,1,0:T(8,128)(2,1)S(1)}, bf16[1,64,1152]{2,1,0:T(8,128)(2,1)S(1)}, u32[]{:S(2)}, u32[]{:S(2)}) %collective-permute-start.6) | collective-permute-done | bytes 147488 | tf_op jit(solution)/shard_map/ppermute | solution.py:457
  78.4 0.8 shard_map.144
Async XLA Ops:
  0.6 9.9 %copy-start = (f32[100]{0:T(128)S(1)}, f32[100]{0:T(128)}, u32[]{:S(2)}) copy-start(f32[100]{0:T(128)} %param.15) | copy-start | bytes 1204
  0.6 10.6 %copy-start.1 = (f32[100]{0:T(128)S(1)}, f32[100]{0:T(128)}, u32[]{:S(2)}) copy-start(f32[100]{0:T(128)} %param.17) | copy-start | bytes 1204
  3.2 22.9 %all-to-all-start = ((bf16[16,16,1152]{2,1,0:T(8,128)(2,1)}), bf16[16,16,1152]{2,1,0:T(8,128)(2,1)S(1)}, u32[]{:S(2)}, u32[]{:S(2)}) async-start(bf16[16,16,1152]{2,1,0:T(8,128)(2,1)} %shard_map.138), calls=%async_computation | async-start | bytes 1179648 | tf_op jit(solution)/shard_map/all_to_all | solution.py:502
  41.5 5.1 %collective-permute-start = (bf16[8,64,640]{2,1,0:T(8,128)(2,1)S(1)}, bf16[8,64,640]{2,1,0:T(8,128)(2,1)S(1)}, u32[]{:S(2)}, u32[]{:S(2)}) collective-permute-start(bf16[8,64,640]{2,1,0:T(8,128)(2,1)S(1)} %get-tuple-element.27), channel_id=1, source_target_pairs={{0,1},{1,0},{2,3},{3,2},{4,5},{5,4},{6,7},{7,6},{8,9},{9,8},{10,11... | collective-permute-start | bytes 1966088 | tf_op jit(solution)/shard_map/ppermute | solution.py:457
  41.6 5.0 %collective-permute-start.1 = (bf16[8,64,512]{2,1,0:T(8,128)(2,1)S(1)}, bf16[8,64,512]{2,1,0:T(8,128)(2,1)S(1)}, u32[]{:S(2)}, u32[]{:S(2)}) collective-permute-start(bf16[8,64,512]{2,1,0:T(8,128)(2,1)S(1)} %get-tuple-element.29), channel_id=1, source_target_pairs={{0,1},{1,0},{2,3},{3,2},{4,5},{5,4},{6,7},{7,6},{8,9},{9,8},{10,11... | collective-permute-start | bytes 1572872 | tf_op jit(solution)/shard_map/ppermute | solution.py:457
  42.1 30.2 %all-to-all-start.1 = ((bf16[16,16,1024]{2,1,0:T(8,128)(2,1)}), bf16[16,16,1024]{2,1,0:T(8,128)(2,1)}, u32[]{:S(2)}, u32[]{:S(2)}) async-start(bf16[16,16,1024]{2,1,0:T(8,128)(2,1)} %get-tuple-element.41), calls=%async_computation.1 | async-start | bytes 1048576 | tf_op jit(solution)/shard_map/all_to_all | solution.py:565
  46.9 16.8 %collective-permute-start.2 = (bf16[4,64,640]{2,1,0:T(8,128)(2,1)S(1)}, bf16[4,64,640]{2,1,0:T(8,128)(2,1)S(1)}, u32[]{:S(2)}, u32[]{:S(2)}) collective-permute-start(bf16[4,64,640]{2,1,0:T(8,128)(2,1)S(1)} %bitcast.43), channel_id=1, source_target_pairs={{0,2},{1,3},{2,0},{3,1},{4,6},{5,7},{6,4},{7,5},{8,10},{9,11},{10,... | collective-permute-start | bytes 983048 | tf_op jit(solution)/shard_map/ppermute | solution.py:457
  48.8 14.9 %collective-permute-start.3 = (bf16[4,64,512]{2,1,0:T(8,128)(2,1)S(1)}, bf16[4,64,512]{2,1,0:T(8,128)(2,1)S(1)}, u32[]{:S(2)}, u32[]{:S(2)}) collective-permute-start(bf16[4,64,512]{2,1,0:T(8,128)(2,1)S(1)} %bitcast.44), channel_id=1, source_target_pairs={{0,4},{1,5},{2,6},{3,7},{4,0},{5,1},{6,2},{7,3},{8,12},{9,13},{10,... | collective-permute-start | bytes 786440 | tf_op jit(solution)/shard_map/ppermute | solution.py:457
  63.8 5.8 %collective-permute-start.4 = (bf16[2,64,640]{2,1,0:T(8,128)(2,1)S(1)}, bf16[2,64,640]{2,1,0:T(8,128)(2,1)S(1)}, u32[]{:S(2)}, u32[]{:S(2)}) collective-permute-start(bf16[2,64,640]{2,1,0:T(8,128)(2,1)S(1)} %bitcast.45), channel_id=1, source_target_pairs={{0,4},{1,5},{2,6},{3,7},{4,0},{5,1},{6,2},{7,3},{8,12},{9,13},{10,... | collective-permute-start | bytes 491528 | tf_op jit(solution)/shard_map/ppermute | solution.py:457
  64.4 5.0 %collective-permute-start.5 = (bf16[2,64,512]{2,1,0:T(8,128)(2,1)S(1)}, bf16[2,64,512]{2,1,0:T(8,128)(2,1)S(1)}, u32[]{:S(2)}, u32[]{:S(2)}) collective-permute-start(bf16[2,64,512]{2,1,0:T(8,128)(2,1)S(1)} %bitcast.47), channel_id=1, source_target_pairs={{0,2},{1,3},{2,0},{3,1},{4,6},{5,7},{6,4},{7,5},{8,10},{9,11},{10,... | collective-permute-start | bytes 393224 | tf_op jit(solution)/shard_map/ppermute | solution.py:457
  69.7 8.6 %collective-permute-start.6 = (bf16[1,64,1152]{2,1,0:T(8,128)(2,1)S(1)}, bf16[1,64,1152]{2,1,0:T(8,128)(2,1)S(1)}, u32[]{:S(2)}, u32[]{:S(2)}) collective-permute-start(bf16[1,64,1152]{2,1,0:T(8,128)(2,1)S(1)} %bitcast.46), channel_id=1, source_target_pairs={{0,8},{1,9},{2,10},{3,11},{4,12},{5,13},{6,14},{7,15},{8,0},{9,1},... | collective-permute-start | bytes 442376 | tf_op jit(solution)/shard_map/ppermute | solution.py:457

commit v6 on v5

--- a/solution.py
+++ b/solution.py
@@ -16,7 +16,6 @@
 MIB = 1 << 20
 KEEP = 50
 PACK = 56
-UNROLL = 2
 LAST = 54
 
 f32 = jnp.float32
@@ -294,7 +293,7 @@
                 q = d * d + smooth_sq
                 r = lax.rsqrt(q)
                 fit = fit + q * r
-                grads.append(d * r * (1.0 / members))
+                grads.append(d * r)
             pairs = jnp.zeros((ROWS, LANES), f32)
             apart = [jnp.zeros((ROWS, LANES), f32) for _ in range(members)]
             for j in range(members):
@@ -306,13 +305,13 @@
                     s = d * r
                     apart[j] = apart[j] + s
                     apart[k] = apart[k] - s
-            scaled = weight * inverse_mean
+            scaled = weight * (inverse_mean * (1.0 / members))
             for m in range(members):
-                gradient = grads[m] - (2.0 * spread) * apart[m]
+                gradient = grads[m] - (2.0 * spread * members) * apart[m]
                 dpred[m, at, left : left + LANES] = (gradient * scaled).astype(bf16)
             return loss_sum + weight * (fit * (1.0 / members) - (2.0 * spread) * pairs)
 
-        loss_sum = lax.fori_loop(0, points // ROWS, score, loss_sum, unroll=UNROLL)
+        loss_sum = lax.fori_loop(0, points // ROWS, score, loss_sum, unroll=2)
     loss = jnp.sum(loss_sum, keepdims=True) * (inverse_mean / points_all)
 
     edge_back = prepared[layout.edge_first :, :points]

time: 79.5 us -> 79.5 us (level)
  no operation moved by 1% of the time
where the time goes in v6:
time: 79.5 us; the launch traced here: 79.1 us
  Pallas kernels  30.2 us (38%)
  waiting for transfers between devices  26.3 us (33%)
  starting transfers between devices  20.5 us (26%)
  local copies, waits for them, and re-layouts  1.47 us (2%)
    pallas_call x8, Pallas kernels, call(): pl.pallas_call(kernel, out_shape=out_shape, in_specs=in_specs, out_specs=...  30.2 us
    ppermute x7, waiting for transfers between devices, swap(): return lax.ppermute(value, 'space', [(i, i ^ bit) for i in range(shards)])  17.9 us
    ppermute x7, starting transfers between devices, swap(): return lax.ppermute(value, 'space', [(i, i ^ bit) for i in range(shards)])  8.65 us
    all_to_all x1, waiting for transfers between devices, per_device(): lax.all_to_all(outgoing, 'space', split_axis=0, concat_axis=0, tiled=True)  8.36 us
    all_to_all x1, starting transfers between devices, per_device(): lax.all_to_all(outgoing, 'space', split_axis=0, concat_axis=0, tiled=True)  7.36 us
    all_to_all x1, starting transfers between devices, per_device(): lax.all_to_all(slot_grad, 'space', split_axis=0, concat_axis=0, tiled=True)  4.47 us
  transfers between devices with their start and end apart: 9, of which 5 were waited for; matrix products, arithmetic and copies ran while one was open for 2% of the time, Pallas kernels for 14%

profile of v6, /device:TPU:0, one launch (start us, length us, event | category | flops | bytes accessed | tf_op | source)
XLA Modules:
  0.0 79.1 jit_solution(4801456047599762247)
XLA Ops:
  0.6 0.0 copy-start
  0.6 0.0 copy-start.1
  0.7 2.5 %shard_map.138 = bf16[16,16,1152]{2,1,0:T(8,128)(2,1)} custom-call(s32[1,2,16]{2,1,0:T(2,128)} %bitcast.53, bf16[512,1024]{1,0:T(8,128)(2,1)} %bitcast.48, f32[1,256]{1,0:T(1,128)} %bitcast.51), custom_call_target="tpu_custom_call" | custom-call | flops 16777216 | bytes 2163712 | tf_op jit(solution)/shard_map/pallas_call | solution.py:444
  3.2 7.4 %all-to-all-start = ((bf16[16,16,1152]{2,1,0:T(8,128)(2,1)}), bf16[16,16,1152]{2,1,0:T(8,128)(2,1)S(1)}, u32[]{:S(2)}, u32[]{:S(2)}) async-start(bf16[16,16,1152]{2,1,0:T(8,128)(2,1)} %shard_map.138), calls=%async_computation | async-start | bytes 1179648 | tf_op jit(solution)/shard_map/all_to_all | solution.py:501
  10.5 0.0 copy-done
  10.5 0.7 copy.15.b_out
  11.3 0.0 copy-done.1
  11.3 0.7 copy.16.var_weight
  12.0 5.7 %shard_map.139 = (bf16[1376,1024]{1,0:T(8,128)(2,1)}, bf16[1024,1024]{1,0:T(8,128)(2,1)}) custom-call(bf16[512,1024]{1,0:T(8,128)(2,1)} %bitcast.49, bf16[1024,1024]{1,0:T(8,128)(2,1)} %w_src_hbm.1, s32[3,256]{1,0:T(4,128)} %bitcast.58, f32[3,256]{1,0:T(4,128)} %bitcast.59, f32[1,1024]{1,0:T(1,128)} %bitcast.60, bf16[100,1024]{1,0:T(8,128)(2,1)} %bitcast.57, ...), custom_call_target="tpu_custom_call" | custom-call | flops 2147483648 | bytes 11132704 | tf_op jit(solution)/shard_map/pallas_call | solution.py:444
  17.7 8.4 %all-to-all-done.arrived = bf16[16,16,1152]{2,1,0:T(8,128)(2,1)S(1)} async-done(((bf16[16,16,1152]{2,1,0:T(8,128)(2,1)}), bf16[16,16,1152]{2,1,0:T(8,128)(2,1)S(1)}, u32[]{:S(2)}, u32[]{:S(2)}) %all-to-all-start) | async-done | bytes 589856 | tf_op jit(solution)/shard_map/all_to_all | solution.py:501
  26.1 15.4 %shard_map.140 = (bf16[512,1024]{1,0:T(8,128)(2,1)}, bf16[16,16,1024]{2,1,0:T(8,128)(2,1)}, bf16[8,64,640]{2,1,0:T(8,128)(2,1)S(1)}, bf16[8,64,640]{2,1,0:T(8,12...) custom-call(s32[1]{0:T(128)} %bitcast.me_ref, ...), custom_call_target="tpu_custom_call" | custom-call | flops 17179869184 | bytes 27262976 | tf_op jit(solution)/shard_map/pallas_call | solution.py:444
  41.5 0.1 collective-permute-start
  41.6 0.5 collective-permute-start.1
  42.1 4.5 %all-to-all-start.1 = ((bf16[16,16,1024]{2,1,0:T(8,128)(2,1)}), bf16[16,16,1024]{2,1,0:T(8,128)(2,1)}, u32[]{:S(2)}, u32[]{:S(2)}) async-start(bf16[16,16,1024]{2,1,0:T(8,128)(2,1)} %get-tuple-element.41), calls=%async_computation.1 | async-start | bytes 1048576 | tf_op jit(solution)/shard_map/all_to_all | solution.py:564
  46.6 0.0 collective-permute-done.1
  46.6 0.0 collective-permute-done
  46.6 0.3 shard_map.141
  46.9 1.9 %collective-permute-start.2 = (bf16[4,64,640]{2,1,0:T(8,128)(2,1)S(1)}, bf16[4,64,640]{2,1,0:T(8,128)(2,1)S(1)}, u32[]{:S(2)}, u32[]{:S(2)}) collective-permute-start(bf16[4,64,640]{2,1,0:T(8,128)(2,1)S(1)} %bitcast.43), channel_id=1, source_target_pairs={{0,2},{1,3},{2,0},{3,1},{4,6},{5,7},{6,4},{7,5},{8,10},{9,11},{10,... | collective-permute-start | bytes 983048 | tf_op jit(solution)/shard_map/ppermute | solution.py:456
  48.8 1.5 %collective-permute-start.3 = (bf16[4,64,512]{2,1,0:T(8,128)(2,1)S(1)}, bf16[4,64,512]{2,1,0:T(8,128)(2,1)S(1)}, u32[]{:S(2)}, u32[]{:S(2)}) collective-permute-start(bf16[4,64,512]{2,1,0:T(8,128)(2,1)S(1)} %bitcast.44), channel_id=1, source_target_pairs={{0,4},{1,5},{2,6},{3,7},{4,0},{5,1},{6,2},{7,3},{8,12},{9,13},{10,... | collective-permute-start | bytes 786440 | tf_op jit(solution)/shard_map/ppermute | solution.py:456
  50.3 13.4 %collective-permute-done.3 = bf16[4,64,512]{2,1,0:T(8,128)(2,1)S(1)} collective-permute-done((bf16[4,64,512]{2,1,0:T(8,128)(2,1)S(1)}, bf16[4,64,512]{2,1,0:T(8,128)(2,1)S(1)}, u32[]{:S(2)}, u32[]{:S(2)}) %collective-permute-start.3) | collective-permute-done | bytes 262176 | tf_op jit(solution)/shard_map/ppermute | solution.py:456
  63.7 0.0 collective-permute-done.2
  63.7 0.1 shard_map.142
  63.8 0.5 collective-permute-start.4
  64.3 1.6 %collective-permute-start.5 = (bf16[2,64,512]{2,1,0:T(8,128)(2,1)S(1)}, bf16[2,64,512]{2,1,0:T(8,128)(2,1)S(1)}, u32[]{:S(2)}, u32[]{:S(2)}) collective-permute-start(bf16[2,64,512]{2,1,0:T(8,128)(2,1)S(1)} %bitcast.47), channel_id=1, source_target_pairs={{0,2},{1,3},{2,0},{3,1},{4,6},{5,7},{6,4},{7,5},{8,10},{9,11},{10,... | collective-permute-start | bytes 393224 | tf_op jit(solution)/shard_map/ppermute | solution.py:456
  66.0 3.4 %collective-permute-done.5 = bf16[2,64,512]{2,1,0:T(8,128)(2,1)S(1)} collective-permute-done((bf16[2,64,512]{2,1,0:T(8,128)(2,1)S(1)}, bf16[2,64,512]{2,1,0:T(8,128)(2,1)S(1)}, u32[]{:S(2)}, u32[]{:S(2)}) %collective-permute-start.5) | collective-permute-done | bytes 131104 | tf_op jit(solution)/shard_map/ppermute | solution.py:456
  69.4 0.2 collective-permute-done.4
  69.6 0.1 shard_map.143
  69.7 2.5 %collective-permute-start.6 = (bf16[1,64,1152]{2,1,0:T(8,128)(2,1)S(1)}, bf16[1,64,1152]{2,1,0:T(8,128)(2,1)S(1)}, u32[]{:S(2)}, u32[]{:S(2)}) collective-permute-start(bf16[1,64,1152]{2,1,0:T(8,128)(2,1)S(1)} %bitcast.46), channel_id=1, source_target_pairs={{0,8},{1,9},{2,10},{3,11},{4,12},{5,13},{6,14},{7,15},{8,0},{9,1},... | collective-permute-start | bytes 442376 | tf_op jit(solution)/shard_map/ppermute | solution.py:456
  72.3 0.0 all-to-all-done.1.returned
  72.3 5.3 %shard_map.145 = f32[512,1024]{1,0:T(8,128)} custom-call(s32[1,2,16]{2,1,0:T(2,128)} %bitcast.54, bf16[16,16,1024]{2,1,0:T(8,128)(2,1)} %all-to-all-done.1.returned, bf16[512,1024]{1,0:T(8,128)(2,1)} %get-tuple-element.42.dlocal_hbm, bf16[1024,1024]{1,0:T(8,128)(2,1)} %get-tuple-element.43.w_src_t_hbm), custom_call_target="tpu_custom_call" | custom-call | flops 4294967296 | bytes 6291456 | tf_op jit(solution)/shard_map/pallas_call | solution.py:444
  77.5 0.8 %collective-permute-done.6.got = bf16[1,64,1152]{2,1,0:T(8,128)(2,1)S(1)} collective-permute-done((bf16[1,64,1152]{2,1,0:T(8,128)(2,1)S(1)}, bf16[1,64,1152]{2,1,0:T(8,128)(2,1)S(1)}, u32[]{:S(2)}, u32[]{:S(2)}) %collective-permute-start.6) | collective-permute-done | bytes 147488 | tf_op jit(solution)/shard_map/ppermute | solution.py:456
  78.3 0.8 shard_map.144
Async XLA Ops:
  0.6 9.9 %copy-start = (f32[100]{0:T(128)S(1)}, f32[100]{0:T(128)}, u32[]{:S(2)}) copy-start(f32[100]{0:T(128)} %param.15) | copy-start | bytes 1204
  0.6 10.6 %copy-start.1 = (f32[100]{0:T(128)S(1)}, f32[100]{0:T(128)}, u32[]{:S(2)}) copy-start(f32[100]{0:T(128)} %param.17) | copy-start | bytes 1204
  3.2 22.9 %all-to-all-start = ((bf16[16,16,1152]{2,1,0:T(8,128)(2,1)}), bf16[16,16,1152]{2,1,0:T(8,128)(2,1)S(1)}, u32[]{:S(2)}, u32[]{:S(2)}) async-start(bf16[16,16,1152]{2,1,0:T(8,128)(2,1)} %shard_map.138), calls=%async_computation | async-start | bytes 1179648 | tf_op jit(solution)/shard_map/all_to_all | solution.py:501
  41.5 5.1 %collective-permute-start = (bf16[8,64,640]{2,1,0:T(8,128)(2,1)S(1)}, bf16[8,64,640]{2,1,0:T(8,128)(2,1)S(1)}, u32[]{:S(2)}, u32[]{:S(2)}) collective-permute-start(bf16[8,64,640]{2,1,0:T(8,128)(2,1)S(1)} %get-tuple-element.27), channel_id=1, source_target_pairs={{0,1},{1,0},{2,3},{3,2},{4,5},{5,4},{6,7},{7,6},{8,9},{9,8},{10,11... | collective-permute-start | bytes 1966088 | tf_op jit(solution)/shard_map/ppermute | solution.py:456
  41.6 5.0 %collective-permute-start.1 = (bf16[8,64,512]{2,1,0:T(8,128)(2,1)S(1)}, bf16[8,64,512]{2,1,0:T(8,128)(2,1)S(1)}, u32[]{:S(2)}, u32[]{:S(2)}) collective-permute-start(bf16[8,64,512]{2,1,0:T(8,128)(2,1)S(1)} %get-tuple-element.29), channel_id=1, source_target_pairs={{0,1},{1,0},{2,3},{3,2},{4,5},{5,4},{6,7},{7,6},{8,9},{9,8},{10,11... | collective-permute-start | bytes 1572872 | tf_op jit(solution)/shard_map/ppermute | solution.py:456
  42.1 30.2 %all-to-all-start.1 = ((bf16[16,16,1024]{2,1,0:T(8,128)(2,1)}), bf16[16,16,1024]{2,1,0:T(8,128)(2,1)}, u32[]{:S(2)}, u32[]{:S(2)}) async-start(bf16[16,16,1024]{2,1,0:T(8,128)(2,1)} %get-tuple-element.41), calls=%async_computation.1 | async-start | bytes 1048576 | tf_op jit(solution)/shard_map/all_to_all | solution.py:564
  46.9 16.8 %collective-permute-start.2 = (bf16[4,64,640]{2,1,0:T(8,128)(2,1)S(1)}, bf16[4,64,640]{2,1,0:T(8,128)(2,1)S(1)}, u32[]{:S(2)}, u32[]{:S(2)}) collective-permute-start(bf16[4,64,640]{2,1,0:T(8,128)(2,1)S(1)} %bitcast.43), channel_id=1, source_target_pairs={{0,2},{1,3},{2,0},{3,1},{4,6},{5,7},{6,4},{7,5},{8,10},{9,11},{10,... | collective-permute-start | bytes 983048 | tf_op jit(solution)/shard_map/ppermute | solution.py:456
  48.8 14.9 %collective-permute-start.3 = (bf16[4,64,512]{2,1,0:T(8,128)(2,1)S(1)}, bf16[4,64,512]{2,1,0:T(8,128)(2,1)S(1)}, u32[]{:S(2)}, u32[]{:S(2)}) collective-permute-start(bf16[4,64,512]{2,1,0:T(8,128)(2,1)S(1)} %bitcast.44), channel_id=1, source_target_pairs={{0,4},{1,5},{2,6},{3,7},{4,0},{5,1},{6,2},{7,3},{8,12},{9,13},{10,... | collective-permute-start | bytes 786440 | tf_op jit(solution)/shard_map/ppermute | solution.py:456
  63.8 5.8 %collective-permute-start.4 = (bf16[2,64,640]{2,1,0:T(8,128)(2,1)S(1)}, bf16[2,64,640]{2,1,0:T(8,128)(2,1)S(1)}, u32[]{:S(2)}, u32[]{:S(2)}) collective-permute-start(bf16[2,64,640]{2,1,0:T(8,128)(2,1)S(1)} %bitcast.45), channel_id=1, source_target_pairs={{0,4},{1,5},{2,6},{3,7},{4,0},{5,1},{6,2},{7,3},{8,12},{9,13},{10,... | collective-permute-start | bytes 491528 | tf_op jit(solution)/shard_map/ppermute | solution.py:456
  64.3 5.0 %collective-permute-start.5 = (bf16[2,64,512]{2,1,0:T(8,128)(2,1)S(1)}, bf16[2,64,512]{2,1,0:T(8,128)(2,1)S(1)}, u32[]{:S(2)}, u32[]{:S(2)}) collective-permute-start(bf16[2,64,512]{2,1,0:T(8,128)(2,1)S(1)} %bitcast.47), channel_id=1, source_target_pairs={{0,2},{1,3},{2,0},{3,1},{4,6},{5,7},{6,4},{7,5},{8,10},{9,11},{10,... | collective-permute-start | bytes 393224 | tf_op jit(solution)/shard_map/ppermute | solution.py:456
  69.7 8.6 %collective-permute-start.6 = (bf16[1,64,1152]{2,1,0:T(8,128)(2,1)S(1)}, bf16[1,64,1152]{2,1,0:T(8,128)(2,1)S(1)}, u32[]{:S(2)}, u32[]{:S(2)}) collective-permute-start(bf16[1,64,1152]{2,1,0:T(8,128)(2,1)S(1)} %bitcast.46), channel_id=1, source_target_pairs={{0,8},{1,9},{2,10},{3,11},{4,12},{5,13},{6,14},{7,15},{8,0},{9,1},... | collective-permute-start | bytes 442376 | tf_op jit(solution)/shard_map/ppermute | solution.py:456
